TPU v7x, 32 devices: a whole 2x2x4 slice. The times are simulated.
32 devices in a mesh: blk: 4 (over y, core), batch: 8 (over z, x).
Axes of the slice: x: 2, y: 2, z: 4, core: 2. Of those that a mesh axis runs over, the one named last changes fastest.
Arguments:
- features: bfloat16 [8, 32, 40, 2048], P('batch', 'blk')
- crop_rows: int32 [8], replicated, may hold values from 25 to 32, as said below
- crop_cols: int32 [8], replicated, may hold values from 20 to 40, as said below
- depth_target: float32 [8, 32, 40], P('batch', 'blk'), may hold values from -6 to 6
- labels: int32 [8, 32, 40], P('batch', 'blk'), may hold values from 0 to 39
- first_weight: bfloat16 [2048, 512], P('batch'), may hold values from -0.125 to 0.125
- spatial_weight: bfloat16 [9, 512, 512], P(None, 'batch'), may hold values from -0.09375 to 0.09375
- last_weight: bfloat16 [512, 2048], P('batch'), may hold values from -0.25 to 0.25
- shared_weight: bfloat16 [2048, 512], P('batch'), may hold values from -0.125 to 0.125
- head_weights: bfloat16 [4, 9, 512, 512], P(None, None, 'batch'), may hold values from -0.09375 to 0.09375
- message_weights: bfloat16 [4, 9, 512, 512], P(None, None, 'batch'), may hold values from -0.09375 to 0.09375
- gate_weights: bfloat16 [4, 512, 512], P(None, 'batch'), may hold values from -0.25 to 0.25
- depth_weight: bfloat16 [512], P('batch'), may hold values from -0.5 to 0.5
- class_weight: bfloat16 [512, 40], P('batch'), may hold values from -0.5 to 0.5
- mid_gain: bfloat16 [7, 512], P(None, 'batch'), may hold values from 0.099609375 to 1.8984375
- mid_bias: bfloat16 [7, 512], P(None, 'batch'), may hold values from -0.5 to 0.5
- out_gain: bfloat16 [2048], P('batch'), may hold values from 0.099609375 to 1.8984375
- out_bias: bfloat16 [2048], P('batch'), may hold values from -0.5 to 0.5
Outputs:
- depth_map: float32 [8, 32, 40], P('batch', 'blk')
- class_logits: float32 [8, 32, 40, 40], P('batch', 'blk')
- grad_features: float32 [8, 32, 40, 2048], P('batch', 'blk')
- grad_first: float32 [2048, 512], P('batch')
- grad_spatial: float32 [9, 512, 512], P(None, 'batch')
- grad_last: float32 [512, 2048], P('batch')
- grad_shared: float32 [2048, 512], P('batch')
- grad_heads: float32 [4, 9, 512, 512], P(None, None, 'batch')
- grad_messages: float32 [4, 9, 512, 512], P(None, None, 'batch')
- grad_gates: float32 [4, 512, 512], P(None, 'batch')
- grad_depth: float32 [512], P('batch')
- grad_classes: float32 [512, 40], P('batch')
- grad_mid_gain: float32 [7, 512], P(None, 'batch')
- grad_mid_bias: float32 [7, 512], P(None, 'batch')
- grad_out_gain: float32 [2048], P('batch')
- grad_out_bias: float32 [2048], P('batch')
Inputs may be any that keep to these rules, and one draw needn't show every extreme that they name: `crop_rows`: some image keeps all 32 rows and some keeps the fewest. `crop_cols`: some image keeps all 40 columns and some keeps the fewest.
All inputs are finite; a program needn't handle non-finite values.
Results may differ from a plain program's by a relative error of at most 0.025.
Values may be sent and summed in bfloat16 or wider, within the bound.
A program may use at most 320 MiB of HBM per device.

v0:
```python
import jax
import jax.numpy as jnp
from jax import lax
from jax.sharding import PartitionSpec as P

EPSILON = 1e-05


def extended(cells, sides, width):
    for axis, dim in sides:
        count = lax.axis_size(axis)
        ends = count - 1
        head = lax.slice_in_dim(cells, 0, width, axis=dim)
        tail = lax.slice_in_dim(cells, cells.shape[dim] - width, cells.shape[dim], axis=dim)
        cells = jnp.concatenate(
            [
                lax.ppermute(tail, axis, [(i, (i + 1) % count) for i in range(ends)]),
                cells,
                lax.ppermute(head, axis, [((i + 1) % count, i) for i in range(ends)]),
            ],
            axis=dim,
        )
    return cells


def silu_slope(values):
    sigmoid_value = jax.nn.sigmoid(values)
    return sigmoid_value * (1.0 + values * (1.0 - sigmoid_value))


def side_pad(tile_block):
    return jnp.pad(tile_block, ((0, 0), (1, 1), (0, 0)))


def extend_rows(tile_block):
    return side_pad(extended(tile_block, (("blk", 0),), 1))


def extend_grads(tile_block):
    return side_pad(extended(tile_block, (("blk", 0),), 1))


def conv_forward(padded, kernel, tile_rows, tile_cols):
    channels = padded.shape[2]
    summed = None
    for offset in range(9):
        row_start, col_start = (offset // 3, offset % 3)
        window = padded[
            row_start : row_start + tile_rows, col_start : col_start + tile_cols
        ].reshape(tile_rows * tile_cols, channels)
        product = jnp.dot(window, kernel[offset], preferred_element_type=jnp.float32)
        summed = product if summed is None else summed + product
    return summed


def conv_weights(padded, grad_out, tile_rows, tile_cols):
    channels = padded.shape[2]
    stacked = []
    for offset in range(9):
        row_start, col_start = (offset // 3, offset % 3)
        window = padded[
            row_start : row_start + tile_rows, col_start : col_start + tile_cols
        ].reshape(tile_rows * tile_cols, channels)
        stacked.append(
            jnp.einsum("pc,pd->cd", window, grad_out, preferred_element_type=jnp.float32)
        )
    return jnp.stack(stacked)


def conv_back(padded_grad, kernel, tile_rows, tile_cols):
    channels = padded_grad.shape[2]
    summed = None
    for offset in range(9):
        row_start, col_start = (2 - offset // 3, 2 - offset % 3)
        window = padded_grad[
            row_start : row_start + tile_rows, col_start : col_start + tile_cols
        ].reshape(tile_rows * tile_cols, channels)
        product = jnp.einsum(
            "pd,cd->pc", window, kernel[offset], preferred_element_type=jnp.float32
        )
        summed = product if summed is None else summed + product
    return summed


def normalize(values, inside, valid_count, norm_gain, norm_bias):
    centre = lax.psum(jnp.sum(values * inside, 0), ("blk", "batch")) / valid_count
    shifted = values - centre
    spread = lax.psum(jnp.sum(shifted * shifted * inside, 0), ("blk", "batch")) / valid_count
    inverse = lax.rsqrt(spread + EPSILON)
    normed = shifted * inverse
    return (normed * norm_gain + norm_bias, normed, inverse)


def normalize_back(grad_norm, normed, inverse, norm_gain, inside, valid_count):
    bias_sum, gain_sum = lax.psum(
        (jnp.sum(grad_norm, 0), jnp.sum(grad_norm * normed, 0)), ("blk", "batch")
    )
    grad_pre = (
        inverse
        * norm_gain
        * (grad_norm - bias_sum / valid_count - normed * gain_sum / valid_count)
        * inside
    )
    return (grad_pre.astype(jnp.bfloat16), gain_sum, bias_sum)


def on_device(
    features,
    crop_rows,
    crop_cols,
    depth_target,
    labels,
    first_weight,
    spatial_weight,
    last_weight,
    shared_weight,
    head_weights,
    message_weights,
    gate_weights,
    depth_weight,
    class_weight,
    mid_gain,
    mid_bias,
    out_gain,
    out_bias,
):
    tile_rows, tile_cols, in_width = (features.shape[1], features.shape[2], features.shape[3])
    pixels = tile_rows * tile_cols
    task_count = head_weights.shape[0]
    last_task = task_count - 1
    mid_share = mid_gain.shape[1]
    out_share = out_gain.shape[0]
    image_index = lax.axis_index("batch")
    first_row = lax.axis_index("blk") * tile_rows
    image_rows = lax.dynamic_index_in_dim(crop_rows, image_index, 0, False)
    image_cols = lax.dynamic_index_in_dim(crop_cols, image_index, 0, False)
    row_ids = first_row + jnp.arange(tile_rows, dtype=jnp.int32)
    col_ids = jnp.arange(tile_cols, dtype=jnp.int32)
    inside_grid = ((row_ids[:, None] < image_rows) & (col_ids[None, :] < image_cols)).astype(
        jnp.float32
    )
    inside = inside_grid.reshape(pixels, 1)
    valid_count = jnp.sum(crop_rows * crop_cols).astype(jnp.float32)
    full_first, full_spatial, full_last, gains_mid, biases_mid, gains_out, biases_out = (
        lax.all_gather(first_weight, "batch", axis=0, tiled=True),
        lax.all_gather(spatial_weight, "batch", axis=1, tiled=True),
        lax.all_gather(last_weight, "batch", axis=0, tiled=True),
        lax.all_gather(mid_gain, "batch", axis=1, tiled=True),
        lax.all_gather(mid_bias, "batch", axis=1, tiled=True),
        lax.all_gather(out_gain, "batch", axis=0, tiled=True),
        lax.all_gather(out_bias, "batch", axis=0, tiled=True),
    )
    gain_mid = gains_mid.astype(jnp.float32)
    bias_mid = biases_mid.astype(jnp.float32)
    gain_out = gains_out.astype(jnp.float32)
    bias_out = biases_out.astype(jnp.float32)
    mid_width = full_first.shape[1]
    input_rows = features.reshape(pixels, in_width)
    pre_one = jnp.dot(input_rows, full_first, preferred_element_type=jnp.float32)
    norm_one, normed_one, inverse_one = normalize(
        pre_one, inside, valid_count, gain_mid[0], bias_mid[0]
    )
    act_one = (jax.nn.silu(norm_one) * inside).astype(jnp.bfloat16)
    padded_one = extend_rows(act_one.reshape(tile_rows, tile_cols, mid_width))
    pre_two = conv_forward(padded_one, full_spatial, tile_rows, tile_cols)
    norm_two, normed_two, inverse_two = normalize(
        pre_two, inside, valid_count, gain_mid[1], bias_mid[1]
    )
    act_two = (jax.nn.silu(norm_two) * inside).astype(jnp.bfloat16)
    pre_three = jnp.dot(act_two, full_last, preferred_element_type=jnp.float32)
    norm_three, normed_three, inverse_three = normalize(
        pre_three, inside, valid_count, gain_out, bias_out
    )
    joined = norm_three + input_rows.astype(jnp.float32)
    act_three = (jax.nn.silu(joined) * inside).astype(jnp.bfloat16)
    full_shared, full_heads, full_messages, full_gates, full_depth, full_classes = (
        lax.all_gather(shared_weight, "batch", axis=0, tiled=True),
        lax.all_gather(head_weights, "batch", axis=2, tiled=True),
        lax.all_gather(message_weights, "batch", axis=2, tiled=True),
        lax.all_gather(gate_weights, "batch", axis=1, tiled=True),
        lax.all_gather(depth_weight, "batch", axis=0, tiled=True),
        lax.all_gather(class_weight, "batch", axis=0, tiled=True),
    )
    pre_four = jnp.dot(act_three, full_shared, preferred_element_type=jnp.float32)
    norm_four, normed_four, inverse_four = normalize(
        pre_four, inside, valid_count, gain_mid[2], bias_mid[2]
    )
    shared_act = (jax.nn.silu(norm_four) * inside).astype(jnp.bfloat16)
    padded_shared = extend_rows(shared_act.reshape(tile_rows, tile_cols, mid_width))
    pre_five = jnp.concatenate(
        [
            conv_forward(padded_shared, full_heads[task_id], tile_rows, tile_cols)
            for task_id in range(task_count)
        ],
        1,
    )
    task_gain = gain_mid[3 : 3 + task_count].reshape(-1)
    task_bias = bias_mid[3 : 3 + task_count].reshape(-1)
    norm_five, normed_five, inverse_five = normalize(
        pre_five, inside, valid_count, task_gain, task_bias
    )
    task_act = (jax.nn.silu(norm_five) * inside).astype(jnp.bfloat16)
    padded_tasks = extend_rows(task_act.reshape(tile_rows, tile_cols, task_count * mid_width))
    messages = jnp.concatenate(
        [
            conv_forward(
                padded_tasks[:, :, task_id * mid_width : (task_id + 1) * mid_width],
                full_messages[task_id],
                tile_rows,
                tile_cols,
            )
            for task_id in range(task_count)
        ],
        1,
    )
    gate_pre = jnp.concatenate(
        [
            jnp.dot(
                task_act[:, task_id * mid_width : (task_id + 1) * mid_width],
                full_gates[task_id],
                preferred_element_type=jnp.float32,
            )
            for task_id in range(task_count)
        ],
        1,
    )
    gate_open = jax.nn.sigmoid(gate_pre)
    gated_msgs = gate_open * messages
    task_float = task_act.astype(jnp.float32)
    pieces = [
        gated_msgs[:, task_id * mid_width : (task_id + 1) * mid_width]
        for task_id in range(task_count)
    ]
    summed = pieces[0]
    for task_id in range(1, task_count):
        summed = summed + pieces[task_id]
    depth_feat = (task_float[:, :mid_width] + summed - pieces[0]).astype(jnp.bfloat16)
    sem_feat = (task_float[:, last_task * mid_width :] + summed - pieces[last_task]).astype(
        jnp.bfloat16
    )
    depth_out = jnp.dot(depth_feat, full_depth, preferred_element_type=jnp.float32)
    logits = jnp.dot(sem_feat, full_classes, preferred_element_type=jnp.float32)
    inside_flat = inside[:, 0]
    depth_slope = ((depth_out - depth_target.reshape(pixels)) * inside_flat).astype(jnp.bfloat16)
    classes = logits.shape[1]
    onehot = (labels.reshape(pixels, 1) == jnp.arange(classes, dtype=jnp.int32)[None, :]).astype(
        jnp.float32
    )
    chances = jax.nn.softmax(logits, axis=1)
    logit_slope = ((chances - onehot) * inside).astype(jnp.bfloat16)
    grad_depth_w = jnp.dot(depth_slope, depth_feat, preferred_element_type=jnp.float32)
    grad_class_w = jnp.einsum(
        "pc,pk->ck", sem_feat, logit_slope, preferred_element_type=jnp.float32
    )
    depth_back = depth_slope.astype(jnp.float32)[:, None] * full_depth.astype(jnp.float32)[None, :]
    sem_back = jnp.einsum(
        "pk,ck->pc", logit_slope, full_classes, preferred_element_type=jnp.float32
    )
    piece_grads = []
    for task_id in range(task_count):
        incoming = []
        if task_id != 0:
            incoming.append(depth_back)
        if task_id != last_task:
            incoming.append(sem_back)
        piece_grad = incoming[0]
        for extra in incoming[1:]:
            piece_grad = piece_grad + extra
        piece_grads.append(piece_grad)
    grad_gated = jnp.concatenate(piece_grads, 1)
    grad_msg = (grad_gated * gate_open).astype(jnp.bfloat16)
    grad_gate = (grad_gated * messages * gate_open * (1.0 - gate_open)).astype(jnp.bfloat16)
    padded_grad_msg = extend_grads(grad_msg.reshape(tile_rows, tile_cols, task_count * mid_width))
    gate_grads = []
    message_grads = []
    task_grads = []
    for task_id in range(task_count):
        start_col, stop_col = (task_id * mid_width, (task_id + 1) * mid_width)
        gate_grads.append(
            jnp.einsum(
                "pc,pd->cd",
                task_act[:, start_col:stop_col],
                grad_gate[:, start_col:stop_col],
                preferred_element_type=jnp.float32,
            )
        )
        message_grads.append(
            conv_weights(
                padded_tasks[:, :, start_col:stop_col],
                grad_msg[:, start_col:stop_col],
                tile_rows,
                tile_cols,
            )
        )
        task_grad = jnp.einsum(
            "pd,cd->pc",
            grad_gate[:, start_col:stop_col],
            full_gates[task_id],
            preferred_element_type=jnp.float32,
        )
        task_grad = task_grad + conv_back(
            padded_grad_msg[:, :, start_col:stop_col], full_messages[task_id], tile_rows, tile_cols
        )
        if task_id == 0:
            task_grad = task_grad + depth_back
        if task_id == last_task:
            task_grad = task_grad + sem_back
        task_grads.append(task_grad)
    grad_gate_w = jnp.stack(gate_grads)
    grad_message_w = jnp.stack(message_grads)
    grad_task_act = jnp.concatenate(task_grads, 1)
    grad_norm_five = grad_task_act * inside * silu_slope(norm_five)
    grad_pre_five, gain_five, bias_five = normalize_back(
        grad_norm_five, normed_five, inverse_five, task_gain, inside, valid_count
    )
    padded_grad_five = extend_grads(
        grad_pre_five.reshape(tile_rows, tile_cols, task_count * mid_width)
    )
    grad_head_w = jnp.stack(
        [
            conv_weights(
                padded_shared,
                grad_pre_five[:, task_id * mid_width : (task_id + 1) * mid_width],
                tile_rows,
                tile_cols,
            )
            for task_id in range(task_count)
        ]
    )
    head_share = lax.psum_scatter(grad_head_w, "batch", scatter_dimension=2, tiled=True)
    shared_back = None
    for task_id in range(task_count):
        start_col, stop_col = (task_id * mid_width, (task_id + 1) * mid_width)
        returned = conv_back(
            padded_grad_five[:, :, start_col:stop_col], full_heads[task_id], tile_rows, tile_cols
        )
        shared_back = returned if shared_back is None else shared_back + returned
    grad_norm_four = shared_back * inside * silu_slope(norm_four)
    grad_pre_four, gain_four, bias_four = normalize_back(
        grad_norm_four, normed_four, inverse_four, gain_mid[2], inside, valid_count
    )
    grad_shared_w = jnp.einsum(
        "pc,pd->cd", act_three, grad_pre_four, preferred_element_type=jnp.float32
    )
    three_back = jnp.einsum(
        "pd,cd->pc", grad_pre_four, full_shared, preferred_element_type=jnp.float32
    )
    grad_joined = three_back * inside * silu_slope(joined)
    grad_pre_three, gain_three, bias_three = normalize_back(
        grad_joined, normed_three, inverse_three, gain_out, inside, valid_count
    )
    grad_last_w = jnp.einsum(
        "pc,pd->cd", act_two, grad_pre_three, preferred_element_type=jnp.float32
    )
    two_back = jnp.einsum(
        "pd,cd->pc", grad_pre_three, full_last, preferred_element_type=jnp.float32
    )
    grad_norm_two = two_back * inside * silu_slope(norm_two)
    grad_pre_two, gain_two, bias_two = normalize_back(
        grad_norm_two, normed_two, inverse_two, gain_mid[1], inside, valid_count
    )
    grad_spatial_w = conv_weights(padded_one, grad_pre_two, tile_rows, tile_cols)
    padded_grad_two = extend_grads(grad_pre_two.reshape(tile_rows, tile_cols, mid_width))
    one_back = conv_back(padded_grad_two, full_spatial, tile_rows, tile_cols)
    grad_norm_one = one_back * inside * silu_slope(norm_one)
    grad_pre_one, gain_one, bias_one = normalize_back(
        grad_norm_one, normed_one, inverse_one, gain_mid[0], inside, valid_count
    )
    grad_first_w = jnp.einsum(
        "pc,pd->cd", input_rows, grad_pre_one, preferred_element_type=jnp.float32
    )
    grad_input = (
        jnp.einsum("pd,cd->pc", grad_pre_one, full_first, preferred_element_type=jnp.float32)
        + grad_joined
    )
    (
        share_first,
        share_spatial,
        share_last,
        share_shared,
        share_messages,
        share_gates,
        share_depth,
        share_classes,
    ) = (
        lax.psum_scatter(grad_first_w, "batch", scatter_dimension=0, tiled=True),
        lax.psum_scatter(grad_spatial_w, "batch", scatter_dimension=1, tiled=True),
        lax.psum_scatter(grad_last_w, "batch", scatter_dimension=0, tiled=True),
        lax.psum_scatter(grad_shared_w, "batch", scatter_dimension=0, tiled=True),
        lax.psum_scatter(grad_message_w, "batch", scatter_dimension=2, tiled=True),
        lax.psum_scatter(grad_gate_w, "batch", scatter_dimension=1, tiled=True),
        lax.psum_scatter(grad_depth_w, "batch", scatter_dimension=0, tiled=True),
        lax.psum_scatter(grad_class_w, "batch", scatter_dimension=0, tiled=True),
    )
    (
        red_first,
        red_spatial,
        red_last,
        red_shared,
        red_heads,
        red_messages,
        red_gates,
        red_depth,
        red_classes,
    ) = (
        lax.psum(share_first.astype(jnp.bfloat16), "blk").astype(jnp.float32),
        lax.psum(share_spatial.astype(jnp.bfloat16), "blk").astype(jnp.float32),
        lax.psum(share_last.astype(jnp.bfloat16), "blk").astype(jnp.float32),
        lax.psum(share_shared.astype(jnp.bfloat16), "blk").astype(jnp.float32),
        lax.psum(head_share.astype(jnp.bfloat16), "blk").astype(jnp.float32),
        lax.psum(share_messages.astype(jnp.bfloat16), "blk").astype(jnp.float32),
        lax.psum(share_gates.astype(jnp.bfloat16), "blk").astype(jnp.float32),
        lax.psum(share_depth.astype(jnp.bfloat16), "blk").astype(jnp.float32),
        lax.psum(share_classes.astype(jnp.bfloat16), "blk").astype(jnp.float32),
    )
    mid_gain_full = jnp.concatenate(
        [gain_one[None], gain_two[None], gain_four[None], gain_five.reshape(task_count, mid_width)],
        0,
    )
    mid_bias_full = jnp.concatenate(
        [bias_one[None], bias_two[None], bias_four[None], bias_five.reshape(task_count, mid_width)],
        0,
    )
    grad_mid_gain = lax.dynamic_slice_in_dim(mid_gain_full, image_index * mid_share, mid_share, 1)
    grad_mid_bias = lax.dynamic_slice_in_dim(mid_bias_full, image_index * mid_share, mid_share, 1)
    grad_out_gain = lax.dynamic_slice_in_dim(gain_three, image_index * out_share, out_share, 0)
    grad_out_bias = lax.dynamic_slice_in_dim(bias_three, image_index * out_share, out_share, 0)
    return (
        depth_out.reshape(1, tile_rows, tile_cols),
        logits.reshape(1, tile_rows, tile_cols, classes),
        grad_input.reshape(1, tile_rows, tile_cols, in_width),
        red_first,
        red_spatial,
        red_last,
        red_shared,
        red_heads,
        red_messages,
        red_gates,
        red_depth,
        red_classes,
        grad_mid_gain,
        grad_mid_bias,
        grad_out_gain,
        grad_out_bias,
    )


def solution(mesh):
    placed = (
        P("batch", "blk", None, None),
        P(),
        P(),
        P("batch", "blk", None),
        P("batch", "blk", None),
        P("batch", None),
        P(None, "batch", None),
        P("batch", None),
        P("batch", None),
        P(None, None, "batch", None),
        P(None, None, "batch", None),
        P(None, "batch", None),
        P("batch"),
        P("batch", None),
        P(None, "batch"),
        P(None, "batch"),
        P("batch"),
        P("batch"),
    )
    return jax.shard_map(
        on_device,
        mesh=mesh,
        in_specs=placed,
        out_specs=(
            P("batch", "blk", None),
            P("batch", "blk", None, None),
            P("batch", "blk", None, None),
            P("batch", None),
            P(None, "batch", None),
            P("batch", None),
            P("batch", None),
            P(None, None, "batch", None),
            P(None, None, "batch", None),
            P(None, "batch", None),
            P("batch"),
            P("batch", None),
            P(None, "batch"),
            P(None, "batch"),
            P("batch"),
            P("batch"),
        ),
        check_vma=False,
    )
```

profile of v0, /device:TPU:0, one launch (start us, length us, event | category | flops | bytes accessed | tf_op | source)
XLA Modules:
  0.0 3163.1 jit_solution(10070790290487947501)
XLA Ops:
  15.3 27.9 all-gather.1
  43.3 26.2 all-gather
  71.0 2.5 multiply_reduce_fusion.14
  73.5 39.6 %psum.203 = f32[512]{0:T(512)S(1)} all-reduce(f32[512]{0:T(512)S(1)} %get-tuple-element.291), channel_id=1, replica_groups=mesh['blk'=4,'batch'=8] {'blk','batch'}, use_global_device_ids=true, to_apply=%region_1.2 | all-reduce | flops 512 | bytes 4096 | tf_op jit(solution)/shard_map/psum | solution.py:86
  113.2 41.3 %psum.204 = f32[512]{0:T(512)S(1)} all-reduce(f32[512]{0:T(512)S(1)} %multiply_reduce_fusion.13), channel_id=1, replica_groups=mesh['blk'=4,'batch'=8] {'blk','batch'}, use_global_device_ids=true, to_apply=%region_4.5 | all-reduce | flops 512 | bytes 4096 | tf_op jit(solution)/shard_map/psum | solution.py:88
  156.7 3.0 collective-permute-start
  159.7 19.6 all-gather.3
  179.4 16.4 all-gather.2
  204.2 38.7 %psum.205 = f32[512]{0:T(512)S(1)} all-reduce(f32[512]{0:T(512)S(1)} %get-tuple-element.293), channel_id=1, replica_groups=mesh['blk'=4,'batch'=8] {'blk','batch'}, use_global_device_ids=true, to_apply=%region_6.7 | all-reduce | flops 512 | bytes 4096 | tf_op jit(solution)/shard_map/psum | solution.py:86
  243.1 80.6 %psum.206 = f32[512]{0:T(512)S(1)} all-reduce(f32[512]{0:T(512)S(1)} %multiply_reduce_fusion.11), channel_id=1, replica_groups=mesh['blk'=4,'batch'=8] {'blk','batch'}, use_global_device_ids=true, to_apply=%region_8.9 | all-reduce | flops 512 | bytes 4096 | tf_op jit(solution)/shard_map/psum | solution.py:88
  324.3 2.6 multiply_reduce_fusion.5
  327.0 52.5 %psum.207 = f32[2048]{0:T(1024)S(1)} all-reduce(f32[2048]{0:T(1024)S(1)} %get-tuple-element.295), channel_id=1, replica_groups=mesh['blk'=4,'batch'=8] {'blk','batch'}, use_global_device_ids=true, to_apply=%region_10.11 | all-reduce | flops 2048 | bytes 16384 | tf_op jit(solution)/shard_map/psum | solution.py:86
  379.8 63.5 %psum.208 = f32[2048]{0:T(1024)S(1)} all-reduce(f32[2048]{0:T(1024)S(1)} %multiply_reduce_fusion.4), channel_id=1, replica_groups=mesh['blk'=4,'batch'=8] {'blk','batch'}, use_global_device_ids=true, to_apply=%region_12.13 | all-reduce | flops 2048 | bytes 16384 | tf_op jit(solution)/shard_map/psum | solution.py:88
  443.9 3.5 multiply_convert_fusion.6
  447.5 2.9 multiply_reduce_fusion.10
  450.4 57.5 %psum.209 = f32[512]{0:T(512)S(1)} all-reduce(f32[512]{0:T(512)S(1)} %get-tuple-element.297), channel_id=1, replica_groups=mesh['blk'=4,'batch'=8] {'blk','batch'}, use_global_device_ids=true, to_apply=%region_14.15 | all-reduce | flops 512 | bytes 4096 | tf_op jit(solution)/shard_map/psum | solution.py:86
  508.0 64.4 %psum.210 = f32[512]{0:T(512)S(1)} all-reduce(f32[512]{0:T(512)S(1)} %multiply_reduce_fusion.9), channel_id=1, replica_groups=mesh['blk'=4,'batch'=8] {'blk','batch'}, use_global_device_ids=true, to_apply=%region_16.17 | all-reduce | flops 512 | bytes 4096 | tf_op jit(solution)/shard_map/psum | solution.py:88
  574.6 3.0 collective-permute-start.2
  579.2 27.2 all-reduce.6
  607.6 30.8 all-gather.4
  667.6 68.8 %psum.211 = f32[2048]{0:T(1024)S(1)} all-reduce(f32[2048]{0:T(1024)S(1)} %multiply_reduce_fusion.3), channel_id=1, replica_groups=mesh['blk'=4,'batch'=8] {'blk','batch'}, use_global_device_ids=true, to_apply=%region_18.19 | all-reduce | flops 2048 | bytes 16384 | tf_op jit(solution)/shard_map/psum | solution.py:86
  736.7 63.7 %psum.212 = f32[2048]{0:T(1024)S(1)} all-reduce(f32[2048]{0:T(1024)S(1)} %multiply_reduce_fusion.2), channel_id=1, replica_groups=mesh['blk'=4,'batch'=8] {'blk','batch'}, use_global_device_ids=true, to_apply=%region_20.21 | all-reduce | flops 2048 | bytes 16384 | tf_op jit(solution)/shard_map/psum | solution.py:88
  804.7 3.7 collective-permute-start.4
  808.4 11.3 multiply_convert_fusion.4
  821.5 2.5 fusion.217
  830.8 201.4 %all-gather.25.cloned.1.call-done = bf16[4,9,512,512]{3,2,1,0:T(8,128)(2,1)} async-done(((bf16[4,9,64,512]{3,2,1,0:T(8,128)(2,1)}), bf16[4,9,512,512]{3,2,1,0:T(8,128)(2,1)}) %all-gather.25.cloned.1.call-update) | async-done | bytes 18874384 | tf_op jit(solution)/shard_map/all_gather | solution.py:179
  1039.3 3.6 pad_maximum_fusion.31
  1043.1 3.5 copy-done
  1076.0 3.7 collective-permute-start.6
  1079.7 2.8 fusion.6
  1084.4 2.4 pad_maximum_fusion.2
  1087.2 2.5 fusion.216
  1124.9 2.7 fusion.383
  1127.5 40.5 %all-reduce.12 = (f32[2048]{0:T(1024)S(1)}, f32[2048]{0:T(1024)S(1)}) all-reduce(f32[2048]{0:T(1024)S(1)} %get-tuple-element.83, f32[2048]{0:T(1024)S(1)} %get-tuple-element.82), channel_id=1, replica_groups=mesh['blk'=4,'batch'=8] {'blk','batch'}, use_global_device_ids=true, to_apply=%region_26.27 | all-reduce | flops 4096 | bytes 32768 | tf_op jit(solution)/shard_map/psum | solution.py:95
  1168.7 3.2 multiply_convert_fusion.1
  1173.4 3.0 collective-permute-start.8
  1176.5 3.2 fusion.16
  1203.1 40.1 %all-reduce.11 = (f32[512]{0:T(512)S(1)}, f32[512]{0:T(512)S(1)}) all-reduce(f32[512]{0:T(512)S(1)} %get-tuple-element.89, f32[512]{0:T(512)S(1)} %get-tuple-element.88), channel_id=1, replica_groups=mesh['blk'=4,'batch'=8] {'blk','batch'}, use_global_device_ids=true, to_apply=%region_30.31 | all-reduce | flops 1024 | bytes 8192 | tf_op jit(solution)/shard_map/psum | solution.py:95
  1244.5 6.4 fusion.382
  1250.9 40.4 %all-reduce.10 = (f32[2048]{0:T(1024)S(1)}, f32[2048]{0:T(1024)S(1)}) all-reduce(f32[2048]{0:T(1024)S(1)} %get-tuple-element.81, f32[2048]{0:T(1024)S(1)} %get-tuple-element.80), channel_id=1, replica_groups=mesh['blk'=4,'batch'=8] {'blk','batch'}, use_global_device_ids=true, to_apply=%region_34.35 | all-reduce | flops 4096 | bytes 32768 | tf_op jit(solution)/shard_map/psum | solution.py:95
  1291.4 3.4 multiply_convert_fusion
  1295.8 3.4 fusion.380
  1299.3 4.6 fusion.409
  1304.0 3.9 fusion.385
  1307.9 41.9 %all-reduce.9 = (f32[512]{0:T(512)S(1)}, f32[512]{0:T(512)S(1)}) all-reduce(f32[512]{0:T(512)S(1)} %get-tuple-element.87, f32[512]{0:T(512)S(1)} %get-tuple-element.86), channel_id=1, replica_groups=mesh['blk'=4,'batch'=8] {'blk','batch'}, use_global_device_ids=true, to_apply=%region_38.39 | all-reduce | flops 1024 | bytes 8192 | tf_op jit(solution)/shard_map/psum | solution.py:95
  1352.7 3.0 collective-permute-start.10
  1365.2 43.1 %all-reduce.8 = (f32[512]{0:T(512)S(1)}, f32[512]{0:T(512)S(1)}) all-reduce(f32[512]{0:T(512)S(1)} %get-tuple-element.85, f32[512]{0:T(512)S(1)} %get-tuple-element.84), channel_id=1, replica_groups=mesh['blk'=4,'batch'=8] {'blk','batch'}, use_global_device_ids=true, to_apply=%region_42.43 | all-reduce | flops 1024 | bytes 8192 | tf_op jit(solution)/shard_map/psum | solution.py:95
  1410.6 4.6 convolution_bitcast_fusion
  1415.3 2.5 fusion.98
  1449.6 17.3 pad_maximum_fusion.1
  1485.1 12.7 pad_maximum_fusion
  1505.3 67.5 %reduce-scatter.11.cloned.1.call-done = f32[256,512]{0,1:T(8,128)} async-done(((f32[2048,512]{0,1:T(8,128)}), f32[256,512]{0,1:T(8,128)}) %reduce-scatter.11.cloned.1.call-update) | async-done | bytes 524304 | tf_op jit(solution)/shard_map/reduce_scatter | solution.py:386
  1574.5 165.2 %reduce-scatter.13.cloned.1.call-done = f32[9,64,512]{2,1,0:T(8,128)} async-done(((f32[9,512,512]{2,1,0:T(8,128)}), f32[9,64,512]{2,1,0:T(8,128)}) %reduce-scatter.13.cloned.1.call-update) | async-done | bytes 1179664 | tf_op jit(solution)/shard_map/reduce_scatter | solution.py:387
  1741.8 605.0 %reduce-scatter.21.cloned.1.call-done = f32[4,9,64,512]{3,2,1,0:T(8,128)} async-done(((f32[4,9,512,512]{3,2,1,0:T(8,128)}), f32[4,9,64,512]{3,2,1,0:T(8,128)}) %reduce-scatter.21.cloned.1.call-update) | async-done | bytes 4718608 | tf_op jit(solution)/shard_map/reduce_scatter | solution.py:390
  2346.8 4.1 convert_element_type.201
  2350.9 603.6 %reduce-scatter.19.cloned.1.call-done = f32[4,9,64,512]{3,2,1,0:T(8,128)} async-done(((f32[4,9,512,512]{3,2,1,0:T(8,128)}), f32[4,9,64,512]{3,2,1,0:T(8,128)}) %reduce-scatter.19.cloned.1.call-update) | async-done | bytes 4718608 | tf_op jit(solution)/shard_map/reduce_scatter | solution.py:330
  2954.5 4.1 convert_element_type.199
  2961.1 19.4 all-reduce.7
  2980.6 37.4 %reduce-scatter.25.cloned.1.call-done = f32[64,40]{1,0:T(8,128)} async-done(((f32[512,40]{1,0:T(8,128)}), f32[64,40]{1,0:T(8,128)}) %reduce-scatter.25.cloned.1.call-update) | async-done | bytes 10256
  3018.8 10.1 all-reduce.13
  3032.1 4.0 convolution_add_fusion
  3036.0 106.7 %all-reduce.17.cloned.1.call-done = (bf16[256,512]{0,1:T(8,128)(2,1)}, bf16[9,64,512]{2,1,0:T(8,128)(2,1)}, bf16[64,2048]{1,0:T(8,128)(2,1)}, bf16[256,512]{1,0:...) async-done(((bf16[256,512]{0,1:T(8,128)(2,1)}, bf16[9,64,512]{2,1,0:T(8,128)(2,1)}, ...) | async-done | bytes 6357008 | tf_op jit(solution)/shard_map/psum | solution.py:406
  3149.6 2.8 convert_element_type.200
  3152.5 2.9 convert_element_type.202
  (956 shorter events, 255.3 us)
Async XLA Ops:
  7.2 63.7 %all-gather.13.cloned.1.call-start = ((), (), s32[]{:S(2)}) async-start(), calls=%async_computation.8 | async-start | bytes 2359296 | tf_op jit(solution)/shard_map/all_gather | solution.py:145
  7.9 189.2 %all-gather.15.cloned.1.call-start = ((), (), s32[]{:S(2)}) async-start(), calls=%async_computation.9 | async-start | bytes 5308416 | tf_op jit(solution)/shard_map/all_gather | solution.py:146
  8.7 315.6 %all-gather.17.cloned.1.call-start = ((), (), s32[]{:S(2)}) async-start(), calls=%async_computation.10 | async-start | bytes 2359296 | tf_op jit(solution)/shard_map/all_gather | solution.py:147
  9.4 438.1 %all-gather.19.cloned.1.call-start = ((), (), s32[]{:S(2)}) async-start(), calls=%async_computation.11 | async-start | bytes 2359296 | tf_op jit(solution)/shard_map/all_gather | solution.py:177
  10.0 60.9 %copy-start.61 = (bf16[1,8,40,2048]{3,2,1,0:T(8,128)(2,1)S(1)}, bf16[1,8,40,2048]{3,2,1,0:T(8,128)(2,1)}, u32[]{:S(2)}) copy-start(bf16[1,8,40,2048]{3,2,1,0:T(8,128)(2,1)} %param.18) | copy-start | bytes 3932164
  10.0 630.3 %all-gather.21.cloned.1.call-start = ((), (), s32[]{:S(2)}) async-start(), calls=%async_computation.12 | async-start | bytes 21233664 | tf_op jit(solution)/shard_map/all_gather | solution.py:178
  10.6 810.9 %all-gather.23.cloned.1.call-start = ((), (), s32[]{:S(2)}) async-start(), calls=%async_computation.13 | async-start | bytes 2359296 | tf_op jit(solution)/shard_map/all_gather | solution.py:180
  11.2 1021.0 %all-gather.25.cloned.1.call-start = ((), (), s32[]{:S(2)}) async-start(), calls=%async_computation.14 | async-start | bytes 21233664 | tf_op jit(solution)/shard_map/all_gather | solution.py:179
  11.9 1487.9 %reduce-scatter.23.cloned.1.call-start = ((), (), s32[]{:S(2)}) async-start(), calls=%async_computation.21 | async-start | bytes 4718592 | tf_op jit(solution)/shard_map/reduce_scatter | solution.py:391
  15.2 55.6 %copy-start.241 = (pred[320]{0:T(512)(128)(4,1)}, pred[320]{0:T(512)(128)(4,1)S(1)}, u32[]{:S(2)}) copy-start(pred[320]{0:T(512)(128)(4,1)S(1)} %and.27) | copy-start | bytes 964
  70.8 84.3 %copy-start.228 = (f32[1,512]{1,0:T(1,128)}, f32[1,512]{1,0:T(1,128)S(1)}, u32[]{:S(2)}) copy-start(f32[1,512]{1,0:T(1,128)S(1)} %get-tuple-element.284) | copy-start | bytes 6148
  70.8 253.5 %copy-start.239 = (f32[1,512]{1,0:T(1,128)}, f32[1,512]{1,0:T(1,128)S(1)}, u32[]{:S(2)}) copy-start(f32[1,512]{1,0:T(1,128)S(1)} %get-tuple-element.283) | copy-start | bytes 6148
  70.8 502.2 %copy-start.218 = (f32[1,512]{1,0:T(1,128)}, f32[1,512]{1,0:T(1,128)S(1)}, u32[]{:S(2)}) copy-start(f32[1,512]{1,0:T(1,128)S(1)} %get-tuple-element.282) | copy-start | bytes 6148
  70.9 84.2 %copy-start.208 = (f32[1,512]{1,0:T(1,128)}, f32[1,512]{1,0:T(1,128)S(1)}, u32[]{:S(2)}) copy-start(f32[1,512]{1,0:T(1,128)S(1)} %get-tuple-element.281) | copy-start | bytes 6148
  70.9 253.4 %copy-start.230 = (f32[1,512]{1,0:T(1,128)}, f32[1,512]{1,0:T(1,128)S(1)}, u32[]{:S(2)}) copy-start(f32[1,512]{1,0:T(1,128)S(1)} %get-tuple-element.280) | copy-start | bytes 6148
  70.9 502.1 %copy-start.202 = (f32[1,512]{1,0:T(1,128)}, f32[1,512]{1,0:T(1,128)S(1)}, u32[]{:S(2)}) copy-start(f32[1,512]{1,0:T(1,128)S(1)} %get-tuple-element.279) | copy-start | bytes 6148
  70.9 88.8 %copy-start.245 = (bf16[256]{0:T(256)(128)(2,1)S(1)}, bf16[256]{0:T(256)(128)(2,1)}, u32[]{:S(2)}) copy-start(bf16[256]{0:T(256)(128)(2,1)} %param.35) | copy-start | bytes 1540
  70.9 108.5 %copy-start.246 = (bf16[256]{0:T(256)(128)(2,1)S(1)}, bf16[256]{0:T(256)(128)(2,1)}, u32[]{:S(2)}) copy-start(bf16[256]{0:T(256)(128)(2,1)} %param.34) | copy-start | bytes 1540
  73.5 123.5 %copy-start.56 = (f32[320,512]{1,0:T(8,128)}, f32[320,512]{1,0:T(8,128)S(1)}, u32[]{:S(2)}) copy-start(f32[320,512]{1,0:T(8,128)S(1)} %get-tuple-element.292) | copy-start | bytes 1966084
  113.1 83.9 %copy-start.189 = (f32[512]{0:T(512)}, f32[512]{0:T(512)S(1)}, u32[]{:S(2)}) copy-start(f32[512]{0:T(512)S(1)} %broadcast_divide_fusion.9) | copy-start | bytes 6148
  155.1 41.9 %copy-start.204 = (f32[512]{0:T(512)}, f32[512]{0:T(512)S(1)}, u32[]{:S(2)}) copy-start(f32[512]{0:T(512)S(1)} %get-tuple-element.110) | copy-start | bytes 6148
  155.3 47.5 %copy-start.46 = (bf16[320,512]{1,0:T(8,128)(2,1)}, bf16[320,512]{1,0:T(8,128)(2,1)S(1)}, u32[]{:S(2)}) copy-start(bf16[320,512]{1,0:T(8,128)(2,1)S(1)} %multiply_convert_fusion.12) | copy-start | bytes 983044
  155.4 40.5 %collective-permute-start.1 = (bf16[1,40,512]{2,1,0:T(8,128)(2,1)S(1)}, bf16[1,40,512]{2,1,0:T(8,128)(2,1)S(1)}, u32[]{:S(2)}, u32[]{:S(2)}) collective-permute-start(bf16[1,40,512]{2,1,0:T(8,128)(2,1)S(1)} %get-tuple-element.278), channel_id=1, source_target_pairs={{8,0},{16,8},{24,16},{9,1},{17,9},{25,17},{10,2},{18,10},{26,18},{... | collective-permute-start | bytes 122888 | tf_op jit(solution)/shard_map/ppermute | solution.py:19
  156.7 39.2 %collective-permute-start = (bf16[1,40,512]{2,1,0:T(8,128)(2,1)S(1)}, bf16[1,40,512]{2,1,0:T(8,128)(2,1)S(1)}, u32[]{:S(2)}, u32[]{:S(2)}) collective-permute-start(bf16[1,40,512]{2,1,0:T(8,128)(2,1)S(1)} %get-tuple-element.277), channel_id=1, source_target_pairs={{0,8},{8,16},{16,24},{1,9},{9,17},{17,25},{2,10},{10,18},{18,26},{... | collective-permute-start | bytes 122888 | tf_op jit(solution)/shard_map/ppermute | solution.py:17
  179.4 264.5 %copy-start.191 = (f32[8,1,256]{2,1,0:T(1,128)}, f32[8,1,256]{2,1,0:T(1,128)S(1)}, u32[]{:S(2)}) copy-start(f32[8,1,256]{2,1,0:T(1,128)S(1)} %convert_element_type.212) | copy-start | bytes 24580
  204.2 122.7 %copy-start.58 = (f32[320,512]{1,0:T(8,128)}, f32[320,512]{1,0:T(8,128)S(1)}, u32[]{:S(2)}) copy-start(f32[320,512]{1,0:T(8,128)S(1)} %get-tuple-element.294) | copy-start | bytes 1966084
  243.0 83.9 %copy-start.206 = (f32[512]{0:T(512)}, f32[512]{0:T(512)S(1)}, u32[]{:S(2)}) copy-start(f32[512]{0:T(512)S(1)} %broadcast_divide_fusion.8) | copy-start | bytes 6148
  326.9 120.5 %copy-start.25 = (f32[320,2048]{1,0:T(8,128)}, f32[320,2048]{1,0:T(8,128)S(1)}, u32[]{:S(2)}) copy-start(f32[320,2048]{1,0:T(8,128)S(1)} %get-tuple-element.296) | copy-start | bytes 7864324
  447.4 130.2 %copy-start.238 = (u32[32]{0:T(128)S(1)}, u32[32]{0:T(128)}, u32[]{:S(2)}) copy-start(u32[32]{0:T(128)} %constant.64) | copy-start | bytes 388
  447.4 131.5 %copy-start.247 = (bf16[64]{0:T(256)(128)(2,1)S(1)}, bf16[64]{0:T(256)(128)(2,1)}, u32[]{:S(2)}) copy-start(bf16[64]{0:T(256)(128)(2,1)} %param.30) | copy-start | bytes 388
  447.4 160.1 %copy-start.220 = (bf16[64,40]{0,1:T(8,128)(2,1)S(1)}, bf16[64,40]{0,1:T(8,128)(2,1)}, u32[]{:S(2)}) copy-start(bf16[64,40]{0,1:T(8,128)(2,1)} %param.31) | copy-start | bytes 15364
  447.4 191.1 %copy-start.234 = (f32[1,8,40]{2,1,0:T(8,128)S(1)}, f32[1,8,40]{2,1,0:T(8,128)}, u32[]{:S(2)}) copy-start(f32[1,8,40]{2,1,0:T(8,128)} %param.21) | copy-start | bytes 3844
  447.5 191.8 %copy-start.235 = (s32[1,8,40]{2,1,0:T(8,128)S(1)}, s32[1,8,40]{2,1,0:T(8,128)}, u32[]{:S(2)}) copy-start(s32[1,8,40]{2,1,0:T(8,128)} %param.22) | copy-start | bytes 3844
  450.4 189.5 %copy-start.41 = (f32[320,512]{1,0:T(8,128)}, f32[320,512]{1,0:T(8,128)S(1)}, u32[]{:S(2)}) copy-start(f32[320,512]{1,0:T(8,128)S(1)} %get-tuple-element.298) | copy-start | bytes 1966084
  573.3 91.6 %copy-start.9 = (bf16[320,512]{1,0:T(8,128)(2,1)}, bf16[320,512]{1,0:T(8,128)(2,1)S(1)}, u32[]{:S(2)}) copy-start(bf16[320,512]{1,0:T(8,128)(2,1)S(1)} %multiply_convert_fusion.10) | copy-start | bytes 983044
  573.3 66.6 %collective-permute-start.3 = (bf16[1,40,512]{2,1,0:T(8,128)(2,1)S(1)}, bf16[1,40,512]{2,1,0:T(8,128)(2,1)S(1)}, u32[]{:S(2)}, u32[]{:S(2)}) collective-permute-start(bf16[1,40,512]{2,1,0:T(8,128)(2,1)S(1)} %get-tuple-element.274), channel_id=1, source_target_pairs={{8,0},{16,8},{24,16},{9,1},{17,9},{25,17},{10,2},{18,10},{26,18},{... | collective-permute-start | bytes 122888 | tf_op jit(solution)/shard_map/ppermute | solution.py:19
  574.6 65.3 %collective-permute-start.2 = (bf16[1,40,512]{2,1,0:T(8,128)(2,1)S(1)}, bf16[1,40,512]{2,1,0:T(8,128)(2,1)S(1)}, u32[]{:S(2)}, u32[]{:S(2)}) collective-permute-start(bf16[1,40,512]{2,1,0:T(8,128)(2,1)S(1)} %get-tuple-element.273), channel_id=1, source_target_pairs={{0,8},{8,16},{16,24},{1,9},{9,17},{17,25},{2,10},{10,18},{18,26},{... | collective-permute-start | bytes 122888 | tf_op jit(solution)/shard_map/ppermute | solution.py:17
  666.6 457.8 %copy-start.2 = (f32[320,512]{1,0:T(8,128)}, f32[320,512]{1,0:T(8,128)S(1)}, u32[]{:S(2)}) copy-start(f32[320,512]{1,0:T(8,128)S(1)} %fusion.102) | copy-start | bytes 1966084
  667.0 457.4 %copy-start.4 = (f32[320,512]{1,0:T(8,128)}, f32[320,512]{1,0:T(8,128)S(1)}, u32[]{:S(2)}) copy-start(f32[320,512]{1,0:T(8,128)S(1)} %fusion.101) | copy-start | bytes 1966084
  667.3 141.0 %copy-start.6 = (f32[320,512]{1,0:T(8,128)}, f32[320,512]{1,0:T(8,128)S(1)}, u32[]{:S(2)}) copy-start(f32[320,512]{1,0:T(8,128)S(1)} %fusion.100) | copy-start | bytes 1966084
  803.4 231.2 %collective-permute-start.5 = (bf16[1,40,2048]{2,1,0:T(8,128)(2,1)}, bf16[1,40,2048]{2,1,0:T(8,128)(2,1)S(1)}, u32[]{:S(2)}, u32[]{:S(2)}) collective-permute-start(bf16[1,40,2048]{2,1,0:T(8,128)(2,1)} %get-tuple-element.248), channel_id=1, source_target_pairs={{8,0},{16,8},{24,16},{9,1},{17,9},{25,17},{10,2},{18,10},{26,18},{... | collective-permute-start | bytes 491528 | tf_op jit(solution)/shard_map/ppermute | solution.py:19
  804.7 229.9 %collective-permute-start.4 = (bf16[1,40,2048]{2,1,0:T(8,128)(2,1)}, bf16[1,40,2048]{2,1,0:T(8,128)(2,1)}, u32[]{:S(2)}, u32[]{:S(2)}) collective-permute-start(bf16[1,40,2048]{2,1,0:T(8,128)(2,1)} %get-tuple-element.247), channel_id=1, source_target_pairs={{0,8},{8,16},{16,24},{1,9},{9,17},{17,25},{2,10},{10,18},{18,26},{... | collective-permute-start | bytes 491528 | tf_op jit(solution)/shard_map/ppermute | solution.py:17
  826.4 208.2 %copy-start.27 = (bf16[8,40,2048]{2,1,0:T(8,128)(2,1)S(1)}, bf16[8,40,2048]{2,1,0:T(8,128)(2,1)}, u32[]{:S(2)}) copy-start(bf16[8,40,2048]{2,1,0:T(8,128)(2,1)} %copy-done.26) | copy-start | bytes 3932164
  1074.5 21.4 collective-permute-start.7
  1076.0 19.9 collective-permute-start.6
  1086.8 414.9 %reduce-scatter.15.cloned.1.call-start = ((), (), s32[]{:S(2)}) async-start(), calls=%async_computation.17 | async-start | bytes 4718592 | tf_op jit(solution)/shard_map/reduce_scatter | solution.py:388
  1172.0 9.2 collective-permute-start.9
  1173.4 7.8 collective-permute-start.8
  1201.2 42.0 %copy-start.227 = (f32[512]{0:T(512)S(1)}, f32[512]{0:T(512)}, u32[]{:S(2)}) copy-start(f32[512]{0:T(512)} %get-tuple-element.115) | copy-start | bytes 6148
  1201.2 43.3 %copy-start.192 = (f32[8,1,256]{2,1,0:T(1,128)S(1)}, f32[8,1,256]{2,1,0:T(1,128)}, u32[]{:S(2)}) copy-start(f32[8,1,256]{2,1,0:T(1,128)} %copy-done.191) | copy-start | bytes 24580
  1244.5 46.8 %copy-start.193 = (f32[2048]{0:T(1024)S(1)}, f32[2048]{0:T(1024)}, u32[]{:S(2)}) copy-start(f32[2048]{0:T(1024)} %get-tuple-element.113) | copy-start | bytes 24580
  1299.3 204.2 %reduce-scatter.17.cloned.1.call-start = ((), (), s32[]{:S(2)}) async-start(), calls=%async_computation.18 | async-start | bytes 4718592 | tf_op jit(solution)/shard_map/reduce_scatter | solution.py:389
  1303.9 45.9 %copy-start.224 = (f32[512]{0:T(512)S(1)}, f32[512]{0:T(512)}, u32[]{:S(2)}) copy-start(f32[512]{0:T(512)} %get-tuple-element.111) | copy-start | bytes 6148
  1304.0 268.8 %reduce-scatter.11.cloned.1.call-start = ((), (), s32[]{:S(2)}) async-start(), calls=%async_computation.15 | async-start | bytes 4718592 | tf_op jit(solution)/shard_map/reduce_scatter | solution.py:386
  1351.4 4.3 collective-permute-start.11
  1352.7 3.9 collective-permute-start.10
  1363.7 44.7 %copy-start.223 = (f32[512]{0:T(512)S(1)}, f32[512]{0:T(512)}, u32[]{:S(2)}) copy-start(f32[512]{0:T(512)} %get-tuple-element.109) | copy-start | bytes 6148
  1415.3 324.4 %reduce-scatter.13.cloned.1.call-start = ((), (), s32[]{:S(2)}) async-start(), calls=%async_computation.16 | async-start | bytes 10616832 | tf_op jit(solution)/shard_map/reduce_scatter | solution.py:387
  1429.7 917.1 %reduce-scatter.21.cloned.1.call-start = ((), (), s32[]{:S(2)}) async-start(), calls=%async_computation.20 | async-start | bytes 42467328 | tf_op jit(solution)/shard_map/reduce_scatter | solution.py:390
  1466.9 1487.6 %reduce-scatter.19.cloned.1.call-start = ((), (), s32[]{:S(2)}) async-start(), calls=%async_computation.19 | async-start | bytes 42467328 | tf_op jit(solution)/shard_map/reduce_scatter | solution.py:330
  1497.8 1520.2 %reduce-scatter.25.cloned.1.call-start = ((), (), s32[]{:S(2)}) async-start(), calls=%async_computation.22 | async-start | bytes 294912
  1499.8 1642.9 %all-reduce.17.cloned.1.call-start = ((), (), s32[]{:S(2)}) async-start(), calls=%async_computation.23 | async-start | bytes 12713984 | tf_op jit(solution)/shard_map/psum | solution.py:406
  2958.6 73.4 %copy-start.43 = (f32[320,2048]{1,0:T(8,128)S(1)}, f32[320,2048]{1,0:T(8,128)}, u32[]{:S(2)}) copy-start(f32[320,2048]{1,0:T(8,128)} %get-tuple-element.303) | copy-start | bytes 7864324
  2958.6 73.4 %copy-start.149 = (bf16[320,512]{1,0:T(8,128)(2,1)S(1)}, bf16[320,512]{1,0:T(8,128)(2,1)}, u32[]{:S(2)}) copy-start(bf16[320,512]{1,0:T(8,128)(2,1)} %copy-done.148) | copy-start | bytes 983044
  (224 other events, 1176.2 us)
Sparse Core Ops, SparseCore 0:
  10.1 52.1 all-gather.12
  64.5 81.0 all-gather.14
  147.7 47.8 all-gather.16
  197.6 48.1 all-gather.18
  247.2 368.5 all-gather.20
  617.8 49.5 all-gather.22
  668.9 363.2 all-gather.24
  1086.9 88.2 reduce-scatter.22
  1299.4 89.1 reduce-scatter.14
  1392.0 87.9 reduce-scatter.16
  1484.7 88.0 reduce-scatter.10
  1576.2 163.4 reduce-scatter.12
  1743.6 603.1 reduce-scatter.20
  2351.0 603.4 reduce-scatter.18
  2957.7 60.2 reduce-scatter.24
  3021.9 120.8 all-reduce.16
where the time goes:
time: 3170 us; the launch traced here: 3160 us
  waiting for transfers between devices  1790 us (56%)
  blocking collectives  954 us (30%)
  matrix products  203 us (6%)
  other arithmetic  121 us (4%)
  local copies, waits for them, and re-layouts  42.7 us (1%)
    reduce_scatter x1, waiting for transfers between devices, on_device(): lax.psum_scatter(grad_message_w, 'batch', scatter_dimension=2, tiled=True)  605 us
    reduce_scatter x1, waiting for transfers between devices, on_device(): lax.psum_scatter(grad_head_w, 'batch', scatter_dimension=2, tiled=True)  604 us
    psum x5, blocking collectives, normalize(): lax.psum(jnp.sum(shifted * shifted * inside, 0), ('blk', 'batch'))  313 us
    psum x5, blocking collectives, normalize(): lax.psum(jnp.sum(values * inside, 0), ('blk', 'batch')) / valid_count  257 us
    psum x5, blocking collectives, normalize_back(): lax.psum((jnp.sum(grad_norm, 0), jnp.sum(grad_norm * normed, 0)), ('blk',...  206 us
    all_gather x1, waiting for transfers between devices, on_device(): lax.all_gather(message_weights, 'batch', axis=2, tiled=True)  201 us
    reduce_scatter x1, waiting for transfers between devices, on_device(): lax.psum_scatter(grad_spatial_w, 'batch', scatter_dimension=1, tiled=True)  165 us
    psum x1, waiting for transfers between devices, on_device(): lax.psum(share_first.astype(jnp.bfloat16), 'blk').astype(jnp.float32)  107 us
  transfers between devices with their start and end apart: 28, of which 8 were waited for; matrix products, arithmetic and copies ran while one was open for 10% of the time, Pallas kernels for 0%

commit v1 on v0

v1 whole, which is shorter than its diff:
```python
import functools

import jax
import jax.numpy as jnp
from jax import lax
from jax.experimental import pallas as pl
from jax.experimental.pallas import tpu as pltpu
from jax.sharding import PartitionSpec as P

EPSILON = 1e-05
MESH = pl.DeviceIdType.MESH
BF16 = jnp.bfloat16
F32 = jnp.float32
LANES = 128


def greet(peers):
    barrier = pltpu.get_barrier_semaphore()
    for peer in peers:
        pl.semaphore_signal(barrier, inc=1, device_id=peer, device_id_type=MESH)
    pl.semaphore_wait(barrier, len(peers))


def send(src, dst, send_sem, recv_sem, peer):
    copy = pltpu.make_async_remote_copy(
        src_ref=src,
        dst_ref=dst,
        send_sem=send_sem,
        recv_sem=recv_sem,
        device_id=peer,
        device_id_type=MESH,
    )
    copy.start()
    return copy


def first_kernel(images, weight, small, full, smalls, own, zs, xs, cs, ps):
    blk, batch = lax.axis_index("blk"), lax.axis_index("batch")
    half = weight.shape[0] // 2
    rows = pl.ds(pl.multiple_of(lax.rem(blk, 2) * half, half), half)
    side = (blk, batch ^ 1)
    mate = (blk ^ 1, batch)
    lines = range(1, images // 2)
    others = [(blk, batch ^ mask) for mask in range(1, images)]
    greet(others + [mate])
    copies = []
    here = pltpu.make_async_copy(weight, full.at[batch], own.at[0])
    here.start()
    here_small = pltpu.make_async_copy(small, smalls.at[batch], own.at[1])
    here_small.start()
    z_copies = {}
    for mask in lines:
        z_copies[mask] = send(
            weight.at[rows],
            full.at[batch, rows],
            zs.at[0, mask],
            zs.at[1, mask],
            (blk, batch ^ (2 * mask)),
        )
    x_copies = {
        0: send(weight.at[rows], full.at[batch, rows], xs.at[0, 0], xs.at[1, 0], side)
    }
    for place, peer in enumerate(others):
        copies.append(
            send(small, smalls.at[batch], ps.at[0, place], ps.at[1, place], peer)
        )
    core_copies = []

    def hand_over(source, mask):
        block = full.at[source, rows]
        core_copies.append(send(block, block, cs.at[0, mask], cs.at[1, mask], mate))

    for mask in lines:
        z_copies[mask].wait_recv()
        source = batch ^ (2 * mask)
        block = full.at[source, rows]
        x_copies[mask] = send(block, block, xs.at[0, mask], xs.at[1, mask], side)
        hand_over(source, 2 * mask)
    for mask in range(images // 2):
        x_copies[mask].wait_recv()
        hand_over(batch ^ (2 * mask + 1), 2 * mask + 1)
    for copy in core_copies + copies:
        copy.wait()
    for mask in lines:
        z_copies[mask].wait_send()
    for mask in range(images // 2):
        x_copies[mask].wait_send()
    here.wait()
    here_small.wait()


def gather_first(weight, small, images):
    any_place = pl.BlockSpec(memory_space=pl.ANY)
    dma = pltpu.SemaphoreType.DMA
    return pl.pallas_call(
        functools.partial(first_kernel, images),
        out_shape=(
            jax.ShapeDtypeStruct((images,) + weight.shape, weight.dtype),
            jax.ShapeDtypeStruct((images,) + small.shape, small.dtype),
        ),
        in_specs=[any_place] * 2,
        out_specs=(any_place, any_place),
        scratch_shapes=[
            dma((2,)),
            dma((2, images)),
            dma((2, images)),
            dma((2, images)),
            dma((2, images)),
        ],
        compiler_params=pltpu.CompilerParams(collective_id=0, has_side_effects=True),
    )(weight, small)


def tiles_kernel(block, every, own, sems):
    blk, batch = lax.axis_index("blk"), lax.axis_index("batch")
    mate, across = (blk ^ 1, batch), (blk ^ 2, batch)
    greet([mate, across])
    far = send(block, every.at[blk], sems.at[0, 0], sems.at[1, 0], across)
    near = send(block, every.at[blk], sems.at[0, 1], sems.at[1, 1], mate)
    here = pltpu.make_async_copy(block, every.at[blk], own.at[0])
    here.start()
    far.wait_recv()
    passed = every.at[blk ^ 2]
    last = send(passed, passed, sems.at[0, 2], sems.at[1, 2], mate)
    near.wait()
    last.wait()
    far.wait_send()
    here.wait()


def gather_tiles(block, ident):
    any_place = pl.BlockSpec(memory_space=pl.ANY)
    dma = pltpu.SemaphoreType.DMA
    return pl.pallas_call(
        tiles_kernel,
        out_shape=jax.ShapeDtypeStruct((4,) + block.shape, block.dtype),
        in_specs=[any_place],
        out_specs=any_place,
        scratch_shapes=[dma((1,)), dma((2, 3))],
        compiler_params=pltpu.CompilerParams(collective_id=ident, has_side_effects=True),
    )(block)


def sum_kernel(parts, total, near_in, pair, far_in, sems):
    blk, batch = lax.axis_index("blk"), lax.axis_index("batch")
    mate, across = (blk ^ 1, batch), (blk ^ 2, batch)
    greet([mate, across])
    far_first = send(parts.at[blk ^ 3], near_in.at[0], sems.at[0, 0], sems.at[1, 0], mate)
    near_next = send(parts.at[blk ^ 1], near_in.at[1], sems.at[0, 1], sems.at[1, 1], mate)
    far_first.wait_recv()
    pair[...] = (parts[blk ^ 2].astype(F32) + near_in[0].astype(F32)).astype(pair.dtype)
    far = send(pair, far_in, sems.at[0, 2], sems.at[1, 2], across)
    near_next.wait_recv()
    total[...] = parts[blk].astype(F32) + near_in[1].astype(F32)
    far.wait_recv()
    total[...] += far_in[...].astype(F32)
    far_first.wait_send()
    near_next.wait_send()
    far.wait_send()


def sum_tiles(parts, ident):
    dma = pltpu.SemaphoreType.DMA
    block = parts.shape[1:]
    vmem = pl.BlockSpec(memory_space=pltpu.VMEM)
    return pl.pallas_call(
        sum_kernel,
        out_shape=jax.ShapeDtypeStruct(block, F32),
        in_specs=[vmem],
        out_specs=vmem,
        scratch_shapes=[
            pltpu.VMEM((2,) + block, parts.dtype),
            pltpu.VMEM(block, parts.dtype),
            pltpu.VMEM(block, parts.dtype),
            dma((2, 3)),
        ],
        compiler_params=pltpu.CompilerParams(
            collective_id=ident, has_side_effects=True, vmem_limit_bytes=32 * 2**20
        ),
    )(parts)


def combine(slots, weights, half, centred):
    count = slots.shape[0]
    if not centred:
        total = slots[0]
        for at in range(1, count):
            total = total + slots[at]
        return total
    size = weights[0]
    mean = slots[0, :half] * weights[0]
    for at in range(1, count):
        size = size + weights[at]
        mean = mean + slots[at, :half] * weights[at]
    mean = mean / size
    spread = None
    for at in range(count):
        gap = slots[at, :half] - mean
        term = slots[at, half : 2 * half] + weights[at] * gap * gap
        spread = term if spread is None else spread + term
    rest = [jnp.zeros((slots.shape[1] - 2 * half, LANES), F32)] * (slots.shape[1] > 2 * half)
    return jnp.concatenate([mean, spread] + rest, 0)


def sums_kernel(images, half, centred, tiled, own, tile_sizes, sizes, total, *scratch):
    blk, batch = lax.axis_index("blk"), lax.axis_index("batch")
    slots, sems = scratch[0], scratch[1]
    peers = [(blk, batch ^ mask) for mask in range(1, images)]
    mates = [(blk ^ mask, batch) for mask in range(1, 4)] if tiled else []
    greet(peers + mates)
    if tiled:
        tile_slots, tile_sems = scratch[2], scratch[3]
        tile_slots[blk] = own[...]
        copies = [
            send(own, tile_slots.at[blk], tile_sems.at[0, at], tile_sems.at[1, at], peer)
            for at, peer in enumerate(mates)
        ]
        for copy in copies:
            copy.wait()
        slots[batch] = combine(tile_slots, tile_sizes, half, centred)
    else:
        slots[batch] = own[...]
    copies = [
        send(slots.at[batch], slots.at[batch], sems.at[0, at], sems.at[1, at], peer)
        for at, peer in enumerate(peers)
    ]
    for copy in copies:
        copy.wait()
    total[...] = combine(slots, sizes, half, centred)


def all_sums(first, second, tile_sizes, sizes, centred, tiled, ident):
    images = sizes.shape[0]
    channels = first.shape[0]
    half = channels // LANES
    rows = -(-2 * half // 8) * 8
    own = jnp.concatenate(
        [first, second, jnp.zeros(((rows - 2 * half) * LANES,), F32)]
    ).reshape(rows, LANES)
    dma = pltpu.SemaphoreType.DMA
    vmem = pl.BlockSpec(memory_space=pltpu.VMEM)
    scratch = [pltpu.VMEM((images, rows, LANES), F32), dma((2, images))]
    if tiled:
        scratch += [pltpu.VMEM((4, rows, LANES), F32), dma((2, 3))]
    total = pl.pallas_call(
        functools.partial(sums_kernel, images, half, centred, tiled),
        out_shape=jax.ShapeDtypeStruct((rows, LANES), F32),
        in_specs=[vmem] * 3,
        out_specs=vmem,
        scratch_shapes=scratch,
        compiler_params=pltpu.CompilerParams(collective_id=ident, has_side_effects=True),
    )(own, tile_sizes, sizes)
    flat = total.reshape(-1)
    return flat[:channels], flat[channels : 2 * channels]


def silu_slope(values):
    sigmoid_value = jax.nn.sigmoid(values)
    return sigmoid_value * (1.0 + values * (1.0 - sigmoid_value))


def windows(cells, rows, cols, back):
    channels = cells.shape[1]
    padded = jnp.pad(cells.reshape(rows, cols, channels), ((1, 1), (1, 1), (0, 0)))
    taken = []
    for offset in range(9):
        row, col = offset // 3, offset % 3
        if back:
            row, col = 2 - row, 2 - col
        taken.append(padded[row : row + rows, col : col + cols].reshape(rows * cols, channels))
    return jnp.concatenate(taken, 1)


def dot(left, right):
    return jnp.dot(left, right, preferred_element_type=F32)


def dot_t(left, right):
    return jnp.einsum("pd,cd->pc", left, right, preferred_element_type=F32)


def t_dot(left, right):
    return jnp.einsum("pc,pd->cd", left, right, preferred_element_type=F32)


def on_device(
    nt,
    nb,
    features,
    crop_rows,
    crop_cols,
    depth_target,
    labels,
    first_weight,
    spatial_weight,
    last_weight,
    shared_weight,
    head_weights,
    message_weights,
    gate_weights,
    depth_weight,
    class_weight,
    mid_gain,
    mid_bias,
    out_gain,
    out_bias,
):
    tile_rows, cols, width = features.shape[1:]
    tile = tile_rows * cols
    rows = tile_rows * nt
    pixels = rows * cols
    tasks = head_weights.shape[0]
    mid = first_weight.shape[1]
    share = mid // nb
    slim = mid // nt
    piece = width // (nb * nt)
    wide = nb * piece
    classes = class_weight.shape[1]
    blk, batch = lax.axis_index("blk"), lax.axis_index("batch")

    image_rows = lax.dynamic_index_in_dim(crop_rows, batch, 0, False)
    image_cols = lax.dynamic_index_in_dim(crop_cols, batch, 0, False)
    row_ids = jnp.arange(rows, dtype=jnp.int32)
    col_ids = jnp.arange(cols, dtype=jnp.int32)
    inside_grid = (row_ids[:, None] < image_rows) & (col_ids[None, :] < image_cols)
    inside = inside_grid.astype(F32).reshape(pixels, 1)
    inside_tile = lax.dynamic_slice_in_dim(inside, blk * tile, tile, 0)
    sizes_flat = (crop_rows * crop_cols).astype(F32)
    valid_count = jnp.sum(sizes_flat)
    sizes = jnp.broadcast_to(sizes_flat[:, None, None], (nb, 1, LANES))
    tile_counts = jnp.sum(inside.reshape(nt, tile), 1)
    tile_sizes = jnp.broadcast_to(tile_counts[:, None, None], (nt, 1, LANES))
    image_size = jnp.maximum(jnp.sum(inside), 1.0)
    tile_size = jnp.maximum(jnp.sum(inside_tile), 1.0)

    params = jnp.concatenate(
        [
            mid_gain.reshape(-1),
            mid_bias.reshape(-1),
            out_gain,
            out_bias,
            depth_weight,
            class_weight.reshape(-1),
        ]
    )
    room = -(-params.shape[0] // (16 * LANES)) * 16 * LANES
    small = jnp.pad(params, (0, room - params.shape[0])).reshape(-1, LANES)
    full_first, smalls = gather_first(first_weight, small, nb)
    full_first = full_first.reshape(width, mid)
    smalls = smalls.reshape(nb, room)
    at = 0

    def taken(count):
        nonlocal at
        found = smalls[:, at : at + count]
        at += count
        return found

    norms = mid_gain.shape[0]
    gain_mid = taken(norms * share).reshape(nb, norms, share).swapaxes(0, 1)
    gain_mid = gain_mid.reshape(norms, mid).astype(F32)
    bias_mid = taken(norms * share).reshape(nb, norms, share).swapaxes(0, 1)
    bias_mid = bias_mid.reshape(norms, mid).astype(F32)
    gain_out = lax.dynamic_index_in_dim(taken(nt * piece).reshape(nb, nt, piece), blk, 1, False)
    gain_out = gain_out.reshape(wide).astype(F32)
    bias_out = lax.dynamic_index_in_dim(taken(nt * piece).reshape(nb, nt, piece), blk, 1, False)
    bias_out = bias_out.reshape(wide).astype(F32)
    full_depth = taken(share).reshape(mid, 1)
    full_classes = taken(share * classes).reshape(mid, classes)
    stream_weight = jnp.concatenate([full_depth, full_classes], 1)

    spatial = lax.all_gather(
        lax.dynamic_slice_in_dim(spatial_weight, blk * slim, slim, 2), "batch", axis=1, tiled=True
    )
    last = lax.dynamic_index_in_dim(last_weight.reshape(share, nb, nt, piece), blk, 2, False)
    last = lax.all_gather(last.reshape(share, wide), "batch", axis=0, tiled=True)
    shared = lax.dynamic_slice_in_dim(shared_weight, blk * piece, piece, 0)
    shared = lax.all_gather(shared, "batch", axis=0, tiled=True)
    head = lax.all_gather(
        lax.dynamic_index_in_dim(head_weights, blk, 0, False), "batch", axis=1, tiled=True
    )
    message = lax.all_gather(
        lax.dynamic_index_in_dim(message_weights, blk, 0, False), "batch", axis=1, tiled=True
    )
    gate = lax.all_gather(
        lax.dynamic_index_in_dim(gate_weights, blk, 0, False), "batch", axis=0, tiled=True
    )

    flat_features = features.reshape(tile, width)
    cut = flat_features.reshape(tile, nb, nt, piece).transpose(2, 0, 1, 3).reshape(nt, tile, wide)
    wide_features = swap_tiles(cut, blk, nt)

    def slim_of(vector):
        return lax.dynamic_slice_in_dim(vector, blk * slim, slim, 0)

    def normalize(values, mask, local_size, gain, bias, tiled, ident):
        mean = jnp.sum(values * mask, 0) / local_size
        gap = values - mean
        spread = jnp.sum(gap * gap * mask, 0)
        centre, total = all_sums(mean, spread, tile_sizes, sizes, True, tiled, ident)
        inverse = lax.rsqrt(total / valid_count + EPSILON)
        normed = (values - centre) * inverse
        return normed * gain + bias, normed, inverse

    def normalize_back(grad, normed, inverse, gain, mask, tiled, ident):
        bias_sum, gain_sum = all_sums(
            jnp.sum(grad, 0), jnp.sum(grad * normed, 0), tile_sizes, sizes, False, tiled, ident
        )
        back = (
            inverse * gain * (grad - bias_sum / valid_count - normed * gain_sum / valid_count) * mask
        )
        return back.astype(BF16), gain_sum, bias_sum

    def act(values, mask):
        return (jax.nn.silu(values) * mask).astype(BF16)

    def by_rows(blocks):
        return blocks.reshape(pixels, blocks.shape[2])

    def by_channels(blocks):
        return blocks.swapaxes(0, 1).reshape(pixels, nt * blocks.shape[2])

    def cut_channels(values):
        return values.astype(BF16).reshape(pixels, nt, slim).swapaxes(0, 1)

    pre_one = dot(flat_features, full_first)
    norm_one, normed_one, inverse_one = normalize(
        pre_one, inside_tile, tile_size, gain_mid[0], bias_mid[0], True, 1
    )
    act_one = by_rows(gather_tiles(act(norm_one, inside_tile), 2))
    pre_two = dot(windows(act_one, rows, cols, False), spatial.reshape(9 * mid, slim))
    gain_two, bias_two = slim_of(gain_mid[1]), slim_of(bias_mid[1])
    norm_two, normed_two, inverse_two = normalize(
        pre_two, inside, image_size, gain_two, bias_two, False, 3
    )
    act_two = by_channels(gather_tiles(act(norm_two, inside), 4))
    pre_three = dot(act_two, last)
    norm_three, normed_three, inverse_three = normalize(
        pre_three, inside, image_size, gain_out, bias_out, False, 5
    )
    joined = norm_three + wide_features.astype(F32)
    act_three = act(joined, inside)
    pre_four = sum_tiles(cut_channels(dot(act_three, shared)), 6)
    gain_four, bias_four = slim_of(gain_mid[2]), slim_of(bias_mid[2])
    norm_four, normed_four, inverse_four = normalize(
        pre_four, inside, image_size, gain_four, bias_four, False, 3
    )
    shared_act = by_channels(gather_tiles(act(norm_four, inside), 4))

    gain_task = lax.dynamic_index_in_dim(gain_mid, 3 + blk, 0, False)
    bias_task = lax.dynamic_index_in_dim(bias_mid, 3 + blk, 0, False)
    pre_five = dot(windows(shared_act, rows, cols, False), head.reshape(9 * mid, mid))
    norm_five, normed_five, inverse_five = normalize(
        pre_five, inside, image_size, gain_task, bias_task, False, 5
    )
    task_act = act(norm_five, inside)
    messages = dot(windows(task_act, rows, cols, False), message.reshape(9 * mid, mid))
    gate_open = jax.nn.sigmoid(dot(task_act, gate))
    gated = (gate_open * messages).astype(BF16)
    is_first, is_last = blk == 0, blk == tasks - 1
    depth_part = jnp.where(is_first, task_act, gated)
    sem_part = jnp.where(is_last, task_act, gated)
    depth_share = jnp.einsum("pc,co->op", depth_part, full_depth, preferred_element_type=F32)
    class_share = jnp.einsum("pc,co->op", sem_part, full_classes, preferred_element_type=F32)
    lift = -(-(1 + classes) // 8) * 8 - 1 - classes
    shares = jnp.concatenate([depth_share, class_share, jnp.zeros((lift, pixels), F32)], 0)
    streams = jnp.sum(gather_tiles(shares, 7), 0).T
    depth_out = lax.dynamic_slice_in_dim(streams, blk * tile, tile, 0)[:, 0]
    logits = lax.dynamic_slice_in_dim(streams, blk * tile, tile, 0)[:, 1 : 1 + classes]
    targets = by_rows(gather_tiles_pair(depth_target, labels, tile))
    all_depth, all_logits = streams[:, :1], streams[:, 1 : 1 + classes]
    depth_slope = ((all_depth - targets[:, :1]) * inside).astype(BF16)
    onehot = (targets[:, 1:2] == jnp.arange(classes, dtype=jnp.int32)[None, :].astype(F32)).astype(F32)
    logit_slope = ((jax.nn.softmax(all_logits, axis=1) - onehot) * inside).astype(BF16)
    grad_depth = t_dot(depth_part, depth_slope)
    grad_classes = t_dot(sem_part, logit_slope)
    depth_back = depth_slope.astype(F32) * full_depth.astype(F32).reshape(1, mid)
    sem_back = dot_t(logit_slope, full_classes)
    zero = jnp.zeros((), F32)
    grad_gated = jnp.where(is_first, zero, depth_back) + jnp.where(is_last, zero, sem_back)
    grad_direct = jnp.where(is_first, depth_back, zero) + jnp.where(is_last, sem_back, zero)

    grad_msg = (grad_gated * gate_open).astype(BF16)
    grad_gate = (grad_gated * messages * gate_open * (1.0 - gate_open)).astype(BF16)
    msg_windows = windows(grad_msg, rows, cols, True)
    gate_grads = t_dot(task_act, grad_gate).astype(BF16)
    message_grads = t_dot(task_act, msg_windows).astype(BF16)
    share_messages = lax.psum_scatter(message_grads, "batch", scatter_dimension=0, tiled=True)
    task_grad = (
        grad_direct
        + dot_t(grad_gate, gate)
        + dot(msg_windows, message.swapaxes(1, 2).reshape(9 * mid, mid))
    )
    grad_norm_five = task_grad * inside * silu_slope(norm_five)
    grad_pre_five, gain_sum_five, bias_sum_five = normalize_back(
        grad_norm_five, normed_five, inverse_five, gain_task, inside, False, 8
    )
    five_windows = windows(grad_pre_five, rows, cols, True)
    head_grads = t_dot(shared_act, five_windows).astype(BF16)
    share_heads = lax.psum_scatter(head_grads, "batch", scatter_dimension=0, tiled=True)
    shared_back = dot(five_windows, head.swapaxes(1, 2).reshape(9 * mid, mid))
    shared_back = sum_tiles(cut_channels(shared_back), 6)

    grad_norm_four = shared_back * inside * silu_slope(norm_four)
    grad_pre_four, gain_sum_four, bias_sum_four = normalize_back(
        grad_norm_four, normed_four, inverse_four, gain_four, inside, False, 9
    )
    grad_four = by_channels(gather_tiles(grad_pre_four, 4))
    shared_grads = t_dot(act_three, grad_four).astype(BF16)
    grad_joined = dot_t(grad_four, shared) * inside * silu_slope(joined)
    grad_three, gain_sum_three, bias_sum_three = normalize_back(
        grad_joined, normed_three, inverse_three, gain_out, inside, False, 8
    )
    last_grads = t_dot(act_two, grad_three).astype(BF16)
    two_back = sum_tiles(cut_channels(dot_t(grad_three, last)), 6)
    grad_norm_two = two_back * inside * silu_slope(norm_two)
    grad_two, gain_sum_two, bias_sum_two = normalize_back(
        grad_norm_two, normed_two, inverse_two, gain_two, inside, False, 9
    )
    two_windows = windows(grad_two, rows, cols, True)
    spatial_grads = t_dot(act_one, two_windows).astype(BF16)
    one_back = dot(two_windows, spatial.swapaxes(1, 2).reshape(9 * slim, mid))
    one_back = sum_tiles(one_back.astype(BF16).reshape(nt, tile, mid), 10)
    grad_norm_one = one_back * inside_tile * silu_slope(norm_one)
    grad_one, gain_sum_one, bias_sum_one = normalize_back(
        grad_norm_one, normed_one, inverse_one, gain_mid[0], inside_tile, True, 11
    )
    all_one = by_rows(gather_tiles(grad_one, 2))
    first_grads = t_dot(wide_features, all_one).astype(BF16)
    joined_tiles = swap_tiles(grad_joined.astype(BF16).reshape(nt, tile, wide), blk, nt)
    joined_tiles = joined_tiles.reshape(nt, tile, nb, piece).transpose(1, 2, 0, 3).reshape(tile, width)
    grad_input = dot_t(grad_one, full_first) + joined_tiles.astype(F32)

    stream_grads = jnp.concatenate([grad_depth, grad_classes], 1)
    stream_grads = jnp.pad(stream_grads, ((0, 0), (0, LANES - 1 - classes))).astype(BF16)
    late = jnp.concatenate(
        [spatial_grads, shared_grads.reshape(nb, piece, mid).reshape(mid, -1),
         last_grads, first_grads.reshape(mid, -1), gate_grads, stream_grads],
        1,
    )
    late_share = lax.psum_scatter(late, "batch", scatter_dimension=0, tiled=True)
    early_share = jnp.concatenate([share_messages, share_heads], 1)
    early = lax.all_gather(early_share, "blk", axis=0, tiled=False).astype(F32)
    late_all = gather_tiles(late_share, 12).astype(F32)
    early = early.reshape(nt, share, 2, 9, mid).transpose(2, 0, 3, 1, 4)
    red_messages, red_heads = early[0], early[1]
    at = 0

    def part(count):
        nonlocal at
        found = late_all[:, :, at : at + count]
        at += count
        return found

    red_spatial = part(9 * slim).reshape(nt, share, 9, slim).transpose(2, 1, 0, 3).reshape(9, share, mid)
    red_shared = part(wide * mid // mid).reshape(nt * piece, mid)
    red_last = part(wide).reshape(nt, share, nb, piece).transpose(1, 2, 0, 3).reshape(share, width)
    red_first = part(wide * mid // mid).reshape(nt * piece, mid)
    red_gates = part(mid)
    streams_red = jnp.sum(part(LANES), 0)
    red_depth = streams_red[:, 0]
    red_classes = streams_red[:, 1 : 1 + classes]

    sums = jnp.concatenate(
        [
            gain_sum_five,
            bias_sum_five,
            gain_sum_three,
            bias_sum_three,
            gain_sum_two,
            bias_sum_two,
            gain_sum_four,
            bias_sum_four,
        ]
    ).reshape(-1, LANES)
    sums = jnp.pad(sums, ((0, -sums.shape[0] % 8), (0, 0)))
    sums = gather_tiles(sums, 13).reshape(nt, -1)
    five_gain, five_bias = sums[:, :mid], sums[:, mid : 2 * mid]
    at_out = 2 * mid
    three_gain = sums[:, at_out : at_out + wide].reshape(nt, nb, piece)
    three_bias = sums[:, at_out + wide : at_out + 2 * wide].reshape(nt, nb, piece)
    at_slim = at_out + 2 * wide
    slims = [
        sums[:, at_slim + i * slim : at_slim + (i + 1) * slim].reshape(1, mid) for i in range(4)
    ]
    mid_gains = jnp.concatenate([gain_sum_one[None], slims[0], slims[2], five_gain], 0)
    mid_biases = jnp.concatenate([bias_sum_one[None], slims[1], slims[3], five_bias], 0)
    grad_mid_gain = lax.dynamic_slice_in_dim(mid_gains, batch * share, share, 1)
    grad_mid_bias = lax.dynamic_slice_in_dim(mid_biases, batch * share, share, 1)
    grad_out_gain = lax.dynamic_index_in_dim(three_gain, batch, 1, False).reshape(nt * piece)
    grad_out_bias = lax.dynamic_index_in_dim(three_bias, batch, 1, False).reshape(nt * piece)
    return (
        depth_out.reshape(1, tile_rows, cols),
        logits.reshape(1, tile_rows, cols, classes),
        grad_input.reshape(1, tile_rows, cols, width),
        red_first,
        red_spatial,
        red_last,
        red_shared,
        red_heads,
        red_messages,
        red_gates,
        red_depth,
        red_classes,
        grad_mid_gain,
        grad_mid_bias,
        grad_out_gain,
        grad_out_bias,
    )


def swap_tiles(blocks, blk, nt):
    out = jnp.zeros_like(blocks)
    out = lax.dynamic_update_index_in_dim(
        out, lax.dynamic_index_in_dim(blocks, blk, 0, False), blk, 0
    )
    for mask in range(1, nt):
        sent = lax.dynamic_index_in_dim(blocks, blk ^ mask, 0, False)
        came = lax.ppermute(sent, "blk", [(i, i ^ mask) for i in range(nt)])
        out = lax.dynamic_update_index_in_dim(out, came, blk ^ mask, 0)
    return out.reshape(-1, blocks.shape[2])


def gather_tiles_pair(depth_target, labels, tile):
    pair = jnp.stack([depth_target.reshape(tile), labels.reshape(tile).astype(F32)], 0)
    pair = jnp.pad(pair, ((0, 6), (0, 0)))
    return gather_tiles(pair, 14).swapaxes(1, 2)


def solution(mesh):
    nt, nb = mesh.shape["blk"], mesh.shape["batch"]
    placed = (
        P("batch", "blk", None, None),
        P(),
        P(),
        P("batch", "blk", None),
        P("batch", "blk", None),
        P("batch", None),
        P(None, "batch", None),
        P("batch", None),
        P("batch", None),
        P(None, None, "batch", None),
        P(None, None, "batch", None),
        P(None, "batch", None),
        P("batch"),
        P("batch", None),
        P(None, "batch"),
        P(None, "batch"),
        P("batch"),
        P("batch"),
    )
    return jax.shard_map(
        functools.partial(on_device, nt, nb),
        mesh=mesh,
        in_specs=placed,
        out_specs=(
            P("batch", "blk", None),
            P("batch", "blk", None, None),
            P("batch", "blk", None, None),
            P("batch", None),
            P(None, "batch", None),
            P("batch", None),
            P("batch", None),
            P(None, None, "batch", None),
            P(None, None, "batch", None),
            P(None, "batch", None),
            P("batch"),
            P("batch", None),
            P(None, "batch"),
            P(None, "batch"),
            P("batch"),
            P("batch"),
        ),
        check_vma=False,
    )
```

time: 3170 us -> 866 us (0.27)
  waiting for transfers between devices: 1790 us -> 43.8 us
  blocking collectives: 954 us -> 105 us
  Pallas kernels: 0 us -> 265 us
  local copies, waits for them, and re-layouts: 42.7 us -> 234 us
  matrix products: 203 us -> 121 us
  other arithmetic: 121 us -> 66.5 us
    reduce_scatter x7 -> x3, waiting for transfers between devices: 1440 us -> 35.2 us  [the longest x1 35.1 us: on_device(): lax.psum_scatter(late, 'batch', scatter_dimension=0, tiled=True)]
    psum x16 -> x0, blocking collectives: 787 us -> none  [the longest x5 313 us: normalize(): lax.psum(jnp.sum(shifted * shifted * inside, 0), ('blk', 'batch'))]
    pallas_call x0 -> x24, Pallas kernels: none -> 265 us  [the longest x9 103 us: gather_tiles(): pl.pallas_call(tiles_kernel, out_shape=jax.ShapeDtypeStruct((4,) + block....]
    all_gather x7 -> x4, waiting for transfers between devices: 201 us -> 8.44 us  [the longest x1 8.44 us: on_device(): early = lax.all_gather(early_share, 'blk', axis=0, tiled=False).astype(F32)]
    psum x1 -> x0, waiting for transfers between devices: 107 us -> none  [on_device(): lax.psum(share_first.astype(jnp.bfloat16), 'blk').astype(jnp.float32)]
    dot_general x268 -> x26, matrix products: 202 us -> 121 us  [the longest x10 62.3 us: dot(): return jnp.dot(left, right, preferred_element_type=F32)]
    transpose x0 -> x12, local copies, waits for them, and re-layouts: none -> 47.5 us  [the longest x4 13.5 us: by_channels(): return blocks.swapaxes(0, 1).reshape(pixels, nt * blocks.shape[2])]
    unnamed x2 -> x0, blocking collectives: 46.6 us -> none
  transfers between devices with their start and end apart: 28 -> 13, of which waited for: 8 -> 2; matrix products, arithmetic and copies ran while one was open for 10% -> 36% of each run, Pallas kernels for 0% -> 30%
where the time goes in v1:
time: 866 us; the launch traced here: 858 us
  Pallas kernels  265 us (31%)
  local copies, waits for them, and re-layouts  234 us (27%)
  matrix products  121 us (14%)
  blocking collectives  105 us (12%)
  other arithmetic  66.5 us (8%)
  waiting for transfers between devices  43.8 us (5%)
  between operations  17.6 us (2%)
    pallas_call x9, Pallas kernels, gather_tiles(): pl.pallas_call(tiles_kernel, out_shape=jax.ShapeDtypeStruct((4,) + block....  103 us
    pallas_call x10, Pallas kernels, all_sums(): pl.pallas_call(functools.partial(sums_kernel, images, half, centred, tile...  88.3 us
    unnamed x270, local copies, waits for them, and re-layouts  66.9 us
    dot_general x10, matrix products, dot(): return jnp.dot(left, right, preferred_element_type=F32)  62.3 us
    pallas_call x4, Pallas kernels, sum_tiles(): pl.pallas_call(sum_kernel, out_shape=jax.ShapeDtypeStruct(block, F32), in...  44.2 us
    all_gather x1, blocking collectives, on_device(): lax.all_gather(lax.dynamic_index_in_dim(gate_weights, blk, 0, False), 'ba...  37.3 us
    reduce_scatter x1, waiting for transfers between devices, on_device(): lax.psum_scatter(late, 'batch', scatter_dimension=0, tiled=True)  35.1 us
    all_gather x1, blocking collectives, on_device(): lax.all_gather(last.reshape(share, wide), 'batch', axis=0, tiled=True)  35 us
  transfers between devices with their start and end apart: 13, of which 2 were waited for; matrix products, arithmetic and copies ran while one was open for 36% of the time, Pallas kernels for 30%

profile of v1, /device:TPU:0, one launch (start us, length us, event | category | flops | bytes accessed | tf_op | source)
XLA Modules:
  0.0 858.3 jit_solution(7646311237235503921)
XLA Ops:
  10.0 5.9 reshape_reshape.12
  15.9 4.9 copy.260
  34.5 29.1 %shard_map.297 = (bf16[8,256,512]{2,1,0:T(8,128)(2,1)}, bf16[8,32,128]{2,1,0:T(8,128)(2,1)}) custom-call(bf16[256,512]{1,0:T(8,128)(2,1)} %weight.1, bf16[32,128]{1,0:T(8,128)(2,1)} %pad_bitcast_fusion.small), custom_call_target="tpu_custom_call" | custom-call | tf_op jit(solution)/shard_map/pallas_call | solution.py:95
  66.5 2.9 multiply_reduce_fusion.13
  71.2 5.3 shard_map.308
  78.3 37.3 %all-gather.1 = bf16[1,512,512]{2,1,0:T(8,128)(2,1)} all-gather(bf16[1,64,512]{2,1,0:T(8,128)(2,1)S(1)} %constant_dynamic-slice_fusion.3), channel_id=3, replica_groups=mesh['blk'=4,'batch'=8] {'batch'}, dimensions={1}, use_global_device_ids=true | all-gather | bytes 589824 | tf_op jit(solution)/shard_map/all_gather | solution.py:385
  116.5 33.0 %all_gather.26 = bf16[512,512]{1,0:T(8,128)(2,1)S(1)} all-gather(bf16[64,512]{1,0:T(8,128)(2,1)S(1)} %constant_dynamic-slice_fusion.9), channel_id=1, replica_groups=mesh['blk'=4,'batch'=8] {'batch'}, dimensions={0}, use_global_device_ids=true | all-gather | bytes 589824 | tf_op jit(solution)/shard_map/all_gather | solution.py:378
  154.9 11.2 %shard_map.298 = f32[8,128]{1,0:T(8,128)} custom-call(f32[8,128]{1,0:T(8,128)} %pad_maximum_fusion.6.own, f32[4,1,128]{2,1,0:T(1,128)} %broadcast_in_dim.35.tile_sizes, f32[8,1,128]{2,1,0:T(1,128)} %broadcast_in_dim.36.sizes), custom_call_target="tpu_custom_call" | custom-call | tf_op jit(solution)/shard_map/pallas_call | solution.py:245
  168.5 11.6 %shard_map.299 = bf16[4,320,512]{2,1,0:T(8,128)(2,1)} custom-call(bf16[320,512]{1,0:T(8,128)(2,1)} %multiply_convert_fusion.11.block), custom_call_target="tpu_custom_call" | custom-call | tf_op jit(solution)/shard_map/pallas_call | solution.py:134
  180.3 9.0 %pad_slice_fusion.32 = (bf16[32,40,512]{2,1,0:T(8,128)(2,1)}, bf16[32,40,512]{2,1,0:T(8,128)(2,1)S(1)}, bf16[32,40,512]{2,1,0:T(8,128)(2,1)}, bf16[32,40,512]{2,...) fusion(bf16[32,40,512]{2,1,0:T(8,128)(2,1)} %bitcast.338), kind=kLoop, calls=%fused_computation.76 | loop fusion | bytes 11796480 | tf_op jit(solution)/shard_map/slice | solution.py:270
  202.8 35.0 %all_gather.25 = bf16[512,512]{1,0:T(8,128)(2,1)} all-gather(bf16[64,512]{1,0:T(8,128)(2,1)S(1)} %reshape.715), channel_id=1, replica_groups=mesh['blk'=4,'batch'=8] {'batch'}, dimensions={0}, use_global_device_ids=true | all-gather | bytes 589824 | tf_op jit(solution)/shard_map/all_gather | solution.py:376
  242.9 6.5 multiply_reduce_fusion.11
  250.3 8.0 shard_map.300
  261.2 12.5 %shard_map.301 = bf16[4,1280,128]{2,1,0:T(8,128)(2,1)} custom-call(bf16[1280,128]{1,0:T(8,128)(2,1)} %multiply_convert_fusion.10.block), custom_call_target="tpu_custom_call" | custom-call | tf_op jit(solution)/shard_map/pallas_call | solution.py:134
  280.2 8.0 shard_map.302
  297.7 10.2 %shard_map.303 = f32[1280,128]{1,0:T(8,128)S(1)} custom-call(bf16[4,1280,128]{2,1,0:T(8,128)(2,1)S(1)} %bitcast.327), custom_call_target="tpu_custom_call" | custom-call | tf_op jit(solution)/shard_map/pallas_call | solution.py:166
  309.1 8.0 shard_map.304
  320.0 13.2 %shard_map.305 = bf16[4,1280,128]{2,1,0:T(8,128)(2,1)} custom-call(bf16[1280,128]{1,0:T(8,128)(2,1)} %multiply_convert_fusion.9.block), custom_call_target="tpu_custom_call" | custom-call | tf_op jit(solution)/shard_map/pallas_call | solution.py:134
  335.8 6.9 copy.266
  345.3 6.4 pad_slice_fusion.24
  364.0 4.3 copy-done.49
  384.7 10.6 %multiply_reduce_fusion.3 = (f32[512]{0:T(512)S(1)}, f32[1280,512]{1,0:T(8,128)S(1)}) fusion(f32[1280]{0:T(1024)S(1)} %reshape.799, bf16[1280,4608]{0,1:T(8,128)(2,1)} %constant_dynamic-update-slice_fusion.9, bf16[4608,512]{1,0:T(8,128)(2,1)} %bitcast.390), kind=kOutput, calls=%fused_computation.38 | convolution fusion | flops 6041107968 | bytes 19143680 | tf_op jit(solution)/shard_map/dot_general | solution.py:275
  397.8 8.0 shard_map.306
  410.0 4.5 pad_slice_fusion.16
  426.2 10.5 %fusion.69 = f32[1280,512]{1,0:T(8,128)S(1)} fusion(bf16[1280,4608]{1,0:T(8,128)(2,1)} %constant_dynamic-update-slice_fusion.18, bf16[4608,512]{1,0:T(8,128)(2,1)} %bitcast.392), kind=kOutput, calls=%fused_computation.358 | convolution fusion | flops 6039797760 | bytes 19136512 | tf_op jit(solution)/shard_map/dot_general | solution.py:275
  441.3 8.6 %shard_map.307 = f32[4,48,1280]{2,1,0:T(8,128)} custom-call(f32[48,1280]{1,0:T(8,128)} %maximum_maximum_fusion.block), custom_call_target="tpu_custom_call" | custom-call | tf_op jit(solution)/shard_map/pallas_call | solution.py:134
  452.1 6.6 copy.279
  458.7 6.6 copy.280
  467.2 5.6 multiply_convert_fusion.3
  472.8 4.2 pad_slice_fusion.8
  477.9 4.3 copy-done.50
  482.2 7.9 convolution_convert_fusion.1
  490.1 12.0 %fusion.70 = f32[1280,512]{1,0:T(8,128)} fusion(bf16[1280,4608]{1,0:T(8,128)(2,1)} %copy-done.50, bf16[4608,512]{1,0:T(8,128)(2,1)} %bitcast.397), kind=kOutput, calls=%fused_computation.359 | convolution fusion | flops 6039797760 | bytes 19136512 | tf_op jit(solution)/shard_map/dot_general | solution.py:275
  503.4 5.5 fusion.56
  509.4 8.7 %shard_map.309 = f32[8,128]{1,0:T(8,128)} custom-call(f32[8,128]{1,0:T(8,128)} %pad_maximum_fusion.9.own, f32[4,1,128]{2,1,0:T(1,128)} %broadcast_in_dim.35.tile_sizes, f32[8,1,128]{2,1,0:T(1,128)} %broadcast_in_dim.36.sizes), custom_call_target="tpu_custom_call" | custom-call | tf_op jit(solution)/shard_map/pallas_call | solution.py:245
  520.9 4.0 multiply_convert_fusion.1
  524.9 4.3 pad_slice_fusion
  530.0 5.2 copy-done.51
  535.3 10.6 %convolution_convert_fusion.6 = bf16[1280,512]{0,1:T(8,128)(2,1)} fusion(bf16[1280,4608]{1,0:T(8,128)(2,1)} %copy-done.51, bf16[4608,512]{1,0:T(8,128)(2,1)S(1)} %bitcast.396), kind=kOutput, calls=%fused_computation.21 | convolution fusion | flops 6040453120 | bytes 17825792 | tf_op jit(solution)/shard_map/dot_general | solution.py:275
  547.7 12.1 %shard_map.310 = f32[1280,128]{1,0:T(8,128)S(1)} custom-call(bf16[4,1280,128]{2,1,0:T(8,128)(2,1)S(1)} %bitcast.328), custom_call_target="tpu_custom_call" | custom-call | tf_op jit(solution)/shard_map/pallas_call | solution.py:166
  560.9 8.0 shard_map.311
  572.0 11.8 %shard_map.312 = bf16[4,1280,128]{2,1,0:T(8,128)(2,1)} custom-call(bf16[1280,128]{1,0:T(8,128)(2,1)} %multiply_convert_fusion.8.block), custom_call_target="tpu_custom_call" | custom-call | tf_op jit(solution)/shard_map/pallas_call | solution.py:134
  586.2 12.5 %convolution_convert_fusion = bf16[512,4608]{1,0:T(8,128)(2,1)} fusion(bf16[1280,512]{0,1:T(8,128)(2,1)S(1)} %bitcast.346, bf16[1280,4608]{1,0:T(8,128)(2,1)} %copy-done.51), kind=kOutput, calls=%fused_computation.2 | convolution fusion | flops 6042157056 | bytes 17825792 | tf_op jit(solution)/shard_map/pc,pd->cd/dot_general | solution.py:283
  600.1 5.1 fusion.55
  605.8 8.1 shard_map.313
  616.6 6.1 multiply_convert_fusion
  626.5 11.7 %shard_map.314 = f32[1280,128]{1,0:T(8,128)S(1)} custom-call(bf16[4,1280,128]{2,1,0:T(8,128)(2,1)S(1)} %bitcast.329), custom_call_target="tpu_custom_call" | custom-call | tf_op jit(solution)/shard_map/pallas_call | solution.py:166
  639.3 8.6 %shard_map.315 = f32[8,128]{1,0:T(8,128)} custom-call(f32[8,128]{1,0:T(8,128)} %fusion.34.own, f32[4,1,128]{2,1,0:T(1,128)} %broadcast_in_dim.35.tile_sizes, f32[8,1,128]{2,1,0:T(1,128)} %broadcast_in_dim.36.sizes), custom_call_target="tpu_custom_call" | custom-call | tf_op jit(solution)/shard_map/pallas_call | solution.py:245
  653.9 10.0 %shard_map.316 = f32[320,512]{1,0:T(8,128)S(1)} custom-call(bf16[4,320,512]{2,1,0:T(8,128)(2,1)S(1)} %bitcast.330), custom_call_target="tpu_custom_call" | custom-call | tf_op jit(solution)/shard_map/pallas_call | solution.py:166
  665.8 11.6 %shard_map.317 = f32[8,128]{1,0:T(8,128)} custom-call(f32[8,128]{1,0:T(8,128)} %pad_maximum_fusion.11.own, f32[4,1,128]{2,1,0:T(1,128)} %broadcast_in_dim.35.tile_sizes, f32[8,1,128]{2,1,0:T(1,128)} %broadcast_in_dim.36.sizes), custom_call_target="tpu_custom_call" | custom-call | tf_op jit(solution)/shard_map/pallas_call | solution.py:245
  681.6 11.5 %shard_map.318 = bf16[4,320,512]{2,1,0:T(8,128)(2,1)} custom-call(bf16[320,512]{1,0:T(8,128)(2,1)} %fusion.21.block), custom_call_target="tpu_custom_call" | custom-call | tf_op jit(solution)/shard_map/pallas_call | solution.py:134
  693.1 4.9 fusion.7
  701.8 3.1 fusion.11
  718.2 13.4 %shard_map.320 = f32[4,24,128]{2,1,0:T(8,128)} custom-call(f32[24,128]{1,0:T(8,128)} %pad.46.block), custom_call_target="tpu_custom_call" | custom-call | tf_op jit(solution)/shard_map/pallas_call | solution.py:134
  737.0 3.9 copy.286
  740.9 3.5 copy.287
  744.3 4.9 convolution_add_fusion.1
  749.2 35.1 %reduce-scatter.4.cloned.1.call-done.block = bf16[64,3328]{1,0:T(8,128)(2,1)} async-done(((bf16[512,3328]{1,0:T(8,128)(2,1)}), bf16[64,3328]{1,0:T(8,128)(2,1)}) %reduce-scatter.4.cloned.1.call-update) | async-done | bytes 426000 | tf_op jit(solution)/shard_map/reduce_scatter | solution.py:541
  784.3 15.6 %shard_map.319 = bf16[4,64,3328]{2,1,0:T(8,128)(2,1)} custom-call(bf16[64,3328]{1,0:T(8,128)(2,1)} %reduce-scatter.4.cloned.1.call-done.block), custom_call_target="tpu_custom_call" | custom-call | tf_op jit(solution)/shard_map/pallas_call | solution.py:134
  815.0 8.4 all-gather.15.cloned.1.call-done
  823.4 10.6 %reshape.806 = f32[4,64,2,9,512]{4,3,2,1,0:T(8,128)} reshape(bf16[256,9216]{1,0:T(8,128)(2,1)} %all-gather.15.cloned.1.call-done) | data formatting | bytes 14155776 | tf_op jit(solution)/shard_map/transpose | solution.py:545
  834.0 7.2 slice_bitcast_fusion
  841.2 5.0 copy.297
  846.2 5.0 copy.296
  (507 shorter events, 206.1 us)
Async XLA Ops:
  7.2 235.7 %all-gather.9.cloned.1.call-start = ((), (), s32[]{:S(2)}) async-start(), calls=%async_computation.3 | async-start | bytes 1327104 | tf_op jit(solution)/shard_map/all_gather | solution.py:372
  9.0 375.7 %all-gather.11.cloned.1.call-start = ((), (), s32[]{:S(2)}) async-start(), calls=%async_computation.7 | async-start | bytes 5308416 | tf_op jit(solution)/shard_map/all_gather | solution.py:379
  10.0 416.2 %all-gather.13.cloned.1.call-start = ((), (), s32[]{:S(2)}) async-start(), calls=%async_computation.8 | async-start | bytes 5308416 | tf_op jit(solution)/shard_map/all_gather | solution.py:382
  21.0 7.2 copy-start.102
  21.0 9.7 %copy-start.101 = (s32[8]{0:T(128)S(1)}, s32[8]{0:T(128)}, u32[]{:S(2)}) copy-start(s32[8]{0:T(128)} %param.20) | copy-start | bytes 100
  21.1 12.3 %copy-start.91 = (bf16[7,64]{1,0:T(8,128)(2,1)S(1)}, bf16[7,64]{1,0:T(8,128)(2,1)}, u32[]{:S(2)}) copy-start(bf16[7,64]{1,0:T(8,128)(2,1)} %param.32) | copy-start | bytes 2692
  21.1 12.4 %copy-start.92 = (bf16[7,64]{1,0:T(8,128)(2,1)S(1)}, bf16[7,64]{1,0:T(8,128)(2,1)}, u32[]{:S(2)}) copy-start(bf16[7,64]{1,0:T(8,128)(2,1)} %param.33) | copy-start | bytes 2692
  21.1 12.4 %copy-start.71 = (bf16[64,40]{0,1:T(8,128)(2,1)S(1)}, bf16[64,40]{0,1:T(8,128)(2,1)}, u32[]{:S(2)}) copy-start(bf16[64,40]{0,1:T(8,128)(2,1)} %param.31) | copy-start | bytes 15364
  21.1 12.6 %copy-start.98 = (bf16[256]{0:T(256)(128)(2,1)S(1)}, bf16[256]{0:T(256)(128)(2,1)}, u32[]{:S(2)}) copy-start(bf16[256]{0:T(256)(128)(2,1)} %param.34) | copy-start | bytes 1540
  21.1 12.6 %copy-start.99 = (bf16[256]{0:T(256)(128)(2,1)S(1)}, bf16[256]{0:T(256)(128)(2,1)}, u32[]{:S(2)}) copy-start(bf16[256]{0:T(256)(128)(2,1)} %param.35) | copy-start | bytes 1540
  21.1 12.6 %copy-start.100 = (bf16[64]{0:T(256)(128)(2,1)S(1)}, bf16[64]{0:T(256)(128)(2,1)}, u32[]{:S(2)}) copy-start(bf16[64]{0:T(256)(128)(2,1)} %param.30) | copy-start | bytes 388
  22.0 215.7 %collective-permute-start = (bf16[320,512]{1,0:T(8,128)(2,1)}, bf16[320,512]{1,0:T(8,128)(2,1)}, u32[]{:S(2)}, u32[]{:S(2)}) collective-permute-start(bf16[320,512]{1,0:T(8,128)(2,1)} %bitcast.36), channel_id=1, source_target_pairs={{0,8},{8,0},{16,24},{24,16},{1,9},{9,1},{17,25},{25,17},{2,10},{10... | collective-permute-start | bytes 983048 | tf_op jit(solution)/shard_map/ppermute | solution.py:619
  23.4 216.1 %collective-permute-start.1 = (bf16[320,512]{1,0:T(8,128)(2,1)}, bf16[320,512]{1,0:T(8,128)(2,1)}, u32[]{:S(2)}, u32[]{:S(2)}) collective-permute-start(bf16[320,512]{1,0:T(8,128)(2,1)} %bitcast.38), channel_id=1, source_target_pairs={{0,16},{8,24},{16,0},{24,8},{1,17},{9,25},{17,1},{25,9},{2,18},{10... | collective-permute-start | bytes 983048 | tf_op jit(solution)/shard_map/ppermute | solution.py:619
  26.1 215.1 %collective-permute-start.2 = (bf16[320,512]{1,0:T(8,128)(2,1)S(1)}, bf16[320,512]{1,0:T(8,128)(2,1)}, u32[]{:S(2)}, u32[]{:S(2)}) collective-permute-start(bf16[320,512]{1,0:T(8,128)(2,1)S(1)} %bitcast.429), channel_id=1, source_target_pairs={{0,24},{8,16},{16,8},{24,0},{1,25},{9,17},{17,9},{25,1},{2,26},{10... | collective-permute-start | bytes 983048 | tf_op jit(solution)/shard_map/ppermute | solution.py:619
  28.2 679.1 %reduce-scatter.6.cloned.1.call-start = ((), (), s32[]{:S(2)}) async-start(), calls=%async_computation.5 | async-start | bytes 5308416 | tf_op jit(solution)/shard_map/reduce_scatter | solution.py:488
  65.8 101.7 %copy-start.53 = (f32[320]{0:T(512)}, f32[320]{0:T(512)S(1)}, u32[]{:S(2)}) copy-start(f32[320]{0:T(512)S(1)} %get-tuple-element.133) | copy-start | bytes 3844
  66.5 82.9 %copy-start.48 = (bf16[64,2048]{1,0:T(8,128)(2,1)S(1)}, bf16[64,2048]{1,0:T(8,128)(2,1)}, u32[]{:S(2)}) copy-start(bf16[64,2048]{1,0:T(8,128)(2,1)} %param.25) | copy-start | bytes 786436
  69.4 99.1 %copy-start.11 = (f32[512,320]{0,1:T(8,128)}, f32[512,320]{0,1:T(8,128)S(1)}, u32[]{:S(2)}) copy-start(f32[512,320]{0,1:T(8,128)S(1)} %get-tuple-element.251) | copy-start | bytes 1966084
  77.4 72.6 %copy-start.52 = (f32[1280,8]{0,1:T(8,128)}, f32[1280,8]{0,1:T(8,128)S(1)}, u32[]{:S(2)}) copy-start(f32[1280,8]{0,1:T(8,128)S(1)} %reshape.743) | copy-start | bytes 122884
  149.5 144.0 %copy-start.44 = (bf16[512,512]{1,0:T(8,128)(2,1)}, bf16[512,512]{1,0:T(8,128)(2,1)S(1)}, u32[]{:S(2)}) copy-start(bf16[512,512]{1,0:T(8,128)(2,1)S(1)} %all_gather.26) | copy-start | bytes 1572868
  152.2 37.1 %copy-start.64 = (f32[512]{0:T(512)}, f32[512]{0:T(512)S(1)}, u32[]{:S(2)}) copy-start(f32[512]{0:T(512)S(1)} %mul.548) | copy-start | bytes 6148
  152.5 166.5 %copy-start.93 = (f32[128]{0:T(128)}, f32[128]{0:T(128)S(1)}, u32[]{:S(2)}) copy-start(f32[128]{0:T(128)S(1)} %fusion.50) | copy-start | bytes 1540
  152.6 36.7 %copy-start.66 = (f32[512]{0:T(512)}, f32[512]{0:T(512)S(1)}, u32[]{:S(2)}) copy-start(f32[512]{0:T(512)S(1)} %add.260) | copy-start | bytes 6148
  167.5 21.7 %copy-start.58 = (f32[512]{0:T(512)}, f32[512]{0:T(512)S(1)}, u32[]{:S(2)}) copy-start(f32[512]{0:T(512)S(1)} %get-tuple-element.244) | copy-start | bytes 6148
  167.5 23.0 %copy-start.55 = (f32[4,128]{1,0:T(4,128)}, f32[4,128]{1,0:T(4,128)S(1)}, u32[]{:S(2)}) copy-start(f32[4,128]{1,0:T(4,128)S(1)} %get-tuple-element.245) | copy-start | bytes 6148
  190.6 228.7 %copy-start.68 = (f32[1,512]{1,0:T(1,128)}, f32[1,512]{1,0:T(1,128)S(1)}, u32[]{:S(2)}) copy-start(f32[1,512]{1,0:T(1,128)S(1)} %constant_dynamic-slice_fusion.4) | copy-start | bytes 6148
  237.7 22.5 %copy-start.95 = (f32[128]{0:T(128)}, f32[128]{0:T(128)S(1)}, u32[]{:S(2)}) copy-start(f32[128]{0:T(128)S(1)} %fusion.49) | copy-start | bytes 1540
  249.4 26.0 %copy-start.13 = (f32[1280,128]{1,0:T(8,128)}, f32[1280,128]{1,0:T(8,128)S(1)}, u32[]{:S(2)}) copy-start(f32[1280,128]{1,0:T(8,128)S(1)} %get-tuple-element.253) | copy-start | bytes 1966084
  260.2 15.2 %copy-start.75 = (f32[1,128]{1,0:T(1,128)}, f32[1,128]{1,0:T(1,128)S(1)}, u32[]{:S(2)}) copy-start(f32[1,128]{1,0:T(1,128)S(1)} %get-tuple-element.136) | copy-start | bytes 1540
  260.2 15.2 %copy-start.77 = (f32[128]{0:T(128)}, f32[128]{0:T(128)S(1)}, u32[]{:S(2)}) copy-start(f32[128]{0:T(128)S(1)} %get-tuple-element.243) | copy-start | bytes 1540
  260.2 15.2 %copy-start.83 = (f32[128]{0:T(128)}, f32[128]{0:T(128)S(1)}, u32[]{:S(2)}) copy-start(f32[128]{0:T(128)S(1)} %get-tuple-element.246) | copy-start | bytes 1540
  319.0 16.7 %copy-start.79 = (f32[1,128]{1,0:T(1,128)}, f32[1,128]{1,0:T(1,128)S(1)}, u32[]{:S(2)}) copy-start(f32[1,128]{1,0:T(1,128)S(1)} %get-tuple-element.141) | copy-start | bytes 1540
  319.0 16.7 %copy-start.81 = (f32[128]{0:T(128)}, f32[128]{0:T(128)S(1)}, u32[]{:S(2)}) copy-start(f32[128]{0:T(128)S(1)} %get-tuple-element.242) | copy-start | bytes 1540
  319.0 16.7 %copy-start.85 = (f32[128]{0:T(128)}, f32[128]{0:T(128)S(1)}, u32[]{:S(2)}) copy-start(f32[128]{0:T(128)S(1)} %get-tuple-element.247) | copy-start | bytes 1540
  409.9 67.9 %copy-start.6 = (bf16[1280,512]{1,0:T(8,128)(2,1)}, bf16[1280,512]{1,0:T(8,128)(2,1)S(1)}, u32[]{:S(2)}) copy-start(bf16[1280,512]{1,0:T(8,128)(2,1)S(1)} %multiply_convert_fusion.5) | copy-start | bytes 3932164
  426.2 10.5 %copy-start.47 = (bf16[1,512,512]{2,1,0:T(8,128)(2,1)S(1)}, bf16[1,512,512]{2,1,0:T(8,128)(2,1)}, u32[]{:S(2)}) copy-start(bf16[1,512,512]{2,1,0:T(8,128)(2,1)} %all-gather.1) | copy-start | bytes 1572868
  502.1 205.3 %reduce-scatter.8.cloned.1.call-start = ((), (), s32[]{:S(2)}) async-start(), calls=%async_computation.6 | async-start | bytes 5308416 | tf_op jit(solution)/shard_map/reduce_scatter | solution.py:500
  503.4 15.5 %copy-start.70 = (f32[2560]{0:T(1024)S(1)}, f32[2560]{0:T(1024)}, u32[]{:S(2)}) copy-start(f32[2560]{0:T(1024)} %custom-call) | copy-start | bytes 30724
  545.9 14.0 %copy-start.80 = (f32[1,128]{1,0:T(1,128)S(1)}, f32[1,128]{1,0:T(1,128)}, u32[]{:S(2)}) copy-start(f32[1,128]{1,0:T(1,128)} %copy-done.79) | copy-start | bytes 1540
  545.9 14.0 %copy-start.82 = (f32[128]{0:T(128)S(1)}, f32[128]{0:T(128)}, u32[]{:S(2)}) copy-start(f32[128]{0:T(128)} %copy-done.81) | copy-start | bytes 1540
  545.9 14.0 %copy-start.86 = (f32[128]{0:T(128)S(1)}, f32[128]{0:T(128)}, u32[]{:S(2)}) copy-start(f32[128]{0:T(128)} %copy-done.85) | copy-start | bytes 1540
  545.9 14.0 %copy-start.94 = (f32[128]{0:T(128)S(1)}, f32[128]{0:T(128)}, u32[]{:S(2)}) copy-start(f32[128]{0:T(128)} %copy-done.93) | copy-start | bytes 1540
  547.7 22.6 %copy-start.90 = (f32[128]{0:T(128)S(1)}, f32[128]{0:T(128)}, u32[]{:S(2)}) copy-start(f32[128]{0:T(128)} %get-tuple-element.140) | copy-start | bytes 1540
  570.3 15.9 %copy-start.16 = (bf16[1280,4,128]{0,2,1:T(8,128)(2,1)S(1)}, bf16[1280,4,128]{0,2,1:T(8,128)(2,1)}, u32[]{:S(2)}) copy-start(bf16[1280,4,128]{0,2,1:T(8,128)(2,1)} %copy.267) | copy-start | bytes 3932164
  598.7 185.6 %reduce-scatter.4.cloned.1.call-start = ((), (), s32[]{:S(2)}) async-start(), calls=%async_computation.4 | async-start | bytes 3833856 | tf_op jit(solution)/shard_map/reduce_scatter | solution.py:541
  600.1 16.5 %copy-start.73 = (f32[512]{0:T(512)S(1)}, f32[512]{0:T(512)}, u32[]{:S(2)}) copy-start(f32[512]{0:T(512)} %get-tuple-element.138) | copy-start | bytes 6148
  624.7 13.6 %copy-start.14 = (f32[1280,128]{1,0:T(8,128)S(1)}, f32[1280,128]{1,0:T(8,128)}, u32[]{:S(2)}) copy-start(f32[1280,128]{1,0:T(8,128)} %copy-done.13) | copy-start | bytes 1966084
  624.7 13.6 %copy-start.76 = (f32[1,128]{1,0:T(1,128)S(1)}, f32[1,128]{1,0:T(1,128)}, u32[]{:S(2)}) copy-start(f32[1,128]{1,0:T(1,128)} %copy-done.75) | copy-start | bytes 1540
  624.7 13.6 %copy-start.78 = (f32[128]{0:T(128)S(1)}, f32[128]{0:T(128)}, u32[]{:S(2)}) copy-start(f32[128]{0:T(128)} %copy-done.77) | copy-start | bytes 1540
  624.7 13.6 %copy-start.84 = (f32[128]{0:T(128)S(1)}, f32[128]{0:T(128)}, u32[]{:S(2)}) copy-start(f32[128]{0:T(128)} %copy-done.83) | copy-start | bytes 1540
  624.7 13.6 %copy-start.96 = (f32[128]{0:T(128)S(1)}, f32[128]{0:T(128)}, u32[]{:S(2)}) copy-start(f32[128]{0:T(128)} %copy-done.95) | copy-start | bytes 1540
  626.5 22.8 %copy-start.89 = (f32[128]{0:T(128)S(1)}, f32[128]{0:T(128)}, u32[]{:S(2)}) copy-start(f32[128]{0:T(128)} %get-tuple-element.135) | copy-start | bytes 1540
  652.0 12.0 %copy-start.12 = (f32[512,320]{0,1:T(8,128)S(1)}, f32[512,320]{0,1:T(8,128)}, u32[]{:S(2)}) copy-start(f32[512,320]{0,1:T(8,128)} %copy-done.11) | copy-start | bytes 1966084
  652.0 12.0 %copy-start.54 = (f32[320]{0:T(512)S(1)}, f32[320]{0:T(512)}, u32[]{:S(2)}) copy-start(f32[320]{0:T(512)} %copy-done.53) | copy-start | bytes 3844
  652.0 12.0 %copy-start.56 = (f32[4,128]{1,0:T(4,128)S(1)}, f32[4,128]{1,0:T(4,128)}, u32[]{:S(2)}) copy-start(f32[4,128]{1,0:T(4,128)} %copy-done.55) | copy-start | bytes 6148
  652.0 12.0 %copy-start.59 = (f32[512]{0:T(512)S(1)}, f32[512]{0:T(512)}, u32[]{:S(2)}) copy-start(f32[512]{0:T(512)} %copy-done.58) | copy-start | bytes 6148
  652.0 12.0 %copy-start.65 = (f32[512]{0:T(512)S(1)}, f32[512]{0:T(512)}, u32[]{:S(2)}) copy-start(f32[512]{0:T(512)} %copy-done.64) | copy-start | bytes 6148
  652.0 12.0 %copy-start.67 = (f32[512]{0:T(512)S(1)}, f32[512]{0:T(512)}, u32[]{:S(2)}) copy-start(f32[512]{0:T(512)} %copy-done.66) | copy-start | bytes 6148
  653.9 25.0 %copy-start.72 = (f32[1,512]{1,0:T(1,128)S(1)}, f32[1,512]{1,0:T(1,128)}, u32[]{:S(2)}) copy-start(f32[1,512]{1,0:T(1,128)} %mul.600) | copy-start | bytes 6148
  664.0 29.1 %copy-start.10 = (bf16[4,320,512]{2,1,0:T(8,128)(2,1)S(1)}, bf16[4,320,512]{2,1,0:T(8,128)(2,1)}, u32[]{:S(2)}) copy-start(bf16[4,320,512]{2,1,0:T(8,128)(2,1)} %shard_map.299) | copy-start | bytes 3932164
  707.3 116.1 %all-gather.15.cloned.1.call-start = ((), (), s32[]{:S(2)}) async-start(), calls=%async_computation.9 | async-start | bytes 5898240 | tf_op jit(solution)/shard_map/all_gather | solution.py:543
  712.9 21.8 %collective-permute-start.5 = (bf16[320,512]{1,0:T(8,128)(2,1)S(1)}, bf16[320,512]{1,0:T(8,128)(2,1)S(1)}, u32[]{:S(2)}, u32[]{:S(2)}) collective-permute-start(bf16[320,512]{1,0:T(8,128)(2,1)S(1)} %get-tuple-element.163), channel_id=1, source_target_pairs={{0,24},{8,16},{16,8},{24,0},{1,25},{9,17},{17,9},{25,1},{2,26},{10... | collective-permute-start | bytes 983048 | tf_op jit(solution)/shard_map/ppermute | solution.py:619
  713.8 20.8 %collective-permute-start.4 = (bf16[320,512]{1,0:T(8,128)(2,1)S(1)}, bf16[320,512]{1,0:T(8,128)(2,1)S(1)}, u32[]{:S(2)}, u32[]{:S(2)}) collective-permute-start(bf16[320,512]{1,0:T(8,128)(2,1)S(1)} %get-tuple-element.164), channel_id=1, source_target_pairs={{0,16},{8,24},{16,0},{24,8},{1,17},{9,25},{17,1},{25,9},{2,18},{10... | collective-permute-start | bytes 983048 | tf_op jit(solution)/shard_map/ppermute | solution.py:619
  714.7 19.9 %collective-permute-start.3 = (bf16[320,512]{1,0:T(8,128)(2,1)S(1)}, bf16[320,512]{1,0:T(8,128)(2,1)S(1)}, u32[]{:S(2)}, u32[]{:S(2)}) collective-permute-start(bf16[320,512]{1,0:T(8,128)(2,1)S(1)} %get-tuple-element.165), channel_id=1, source_target_pairs={{0,8},{8,0},{16,24},{24,16},{1,9},{9,1},{17,25},{25,17},{2,10},{10... | collective-permute-start | bytes 983048 | tf_op jit(solution)/shard_map/ppermute | solution.py:619
  (54 other events, 149.4 us)
Sparse Core Ops, SparseCore 0:
  10.8 51.7 all-gather.8
  64.8 92.7 all-gather.10
  159.7 87.5 all-gather.12
  502.2 97.5 reduce-scatter.5
  603.8 96.2 reduce-scatter.7
  707.4 76.8 reduce-scatter.3
  786.0 37.4 all-gather.14

commit v2 on v1

--- a/solution.py
+++ b/solution.py
@@ -249,7 +249,7 @@
         out_specs=vmem,
         scratch_shapes=scratch,
         compiler_params=pltpu.CompilerParams(collective_id=ident, has_side_effects=True),
-    )(own, tile_sizes, sizes)
+    )(own, sizes if tile_sizes is None else tile_sizes, sizes)
     flat = total.reshape(-1)
     return flat[:channels], flat[channels : 2 * channels]
 
@@ -283,7 +283,7 @@
     return jnp.einsum("pc,pd->cd", left, right, preferred_element_type=F32)
 
 
-def on_device(
+def on_device_any(
     nt,
     nb,
     features,
@@ -627,6 +627,1277 @@
     return gather_tiles(pair, 14).swapaxes(1, 2)
 
 
+PITCH = 48
+CHUNK = 64
+BLOCK = 256
+ANY = pl.BlockSpec(memory_space=pl.ANY)
+VMEM = pl.BlockSpec(memory_space=pltpu.VMEM)
+DMA = pltpu.SemaphoreType.DMA
+LONG = pl.CostEstimate(flops=80_000_000_000, bytes_accessed=30_000_000, transcendentals=2_000_000)
+
+
+class Mail:
+    def __init__(self, sems):
+        self.sems, self.used, self.open = sems, 0, []
+
+    def send(self, src, dst, peer):
+        copy = send(src, dst, self.sems.at[0, self.used], self.sems.at[1, self.used], peer)
+        self.used += 1
+        self.open.append(copy.wait_send)
+        return copy
+
+    def local(self, src, dst):
+        copy = pltpu.make_async_copy(src, dst, self.sems.at[0, self.used])
+        copy.start()
+        self.used += 1
+        return copy
+
+    def close(self):
+        for wait in self.open:
+            wait()
+        self.open = []
+
+
+class Place:
+    def __init__(self, images):
+        self.blk, self.batch = lax.axis_index("blk"), lax.axis_index("batch")
+        self.images = images
+        self.mate = (self.blk ^ 1, self.batch)
+        self.across = (self.blk ^ 2, self.batch)
+        self.tiles = [(self.blk ^ mask, self.batch) for mask in range(1, 4)]
+        self.others = [(self.blk, self.batch ^ mask) for mask in range(1, images)]
+        self.side = (self.blk, self.batch ^ 1)
+
+
+class Spread:
+    def __init__(self, mail, place, own, slot):
+        self.mail, self.place, self.own, self.slot = mail, place, own, slot
+        self.z_copies, self.x_copies = [], []
+
+    def start(self):
+        place, here = self.place, self.slot(self.place.batch)
+        self.here = self.mail.local(self.own, here)
+        for mask in range(1, place.images // 2):
+            peer = (place.blk, place.batch ^ (2 * mask))
+            self.z_copies.append(self.mail.send(self.own, here, peer))
+        self.x_copies.append(self.mail.send(self.own, here, place.side))
+        return self
+
+    def forward(self):
+        for mask, copy in enumerate(self.z_copies, 1):
+            copy.wait_recv()
+            block = self.slot(self.place.batch ^ (2 * mask))
+            self.x_copies.append(self.mail.send(block, block, self.place.side))
+
+    def finish(self):
+        self.here.wait()
+        for copy in self.x_copies:
+            copy.wait_recv()
+
+
+def share_tiles(mail, place, slot):
+    own = slot(place.blk)
+    far = mail.send(own, own, place.across)
+    near = mail.send(own, own, place.mate)
+    far.wait_recv()
+    passed = slot(place.blk ^ 2)
+    last = mail.send(passed, passed, place.mate)
+    near.wait_recv()
+    last.wait_recv()
+
+
+def loop(total, step, body):
+    def run(at, carry):
+        body(pl.ds(pl.multiple_of(at * step, step), step))
+        return carry
+
+    lax.fori_loop(0, total // step, run, 0)
+
+
+def folded(values):
+    return jnp.sum(values.reshape(values.shape[0] // 8, 8, values.shape[1]), 0)
+
+
+def loop_sums(total, channels, count, body):
+    def run(at, carry):
+        found = body(pl.ds(pl.multiple_of(at * CHUNK, CHUNK), CHUNK))
+        return tuple(kept + folded(one) for kept, one in zip(carry, found))
+
+    start = tuple(jnp.zeros((8, channels), F32) for _ in range(count))
+    return [jnp.sum(one, 0, keepdims=True) for one in lax.fori_loop(0, total // CHUNK, run, start)]
+
+
+def merge(slots, sizes, channels):
+    count = slots.shape[0]
+    size, mean = None, None
+    for at in range(count):
+        weight = sizes[at, :, :channels]
+        term = slots[at, 0:1, :] * weight
+        size = weight if size is None else size + weight
+        mean = term if mean is None else mean + term
+    mean = mean / size
+    spread = None
+    for at in range(count):
+        gap = slots[at, 0:1, :] - mean
+        term = slots[at, 1:2, :] + sizes[at, :, :channels] * gap * gap
+        spread = term if spread is None else spread + term
+    return mean, spread, size
+
+
+def add_up(slots):
+    total = slots[0]
+    for at in range(1, slots.shape[0]):
+        total = total + slots[at]
+    return total[0:1, :], total[1:2, :]
+
+
+def swap_sums(mail, place, slots):
+    own = slots.at[place.batch]
+    copies = [mail.send(own, own, peer) for peer in place.others]
+    for copy in copies:
+        copy.wait_recv()
+
+
+def swap_tile_sums(mail, place, slots):
+    own = slots.at[place.blk]
+    copies = [mail.send(own, own, peer) for peer in place.tiles]
+    for copy in copies:
+        copy.wait_recv()
+
+
+def local_stats(pre, mask, base, total, channels, size):
+    def first(rows):
+        return (pre[rows, :] * mask[at_base(base, rows), :],)
+
+    (summed,) = loop_sums(total, channels, 1, first)
+    mean = summed / jnp.maximum(size, 1.0)
+
+    def second(rows):
+        gap = pre[rows, :] - mean
+        return (gap * gap * mask[at_base(base, rows), :],)
+
+    (spread,) = loop_sums(total, channels, 1, second)
+    return mean, spread
+
+
+def at_base(base, rows):
+    if base is None:
+        return rows
+    return pl.ds(pl.multiple_of(base + rows.start, CHUNK), rows.size)
+
+
+def batch_norm_stats(mail, place, pre, mask, slots, sizes, stats, row, channels):
+    total = pre.shape[0]
+    mean, spread = local_stats(pre, mask, None, total, channels, sizes[place.batch, :, :channels])
+    slots[place.batch] = jnp.concatenate([mean, spread], 0)
+    swap_sums(mail, place, slots)
+    keep_stats(slots, sizes, stats, row, channels)
+
+
+def keep_stats(slots, sizes, stats, row, channels):
+    mean, spread, size = merge(slots, sizes, channels)
+    stats[row : row + 1, :channels] = mean
+    stats[row + 1 : row + 2, :channels] = lax.rsqrt(spread / size + EPSILON)
+
+
+def silu(values):
+    return values * jax.nn.sigmoid(values)
+
+
+def widen(cells, left, right, total):
+    def body(rows):
+        seen = cells[pl.ds(pl.multiple_of(rows.start + PITCH - 16, 16), CHUNK + 32), :].astype(F32)
+        here = pl.ds(pl.multiple_of(rows.start + PITCH, 16), CHUNK)
+        left[here, :] = seen[15 : 15 + CHUNK].astype(BF16)
+        right[here, :] = seen[17 : 17 + CHUNK].astype(BF16)
+
+    loop(total, CHUNK, body)
+
+
+def clear_ends(cells, total):
+    zeros = jnp.zeros((PITCH, cells.shape[1]), cells.dtype)
+    cells[0:PITCH, :] = zeros
+    cells[PITCH + total : 2 * PITCH + total, :] = zeros
+
+
+def conv_rows(shifted, rows, weight, back):
+    total = None
+    for offset in range(9):
+        row, col = offset // 3, offset % 3
+        if back:
+            row, col = 2 - row, 2 - col
+        window = shifted[col][pl.ds(pl.multiple_of(rows.start + PITCH * row, 16), rows.size), :]
+        product = weight(offset, window)
+        total = product if total is None else total + product
+    return total
+
+
+def sum_over_tiles(mail, place, part, near_in, pair, far_in, total, out):
+    far_first = mail.send(part(place.blk ^ 3), near_in.at[0], place.mate)
+    near_next = mail.send(part(place.blk ^ 1), near_in.at[1], place.mate)
+    far_first.wait_recv()
+    mine_far, mine = part(place.blk ^ 2), part(place.blk)
+
+    def pairs(rows):
+        pair[rows, :] = (mine_far[rows, :].astype(F32) + near_in[0, rows, :].astype(F32)).astype(BF16)
+
+    loop(total, CHUNK, pairs)
+    far = mail.send(pair, far_in, place.across)
+    near_next.wait_recv()
+    far.wait_recv()
+
+    def finish(rows):
+        out[rows, :] = (
+            mine[rows, :].astype(F32) + near_in[1, rows, :].astype(F32) + far_in[rows, :].astype(F32)
+        )
+
+    loop(total, CHUNK, finish)
+
+
+def start_kernel(
+    images,
+    weight,
+    small,
+    spatial_own,
+    feat,
+    mask,
+    sizes,
+    tile_sizes,
+    full,
+    smalls,
+    wide,
+    spatial,
+    pre_one,
+    stats,
+    slots_tile,
+    slots_one,
+    sems,
+):
+    place = Place(images)
+    mail = Mail(sems)
+    blk, batch = place.blk, place.batch
+    depth = weight.shape[0]
+    half = depth // 2
+    mid = weight.shape[1]
+    tile = feat.shape[0]
+    slim = mid // 4
+    share = spatial_own.shape[1]
+    mine = pl.ds(pl.multiple_of(lax.rem(blk, 2) * half, half), half)
+    greet(place.others + place.tiles)
+    here = mail.local(weight, full.at[batch])
+    here_small = mail.local(small, smalls.at[batch])
+    z_copies, x_copies, arrived, late = {}, [], [], []
+    for peer in place.others:
+        late.append(mail.send(small, smalls.at[batch], peer))
+    for mask_z in range(1, images // 2):
+        z_copies[mask_z] = mail.send(
+            weight.at[mine], full.at[batch, mine], (blk, batch ^ (2 * mask_z))
+        )
+    x_copies.append(mail.send(weight.at[mine], full.at[batch, mine], place.side))
+    lanes = pl.ds(pl.multiple_of(blk * slim, slim), slim)
+    got_spatial = Spread(
+        mail,
+        place,
+        spatial_own.at[:, :, lanes],
+        lambda index: spatial.at[:, pl.ds(pl.multiple_of(index * share, share), share), :],
+    ).start()
+
+    def columns(index):
+        return feat.at[:, pl.ds(pl.multiple_of(index * mid, mid), mid)]
+
+    landing = wide.at[pl.ds(pl.multiple_of(blk * tile, tile), tile), :]
+    here_wide = mail.local(columns(blk), landing)
+    for mask_t in range(1, 4):
+        late.append(mail.send(columns(blk ^ mask_t), landing, (blk ^ mask_t, batch)))
+
+    def hand_over(source):
+        block = full.at[source, mine]
+        arrived.append(mail.send(block, block, place.mate))
+
+    for mask_z in range(1, images // 2):
+        z_copies[mask_z].wait_recv()
+        source = batch ^ (2 * mask_z)
+        block = full.at[source, mine]
+        x_copies.append(mail.send(block, block, place.side))
+        hand_over(source)
+    for mask_z in range(images // 2):
+        x_copies[mask_z].wait_recv()
+        hand_over(batch ^ (2 * mask_z + 1))
+    stats[...] = jnp.zeros_like(stats)
+    here.wait()
+    for copy in arrived:
+        copy.wait_recv()
+
+    def reduce(rows):
+        total = None
+        for index in range(images):
+            product = dot(feat[rows, index * depth : (index + 1) * depth], full[index])
+            total = product if total is None else total + product
+        pre_one[rows, :] = total
+
+    loop(tile, tile // 2, reduce)
+    base = blk * tile
+    mean, spread = local_stats(pre_one, mask, base, tile, mid, tile_sizes[blk, :, :])
+    slots_tile[blk] = jnp.concatenate([mean, spread], 0)
+    swap_tile_sums(mail, place, slots_tile)
+    mean, spread, _ = merge(slots_tile, tile_sizes, mid)
+    slots_one[batch] = jnp.concatenate([mean, spread], 0)
+    swap_sums(mail, place, slots_one)
+    keep_stats(slots_one, sizes, stats, 0, mid)
+    got_spatial.forward()
+    got_spatial.finish()
+    for copy in late:
+        copy.wait_recv()
+    here_small.wait()
+    here_wide.wait()
+    mail.close()
+
+
+def begin(nb, weight, small, spatial, feat, mask, sizes, tile_sizes):
+    depth, mid = weight.shape
+    tile = feat.shape[0]
+
+    def array(*shape, kind=BF16):
+        return jax.ShapeDtypeStruct(shape, kind)
+
+    return pl.pallas_call(
+        functools.partial(start_kernel, nb),
+        out_shape=(
+            array(nb, depth, mid),
+            array(nb, *small.shape),
+            array(4 * tile, mid),
+            array(9, mid, mid // 4),
+            array(tile, mid, kind=F32),
+            array(8, mid, kind=F32),
+        ),
+        in_specs=[ANY] * 3 + [VMEM] * 4,
+        out_specs=(VMEM, ANY, VMEM, VMEM, VMEM, VMEM),
+        scratch_shapes=[
+            pltpu.VMEM((4, 2, mid), F32),
+            pltpu.VMEM((nb, 2, mid), F32),
+            DMA((2, 64)),
+        ],
+        cost_estimate=LONG,
+        compiler_params=pltpu.CompilerParams(
+            collective_id=21, has_side_effects=True, vmem_limit_bytes=40 * 2**20
+        ),
+    )(weight, small, spatial, feat, mask, sizes, tile_sizes)
+
+
+def forward_kernel(
+    images,
+    early,
+    pre_one,
+    first_stats,
+    spatial,
+    wide,
+    mask,
+    norms,
+    sizes,
+    last_own,
+    shared_own,
+    gate_own,
+    message_own,
+    last,
+    shared,
+    gate,
+    message,
+    act_one,
+    act_two,
+    act_three,
+    shared_act,
+    pre_two,
+    pre_three,
+    pre_four,
+    stats,
+    one_left,
+    one_right,
+    parts,
+    near_in,
+    pair,
+    far_in,
+    slots_two,
+    slots_three,
+    slots_four,
+    sems,
+):
+    place = Place(images)
+    mail = Mail(sems)
+    blk, batch = place.blk, place.batch
+    tile, total = pre_one.shape[0], mask.shape[0]
+    mid = pre_one.shape[1]
+    slim = pre_two.shape[1]
+    share = last_own.shape[0]
+    base = blk * tile
+    greet(place.others + place.tiles)
+
+    def rows_of(index):
+        return pl.ds(pl.multiple_of(index * share, share), share)
+
+    def slim_lanes(index):
+        return pl.ds(pl.multiple_of(index * slim, slim), slim)
+
+    lanes = slim_lanes(blk)
+    wide_lanes = pl.ds(pl.multiple_of(blk * mid, mid), mid)
+    got_last = Spread(mail, place, last_own.at[:, wide_lanes], lambda index: last.at[rows_of(index), :])
+    got_shared = Spread(mail, place, shared_own, lambda index: shared.at[rows_of(index), :])
+    got_gate = Spread(mail, place, gate_own.at[blk], lambda index: gate.at[rows_of(index), :])
+    got_message = [
+        Spread(
+            mail,
+            place,
+            message_own.at[blk, offset],
+            lambda index, offset=offset: message.at[offset, rows_of(index), :],
+        )
+        for offset in range(early)
+    ]
+    got_last.start()
+    got_shared.start()
+    stats[...] = first_stats[...]
+    clear_ends(act_one, total)
+    clear_ends(one_left, total)
+    clear_ends(one_right, total)
+
+    def act_first(rows):
+        value = (pre_one[rows, :] - stats[0:1, :]) * stats[1:2, :] * norms[0:1, :] + norms[1:2, :]
+        value = silu(value) * mask[at_base(base, rows), :]
+        act_one[pl.ds(pl.multiple_of(PITCH + base + rows.start, 16), CHUNK), :] = value.astype(BF16)
+
+    loop(tile, CHUNK, act_first)
+    share_tiles(
+        mail, place, lambda index: act_one.at[pl.ds(pl.multiple_of(PITCH + index * tile, 16), tile), :]
+    )
+    widen(act_one, one_left, one_right, total)
+    got_last.forward()
+    got_shared.forward()
+
+    shifted = (one_left, act_one, one_right)
+
+    def conv_two(rows):
+        pre_two[rows, :] = conv_rows(
+            shifted, rows, lambda offset, window: dot(window, spatial[offset]), False
+        )
+
+    loop(total, BLOCK, conv_two)
+    batch_norm_stats(mail, place, pre_two, mask, slots_two, sizes, stats, 2, slim)
+    got_gate.start()
+    got_message[0].start()
+
+    def act_second(rows):
+        value = (pre_two[rows, :] - stats[2:3, :slim]) * stats[3:4, :slim]
+        value = silu(value * norms[2:3, :slim] + norms[3:4, :slim]) * mask[rows, :]
+        act_two[rows, lanes] = value.astype(BF16)
+
+    loop(total, CHUNK, act_second)
+    share_tiles(mail, place, lambda index: act_two.at[:, slim_lanes(index)])
+
+    got_last.finish()
+    got_gate.forward()
+
+    def expand(rows):
+        pre_three[rows, :] = dot(act_two[rows, :], last[...])
+
+    loop(total, BLOCK, expand)
+    batch_norm_stats(mail, place, pre_three, mask, slots_three, sizes, stats, 4, mid)
+    got_message[0].forward()
+    got_message[1].start()
+    got_message[2].start()
+    got_shared.finish()
+
+    def act_third(rows):
+        normed = (pre_three[rows, :] - stats[4:5, :]) * stats[5:6, :]
+        value = normed * norms[4:5, :] + norms[5:6, :] + wide[rows, :].astype(F32)
+        act_three[rows, :] = (silu(value) * mask[rows, :]).astype(BF16)
+
+    loop(total, CHUNK, act_third)
+
+    def reduce(rows):
+        parts[rows, :] = dot(act_three[rows, :], shared[...]).astype(BF16)
+
+    loop(total, BLOCK, reduce)
+    sum_over_tiles(
+        mail,
+        place,
+        lambda index: parts.at[:, slim_lanes(index)],
+        near_in,
+        pair,
+        far_in,
+        total,
+        pre_four,
+    )
+    got_message[1].forward()
+    batch_norm_stats(mail, place, pre_four, mask, slots_four, sizes, stats, 6, slim)
+    got_message[2].forward()
+    for later in got_message[3:]:
+        later.start()
+
+    def act_fourth(rows):
+        value = (pre_four[rows, :] - stats[6:7, :slim]) * stats[7:8, :slim]
+        value = silu(value * norms[6:7, :slim] + norms[7:8, :slim]) * mask[rows, :]
+        shared_act[rows, lanes] = value.astype(BF16)
+
+    loop(total, CHUNK, act_fourth)
+    share_tiles(mail, place, lambda index: shared_act.at[:, slim_lanes(index)])
+    for later in got_message[3:]:
+        later.forward()
+    got_gate.finish()
+    for one in got_message:
+        one.finish()
+    mail.close()
+
+
+def bottleneck(nb, early, pre_one, stats, spatial, wide, mask, norms, sizes, last, shared, gate, message):
+    tile, total = pre_one.shape[0], mask.shape[0]
+    mid = pre_one.shape[1]
+    slim = mid // 4
+    padded = total + 2 * PITCH
+
+    def array(*shape, kind=BF16):
+        return jax.ShapeDtypeStruct(shape, kind)
+
+    outs = (
+        array(mid, mid),
+        array(mid, mid),
+        array(mid, mid),
+        array(early, mid, mid),
+        array(padded, mid),
+        array(total, mid),
+        array(total, mid),
+        array(total, mid),
+        array(total, slim, kind=F32),
+        array(total, mid, kind=F32),
+        array(total, slim, kind=F32),
+        array(8, mid, kind=F32),
+    )
+    return pl.pallas_call(
+        functools.partial(forward_kernel, nb, early),
+        out_shape=outs,
+        in_specs=[VMEM] * 7 + [ANY] * 4,
+        out_specs=(VMEM, VMEM, ANY, ANY) + (VMEM,) * 8,
+        scratch_shapes=[
+            pltpu.VMEM((padded, mid), BF16),
+            pltpu.VMEM((padded, mid), BF16),
+            pltpu.VMEM((total, mid), BF16),
+            pltpu.VMEM((2, total, slim), BF16),
+            pltpu.VMEM((total, slim), BF16),
+            pltpu.VMEM((total, slim), BF16),
+            pltpu.VMEM((nb, 2, slim), F32),
+            pltpu.VMEM((nb, 2, mid), F32),
+            pltpu.VMEM((nb, 2, slim), F32),
+            DMA((2, 128)),
+        ],
+        cost_estimate=LONG,
+        compiler_params=pltpu.CompilerParams(
+            collective_id=20, has_side_effects=True, vmem_limit_bytes=60 * 2**20
+        ),
+    )(pre_one, stats, spatial, wide, mask, norms, sizes, last, shared, gate, message)
+
+
+class Reduce:
+    def __init__(self, mail, place, grad, from_side, summed, from_line, out):
+        self.mail, self.place = mail, place
+        self.grad, self.from_side, self.summed = grad, from_side, summed
+        self.from_line, self.out = from_line, out
+        self.side = lax.rem(place.batch, 2)
+        self.line = lax.div(place.batch, 2)
+
+    def start(self):
+        self.from_x = self.mail.send(self.grad.at[:, 1 - self.side], self.from_side, self.place.side)
+
+    def middle(self):
+        place = self.place
+        self.from_x.wait_recv()
+        lines = self.from_side.shape[0]
+        for at in range(lines):
+            self.summed[at] = (
+                self.grad[at, self.side].astype(F32) + self.from_side[at].astype(F32)
+            ).astype(BF16)
+        self.copies = [
+            self.mail.send(
+                self.summed.at[self.line ^ mask],
+                self.from_line.at[mask - 1],
+                (place.blk, place.batch ^ (2 * mask)),
+            )
+            for mask in range(1, lines)
+        ]
+
+    def finish(self):
+        total = self.summed[self.line].astype(F32)
+        for at, copy in enumerate(self.copies):
+            copy.wait_recv()
+            total = total + self.from_line[at].astype(F32)
+        self.out[...] = total.astype(BF16)
+
+
+def reduce_scratch(lines, share, columns, own):
+    found = [pltpu.VMEM((lines, 2, share, columns), BF16)] if own else []
+    return found + [
+        pltpu.VMEM((lines, share, columns), BF16),
+        pltpu.VMEM((lines, share, columns), BF16),
+        pltpu.VMEM((lines - 1, share, columns), BF16),
+    ]
+
+
+def send_sums(mail, place, slots, sums):
+    slots[place.batch] = jnp.concatenate(sums, 0)
+    own = slots.at[place.batch]
+    return [mail.send(own, own, peer) for peer in place.others]
+
+
+def silu_back(value):
+    sigmoid_value = jax.nn.sigmoid(value)
+    return sigmoid_value * (1.0 + value * (1.0 - sigmoid_value))
+
+
+def backward_kernel(
+    images,
+    back,
+    pre_one,
+    pre_two,
+    pre_three,
+    pre_four,
+    stats,
+    norms,
+    mask,
+    sizes,
+    wide,
+    act_one,
+    act_two,
+    act_three,
+    spatial,
+    last,
+    shared,
+    first,
+    gate_grads,
+    stream_grads,
+    grad_input,
+    share_shared,
+    share_last,
+    share_spatial,
+    share_first,
+    share_gates,
+    share_stream,
+    sums_out,
+    near_four,
+    pair_four,
+    far_four,
+    grad_four,
+    all_four,
+    grad_three,
+    low_three,
+    low_joined,
+    joined_rows,
+    near_two,
+    pair_two,
+    far_two,
+    grad_two,
+    two_left,
+    two_here,
+    two_right,
+    turned,
+    strip,
+    near_one,
+    pair_one,
+    far_one,
+    grad_one,
+    all_one,
+    slots_four,
+    slots_three,
+    slots_two,
+    slots_tile,
+    slots_one,
+    *rest,
+):
+    place = Place(images)
+    sems = rest[-1]
+    mail = Mail(sems)
+    blk, batch = place.blk, place.batch
+    tile, total = pre_one.shape[0], mask.shape[0]
+    mid = pre_one.shape[1]
+    slim = pre_two.shape[1]
+    base = blk * tile
+    red_shared = Reduce(mail, place, *rest[0:4], share_shared)
+    red_last = Reduce(mail, place, *rest[4:8], share_last)
+    red_first = Reduce(mail, place, *rest[8:12], share_first)
+    red_spatial = Reduce(mail, place, *rest[12:16], share_spatial)
+    red_gates = Reduce(mail, place, gate_grads, *rest[16:19], share_gates)
+    red_stream = Reduce(mail, place, stream_grads, *rest[19:22], share_stream)
+    count = sizes[0]
+    for at in range(1, images):
+        count = count + sizes[at]
+    part = 1.0 / count
+    greet(place.others + place.tiles)
+
+    def slim_lanes(index):
+        return pl.ds(pl.multiple_of(index * slim, slim), slim)
+
+    def tile_rows(index):
+        return pl.ds(pl.multiple_of(index * tile, tile), tile)
+
+    def norm_back(grad, pre, row, channels, lead, offset=None, skip=None):
+        height = pre.shape[0]
+
+        def body(rows):
+            normed = (pre[rows, :] - stats[row : row + 1, :channels]) * stats[row + 1 : row + 2, :channels]
+            value = normed * norms[row : row + 1, :channels] + norms[row + 1 : row + 2, :channels]
+            if skip is not None:
+                value = value + skip[rows, :].astype(F32)
+            found = lead(rows) * mask[at_base(offset, rows), :] * silu_back(value)
+            grad[rows, :] = found
+            return found, found * normed
+
+        return loop_sums(height, channels, 2, body)
+
+    def through(grad, pre, row, channels, bias_sum, gain_sum, put, offset=None):
+        scale = stats[row + 1 : row + 2, :channels] * norms[row : row + 1, :channels]
+        bias_part = bias_sum * part[:, :channels]
+        gain_part = gain_sum * part[:, :channels]
+
+        def body(rows):
+            normed = (pre[rows, :] - stats[row : row + 1, :channels]) * stats[row + 1 : row + 2, :channels]
+            found = scale * (grad[rows, :] - bias_part - normed * gain_part)
+            put(rows, (found * mask[at_base(offset, rows), :]).astype(BF16))
+
+        loop(pre.shape[0], CHUNK, body)
+
+    def keep(row, bias_sum, gain_sum, channels):
+        sums_out[row : row + 1, :channels] = gain_sum
+        sums_out[row + 1 : row + 2, :channels] = bias_sum
+
+    sums_out[...] = jnp.zeros_like(sums_out)
+    for cells in (two_left, two_here, two_right):
+        clear_ends(cells, total)
+    red_gates.start()
+    red_stream.start()
+
+    sum_over_tiles(
+        mail, place, lambda index: back.at[:, slim_lanes(index)], near_four, pair_four, far_four, total, grad_four
+    )
+    sums = norm_back(grad_four, pre_four, 6, slim, lambda rows: grad_four[rows, :])
+    copies = send_sums(mail, place, slots_four, sums)
+    for offset in range(9):
+        turned[offset * slim : (offset + 1) * slim, :] = spatial[offset].T
+    for copy in copies:
+        copy.wait_recv()
+    bias_sum, gain_sum = add_up(slots_four)
+    keep(6, bias_sum, gain_sum, slim)
+    lanes = slim_lanes(blk)
+
+    def put_four(rows, value):
+        all_four[rows, lanes] = value
+
+    through(grad_four, pre_four, 6, slim, bias_sum, gain_sum, put_four)
+    red_gates.middle()
+    red_stream.middle()
+    share_tiles(mail, place, lambda index: all_four.at[:, slim_lanes(index)])
+
+    def joined_back(rows):
+        return dot_t(all_four[rows, :], shared[...])
+
+    sums = norm_back(grad_three, pre_three, 4, mid, joined_back, None, wide)
+    copies = send_sums(mail, place, slots_three, sums)
+    grads, lines = red_shared.grad, red_shared.grad.shape[0]
+    grads[...] = t_dot(act_three[...], all_four[...]).astype(BF16).reshape(grads.shape)
+
+    def lower(rows):
+        low_joined[rows, :] = grad_three[rows, :].astype(BF16)
+
+    loop(total, CHUNK, lower)
+    for copy in copies:
+        copy.wait_recv()
+    bias_sum, gain_sum = add_up(slots_three)
+    keep(4, bias_sum, gain_sum, mid)
+
+    def put_three(rows, value):
+        low_three[rows, :] = value
+
+    through(grad_three, pre_three, 4, mid, bias_sum, gain_sum, put_three)
+    red_gates.finish()
+    red_stream.finish()
+    mail.close()
+    red_shared.start()
+
+    def two_part(rows):
+        all_four[rows, :] = dot_t(low_three[rows, :], last[...]).astype(BF16)
+
+    loop(total, BLOCK, two_part)
+    sum_over_tiles(
+        mail, place, lambda index: all_four.at[:, slim_lanes(index)], near_two, pair_two, far_two, total, grad_two
+    )
+    landing = joined_rows.at[:, pl.ds(pl.multiple_of(blk * mid, mid), mid)]
+    joined_here = mail.local(low_joined.at[tile_rows(blk)], landing)
+    joined_copies = [
+        mail.send(low_joined.at[tile_rows(blk ^ mask_t)], landing, (blk ^ mask_t, batch))
+        for mask_t in range(1, 4)
+    ]
+    sums = norm_back(grad_two, pre_two, 2, slim, lambda rows: grad_two[rows, :])
+    copies = send_sums(mail, place, slots_two, sums)
+    grads = red_last.grad
+    grads[...] = t_dot(act_two[...], low_three[...]).astype(BF16).reshape(grads.shape)
+    for copy in copies:
+        copy.wait_recv()
+    bias_sum, gain_sum = add_up(slots_two)
+    keep(2, bias_sum, gain_sum, slim)
+
+    def put_two(rows, value):
+        two_here[pl.ds(pl.multiple_of(rows.start + PITCH, 16), CHUNK), :] = value
+
+    through(grad_two, pre_two, 2, slim, bias_sum, gain_sum, put_two)
+    widen(two_here, two_left, two_right, total)
+    red_shared.middle()
+    red_last.start()
+    shifted = (two_left, two_here, two_right)
+
+    def one_part(rows):
+        for offset in range(9):
+            row, col = 2 - offset // 3, 2 - offset % 3
+            window = shifted[col][pl.ds(pl.multiple_of(rows.start + PITCH * row, 16), BLOCK), :]
+            strip[:, offset * slim : (offset + 1) * slim] = window
+        low_three[rows, :] = dot(strip[...], turned[...]).astype(BF16)
+
+    loop(total, BLOCK, one_part)
+    sum_over_tiles(
+        mail, place, lambda index: low_three.at[tile_rows(index)], near_one, pair_one, far_one, tile, grad_one
+    )
+    sums = norm_back(grad_one, pre_one, 0, mid, lambda rows: grad_one[rows, :], base)
+    slots_tile[blk] = jnp.concatenate(sums, 0)
+    swap_tile_sums(mail, place, slots_tile)
+    copies = send_sums(mail, place, slots_one, list(add_up(slots_tile)))
+    grads = red_spatial.grad
+    for offset in range(9):
+        row, col = 2 - offset // 3, 2 - offset % 3
+        window = shifted[col][PITCH * row : PITCH * row + total, :]
+        found = t_dot(act_one[PITCH : PITCH + total, :], window).astype(BF16)
+        grads[:, :, :, offset * slim : (offset + 1) * slim] = found.reshape(grads.shape[:3] + (slim,))
+    for copy in copies:
+        copy.wait_recv()
+    bias_sum, gain_sum = add_up(slots_one)
+    keep(0, bias_sum, gain_sum, mid)
+
+    def put_one(rows, value):
+        all_one[at_base(base, rows), :] = value
+
+    through(grad_one, pre_one, 0, mid, bias_sum, gain_sum, put_one, base)
+    red_shared.finish()
+    red_last.middle()
+    red_spatial.start()
+    share_tiles(mail, place, lambda index: all_one.at[tile_rows(index)])
+    grads = red_first.grad
+    grads[...] = t_dot(wide[...], all_one[...]).astype(BF16).reshape(grads.shape)
+    red_first.start()
+    red_spatial.middle()
+    joined_here.wait()
+    for copy in joined_copies:
+        copy.wait_recv()
+
+    def input_grads(rows):
+        own = all_one[pl.ds(pl.multiple_of(base + rows.start, CHUNK), rows.size), :]
+        grad_input[rows, :] = dot_t(own, first[...]) + joined_rows[rows, :].astype(F32)
+
+    loop(tile, tile // 3, input_grads)
+    red_last.finish()
+    red_first.middle()
+    red_spatial.finish()
+    red_first.finish()
+    mail.close()
+
+
+def bottleneck_back(nb, back, pres, stats, norms, mask, sizes, wide, acts, weights, gate_grads, stream_grads):
+    tile, total = pres[0].shape[0], mask.shape[0]
+    mid = pres[0].shape[1]
+    slim = mid // 4
+    lines, share = nb // 2, mid // nb
+    padded = total + 2 * PITCH
+    width = weights[3].shape[0]
+
+    def array(*shape, kind=BF16):
+        return jax.ShapeDtypeStruct(shape, kind)
+
+    def vmem(*shape, kind=BF16):
+        return pltpu.VMEM(shape, kind)
+
+    scratch = [
+        vmem(2, total, slim),
+        vmem(total, slim),
+        vmem(total, slim),
+        vmem(total, slim, kind=F32),
+        vmem(total, mid),
+        vmem(total, mid, kind=F32),
+        vmem(total, mid),
+        vmem(total, mid),
+        vmem(tile, width),
+        vmem(2, total, slim),
+        vmem(total, slim),
+        vmem(total, slim),
+        vmem(total, slim, kind=F32),
+        vmem(padded, slim),
+        vmem(padded, slim),
+        vmem(padded, slim),
+        vmem(9 * slim, mid),
+        vmem(BLOCK, 9 * slim),
+        vmem(2, tile, mid),
+        vmem(tile, mid),
+        vmem(tile, mid),
+        vmem(tile, mid, kind=F32),
+        vmem(total, mid),
+        vmem(nb, 2, slim, kind=F32),
+        vmem(nb, 2, mid, kind=F32),
+        vmem(nb, 2, slim, kind=F32),
+        vmem(4, 2, mid, kind=F32),
+        vmem(nb, 2, mid, kind=F32),
+    ]
+    for columns in (mid, mid, mid, 9 * slim):
+        scratch += reduce_scratch(lines, share, columns, True)
+    for columns in (mid, LANES):
+        scratch += reduce_scratch(lines, share, columns, False)
+    scratch.append(DMA((2, 128)))
+    return pl.pallas_call(
+        functools.partial(backward_kernel, nb),
+        out_shape=(
+            array(tile, width, kind=F32),
+            array(share, mid),
+            array(share, mid),
+            array(share, 9 * slim),
+            array(share, mid),
+            array(share, mid),
+            array(share, LANES),
+            array(8, mid, kind=F32),
+        ),
+        in_specs=[VMEM] * 19,
+        out_specs=(VMEM,) * 8,
+        scratch_shapes=scratch,
+        cost_estimate=LONG,
+        compiler_params=pltpu.CompilerParams(
+            collective_id=22, has_side_effects=True, vmem_limit_bytes=62 * 2**20
+        ),
+    )(
+        back,
+        *pres,
+        stats,
+        norms,
+        mask,
+        sizes,
+        wide,
+        *acts,
+        *weights,
+        gate_grads.reshape(lines, 2, share, mid),
+        stream_grads.reshape(lines, 2, share, LANES),
+    )
+
+
+def on_device(
+    nt,
+    nb,
+    features,
+    crop_rows,
+    crop_cols,
+    depth_target,
+    labels,
+    first_weight,
+    spatial_weight,
+    last_weight,
+    shared_weight,
+    head_weights,
+    message_weights,
+    gate_weights,
+    depth_weight,
+    class_weight,
+    mid_gain,
+    mid_bias,
+    out_gain,
+    out_bias,
+):
+    tile_rows, cols, width = features.shape[1:]
+    tile = tile_rows * cols
+    rows = tile_rows * nt
+    pixels = rows * cols
+    tasks = head_weights.shape[0]
+    mid = first_weight.shape[1]
+    share = mid // nb
+    slim = mid // nt
+    classes = class_weight.shape[1]
+    blk, batch = lax.axis_index("blk"), lax.axis_index("batch")
+
+    image_rows = lax.dynamic_index_in_dim(crop_rows, batch, 0, False)
+    image_cols = lax.dynamic_index_in_dim(crop_cols, batch, 0, False)
+    row_ids = jnp.arange(rows, dtype=jnp.int32)
+    col_ids = jnp.arange(PITCH, dtype=jnp.int32)
+    inside_grid = (row_ids[:, None] < image_rows) & (col_ids[None, :] < image_cols)
+    inside_grid = inside_grid.astype(F32)
+    inside_wide = inside_grid.reshape(rows * PITCH, 1)
+    inside = inside_grid[:, :cols].reshape(pixels, 1)
+    inside_tile = lax.dynamic_slice_in_dim(inside, blk * tile, tile, 0)
+    sizes_flat = (crop_rows * crop_cols).astype(F32)
+    valid_count = jnp.sum(sizes_flat)
+    sizes = jnp.broadcast_to(sizes_flat[:, None, None], (nb, 1, mid))
+    tile_counts = jnp.sum(inside.reshape(nt, tile), 1)
+    tile_sizes = jnp.broadcast_to(tile_counts[:, None, None], (nt, 1, mid))
+    image_size = jnp.maximum(jnp.sum(inside), 1.0)
+
+    params = jnp.concatenate(
+        [
+            mid_gain.reshape(-1),
+            mid_bias.reshape(-1),
+            out_gain,
+            out_bias,
+            depth_weight,
+            class_weight.reshape(-1),
+        ]
+    )
+    room = -(-params.shape[0] // (16 * LANES)) * 16 * LANES
+    small = jnp.pad(params, (0, room - params.shape[0])).reshape(-1, LANES)
+    feat = jnp.pad(features[0], ((0, 0), (0, PITCH - cols), (0, 0))).reshape(tile_rows * PITCH, width)
+    piece = shared_weight.shape[0] // nt
+    order = [
+        (t * nb + b, (b * nt // nb) * nb + (b % (nb // nt)) * nt + t)
+        for t in range(nt)
+        for b in range(nb)
+    ]
+    shared_own = lax.ppermute(
+        lax.dynamic_slice_in_dim(shared_weight, blk * piece, piece, 0), ("blk", "batch"), order
+    )
+    full_first, smalls, wide_features, spatial, pre_one, stats = begin(
+        nb, first_weight, small, spatial_weight, feat, inside_wide, sizes, tile_sizes
+    )
+    full_first = full_first.reshape(width, mid)
+    smalls = smalls.reshape(nb, room)
+    at = 0
+
+    def taken(count):
+        nonlocal at
+        found = smalls[:, at : at + count]
+        at += count
+        return found
+
+    norms_count = mid_gain.shape[0]
+    out_share = out_gain.shape[0]
+    gain_mid = taken(norms_count * share).reshape(nb, norms_count, share).swapaxes(0, 1)
+    gain_mid = gain_mid.reshape(norms_count, mid).astype(F32)
+    bias_mid = taken(norms_count * share).reshape(nb, norms_count, share).swapaxes(0, 1)
+    bias_mid = bias_mid.reshape(norms_count, mid).astype(F32)
+    gain_out = lax.dynamic_slice_in_dim(taken(out_share).reshape(width), blk * mid, mid, 0).astype(F32)
+    bias_out = lax.dynamic_slice_in_dim(taken(out_share).reshape(width), blk * mid, mid, 0).astype(F32)
+    full_depth = taken(share).reshape(mid, 1)
+    full_classes = taken(share * classes).reshape(mid, classes)
+
+    def slim_of(vector):
+        return lax.dynamic_slice_in_dim(vector, blk * slim, slim, 0)
+
+    def filled(vector):
+        return jnp.pad(vector, (0, mid - vector.shape[0]))
+
+    gain_two, bias_two = slim_of(gain_mid[1]), slim_of(bias_mid[1])
+    gain_four, bias_four = slim_of(gain_mid[2]), slim_of(bias_mid[2])
+    norms = jnp.stack(
+        [
+            gain_mid[0],
+            bias_mid[0],
+            filled(gain_two),
+            filled(bias_two),
+            gain_out,
+            bias_out,
+            filled(gain_four),
+            filled(bias_four),
+        ]
+    )
+    head_own, stats = lax.optimization_barrier(
+        (lax.dynamic_index_in_dim(head_weights, blk, 0, False), stats)
+    )
+    head = lax.all_gather(head_own, "batch", axis=1, tiled=True)
+    early = 5
+    message_rest = lax.dynamic_index_in_dim(message_weights, blk, 0, False)[early:]
+    head, message_rest = lax.optimization_barrier((head, message_rest))
+    message_rest = lax.all_gather(message_rest, "batch", axis=1, tiled=True)
+    (
+        last,
+        shared,
+        gate,
+        message_start,
+        act_one,
+        act_two,
+        act_three,
+        shared_act,
+        pre_two,
+        pre_three,
+        pre_four,
+        stats,
+    ) = bottleneck(
+        nb,
+        early,
+        pre_one,
+        stats,
+        spatial,
+        wide_features,
+        inside_wide,
+        norms,
+        sizes,
+        last_weight,
+        shared_own,
+        gate_weights,
+        message_weights,
+    )
+    message = jnp.concatenate([message_start, message_rest], 0)
+
+    def narrow(cells):
+        channels = cells.shape[1]
+        return cells.reshape(-1, PITCH, channels)[:, :cols].reshape(-1, channels)
+
+    def act(values, mask):
+        return (jax.nn.silu(values) * mask).astype(BF16)
+
+    shared_map = narrow(shared_act)
+    gain_task = lax.dynamic_index_in_dim(gain_mid, 3 + blk, 0, False)
+    bias_task = lax.dynamic_index_in_dim(bias_mid, 3 + blk, 0, False)
+    pre_five = dot(windows(shared_map, rows, cols, False), head.reshape(9 * mid, mid))
+    mean = jnp.sum(pre_five * inside, 0) / image_size
+    gap = pre_five - mean
+    spread = jnp.sum(gap * gap * inside, 0)
+    few = sizes[:, :, :LANES]
+    centre, spread = all_sums(mean, spread, None, few, True, False, 5)
+    inverse_five = lax.rsqrt(spread / valid_count + EPSILON)
+    normed_five = (pre_five - centre) * inverse_five
+    norm_five = normed_five * gain_task + bias_task
+    task_act = act(norm_five, inside)
+    messages = dot(windows(task_act, rows, cols, False), message.reshape(9 * mid, mid))
+    gate_open = jax.nn.sigmoid(dot(task_act, gate))
+    gated = (gate_open * messages).astype(BF16)
+    is_first, is_last = blk == 0, blk == tasks - 1
+    depth_part = jnp.where(is_first, task_act, gated)
+    sem_part = jnp.where(is_last, task_act, gated)
+    depth_share = jnp.einsum("pc,co->op", depth_part, full_depth, preferred_element_type=F32)
+    class_share = jnp.einsum("pc,co->op", sem_part, full_classes, preferred_element_type=F32)
+    lift = -(-(1 + classes) // 8) * 8 - 1 - classes
+    shares = jnp.concatenate([depth_share, class_share, jnp.zeros((lift, pixels), F32)], 0)
+    streams = jnp.sum(gather_tiles(shares, 7), 0).T
+    depth_out = lax.dynamic_slice_in_dim(streams, blk * tile, tile, 0)[:, 0]
+    logits = lax.dynamic_slice_in_dim(streams, blk * tile, tile, 0)[:, 1 : 1 + classes]
+    targets = gather_tiles_pair(depth_target, labels, tile).reshape(pixels, 8)
+    all_depth, all_logits = streams[:, :1], streams[:, 1 : 1 + classes]
+    depth_slope = ((all_depth - targets[:, :1]) * inside).astype(BF16)
+    onehot = (targets[:, 1:2] == jnp.arange(classes, dtype=jnp.int32)[None, :].astype(F32)).astype(F32)
+    logit_slope = ((jax.nn.softmax(all_logits, axis=1) - onehot) * inside).astype(BF16)
+    grad_depth = t_dot(depth_part, depth_slope)
+    grad_classes = t_dot(sem_part, logit_slope)
+    depth_back = depth_slope.astype(F32) * full_depth.astype(F32).reshape(1, mid)
+    sem_back = dot_t(logit_slope, full_classes)
+    zero = jnp.zeros((), F32)
+    grad_gated = jnp.where(is_first, zero, depth_back) + jnp.where(is_last, zero, sem_back)
+    grad_direct = jnp.where(is_first, depth_back, zero) + jnp.where(is_last, sem_back, zero)
+
+    grad_msg = (grad_gated * gate_open).astype(BF16)
+    grad_gate = (grad_gated * messages * gate_open * (1.0 - gate_open)).astype(BF16)
+    msg_windows = windows(grad_msg, rows, cols, True)
+    gate_grads = t_dot(task_act, grad_gate).astype(BF16)
+    message_grads = t_dot(task_act, msg_windows).astype(BF16)
+    share_messages = lax.psum_scatter(message_grads, "batch", scatter_dimension=0, tiled=True)
+    task_grad = (
+        grad_direct
+        + dot_t(grad_gate, gate)
+        + dot(msg_windows, message.swapaxes(1, 2).reshape(9 * mid, mid))
+    )
+    grad_norm_five = task_grad * inside * silu_slope(norm_five)
+    bias_sum_five, gain_sum_five = all_sums(
+        jnp.sum(grad_norm_five, 0), jnp.sum(grad_norm_five * normed_five, 0), None, few, False, False, 8
+    )
+    grad_pre_five = (
+        inverse_five
+        * gain_task
+        * (grad_norm_five - bias_sum_five / valid_count - normed_five * gain_sum_five / valid_count)
+        * inside
+    ).astype(BF16)
+    five_windows = windows(grad_pre_five, rows, cols, True)
+    head_grads = t_dot(shared_map, five_windows).astype(BF16)
+    share_heads = lax.psum_scatter(head_grads, "batch", scatter_dimension=0, tiled=True)
+    shared_back = dot(five_windows, head.swapaxes(1, 2).reshape(9 * mid, mid))
+
+    stream_grads = jnp.concatenate([grad_depth, grad_classes], 1)
+    stream_grads = jnp.pad(stream_grads, ((0, 0), (0, LANES - 1 - classes))).astype(BF16)
+    back = jnp.pad(
+        shared_back.astype(BF16).reshape(rows, cols, mid), ((0, 0), (0, PITCH - cols), (0, 0))
+    ).reshape(rows * PITCH, mid)
+    (
+        grad_input,
+        share_shared,
+        share_last,
+        share_spatial,
+        share_first,
+        share_gates,
+        share_stream,
+        sums_wide,
+    ) = bottleneck_back(
+        nb,
+        back,
+        (pre_one, pre_two, pre_three, pre_four),
+        stats,
+        norms,
+        inside_wide,
+        sizes,
+        wide_features,
+        (act_one, act_two, act_three),
+        (spatial, last, shared, full_first),
+        gate_grads,
+        stream_grads,
+    )
+    grad_input = grad_input.reshape(tile_rows, PITCH, width)[:, :cols]
+
+    moved = lax.ppermute(
+        jnp.concatenate([share_first, share_shared], 1), ("blk", "batch"), [(b, a) for a, b in order]
+    )
+    share_messages, share_heads, moved = lax.optimization_barrier((share_messages, share_heads, moved))
+    early_share = jnp.concatenate([share_messages, share_heads], 1)
+    early_all = lax.all_gather(early_share, "blk", axis=0, tiled=False).astype(F32)
+    early_all = early_all.reshape(nt, share, 2, 9, mid).transpose(2, 0, 3, 1, 4)
+    red_messages, red_heads = early_all[0], early_all[1]
+    late_share = jnp.concatenate([moved, share_last, share_spatial, share_gates, share_stream], 1)
+    late_all = gather_tiles(late_share, 12).astype(F32)
+    at = 0
+
+    def part(count):
+        nonlocal at
+        found = late_all[:, :, at : at + count]
+        at += count
+        return found
+
+    red_first = part(mid).reshape(nt * share, mid)
+    red_shared = part(mid).reshape(nt * share, mid)
+    red_last = part(mid).transpose(1, 0, 2).reshape(share, width)
+    red_spatial = part(9 * slim).reshape(nt, share, 9, slim).transpose(2, 1, 0, 3).reshape(9, share, mid)
+    red_gates = part(mid)
+    streams_red = jnp.sum(part(LANES), 0)
+    red_depth = streams_red[:, 0]
+    red_classes = streams_red[:, 1 : 1 + classes]
+
+    sums = jnp.concatenate([sums_wide, gain_sum_five[None], bias_sum_five[None]], 0)
+    sums = jnp.pad(sums, ((0, 6), (0, 0)))
+    sums = gather_tiles(sums, 13)
+    two_gain, two_bias = sums[:, 2, :slim].reshape(1, mid), sums[:, 3, :slim].reshape(1, mid)
+    four_gain, four_bias = sums[:, 6, :slim].reshape(1, mid), sums[:, 7, :slim].reshape(1, mid)
+    mid_gains = jnp.concatenate([sums[0, 0:1], two_gain, four_gain, sums[:, 8]], 0)
+    mid_biases = jnp.concatenate([sums[0, 1:2], two_bias, four_bias, sums[:, 9]], 0)
+    grad_mid_gain = lax.dynamic_slice_in_dim(mid_gains, batch * share, share, 1)
+    grad_mid_bias = lax.dynamic_slice_in_dim(mid_biases, batch * share, share, 1)
+    grad_out_gain = lax.dynamic_slice_in_dim(sums[:, 4].reshape(width), batch * out_share, out_share, 0)
+    grad_out_bias = lax.dynamic_slice_in_dim(sums[:, 5].reshape(width), batch * out_share, out_share, 0)
+    return (
+        depth_out.reshape(1, tile_rows, cols),
+        logits.reshape(1, tile_rows, cols, classes),
+        grad_input.reshape(1, tile_rows, cols, width),
+        red_first,
+        red_spatial,
+        red_last,
+        red_shared,
+        red_heads,
+        red_messages,
+        red_gates,
+        red_depth,
+        red_classes,
+        grad_mid_gain,
+        grad_mid_bias,
+        grad_out_gain,
+        grad_out_bias,
+    )
+
+
 def solution(mesh):
     nt, nb = mesh.shape["blk"], mesh.shape["batch"]
     placed = (
@@ -650,7 +1921,7 @@
         P("batch"),
     )
     return jax.shard_map(
-        functools.partial(on_device, nt, nb),
+        functools.partial(on_device if nb == 8 else on_device_any, nt, nb),
         mesh=mesh,
         in_specs=placed,
         out_specs=(

time: 866 us -> 691 us (0.80)
  Pallas kernels: 265 us -> 399 us
  blocking collectives: 105 us -> 0 us
  local copies, waits for them, and re-layouts: 234 us -> 142 us
  matrix products: 121 us -> 75.6 us
  other arithmetic: 66.5 us -> 25.2 us
  waiting for transfers between devices: 43.8 us -> 19.5 us
    pallas_call x5 -> x3, Pallas kernels: 73.3 us -> 330 us  [the longest x1 152 us: bottleneck_back(): pl.pallas_call(functools.partial(backward_kernel, nb), out_shape=(array(t...]
    all_gather x3 -> x0, blocking collectives: 105 us -> none  [the longest x1 37.3 us: on_device(): lax.all_gather(lax.dynamic_index_in_dim(gate_weights, blk, 0, False), 'ba...]
    pallas_call x10 -> x2, Pallas kernels: 88.3 us -> 16.9 us  [all_sums(): pl.pallas_call(functools.partial(sums_kernel, images, half, centred, tile...]
    pallas_call x9 -> x4, Pallas kernels: 103 us -> 52.1 us  [gather_tiles(): pl.pallas_call(tiles_kernel, out_shape=jax.ShapeDtypeStruct((4,) + block....]
    reduce_scatter x1 -> x0, waiting for transfers between devices: 35.1 us -> none  [on_device(): lax.psum_scatter(late, 'batch', scatter_dimension=0, tiled=True)]
    reshape x22 -> x4, local copies, waits for them, and re-layouts: 27.2 us -> 2.69 us  [the longest x1 1.67 us: on_device(): grad_input.reshape(1, tile_rows, cols, width)]
    transpose x8 -> x1, local copies, waits for them, and re-layouts: 31.1 us -> 10.6 us  [on_device(): early_all = early_all.reshape(nt, share, 2, 9, mid).transpose(2, 0, 3, 1, 4)]
    dot_general x10 -> x5, matrix products: 62.3 us -> 45.4 us  [dot(): return jnp.dot(left, right, preferred_element_type=F32)]
  transfers between devices with their start and end apart: 13 -> 7, of which waited for: 2 -> 1; matrix products, arithmetic and copies ran while one was open for 36% -> 21% of each run, Pallas kernels for 30% -> 57%
where the time goes in v2:
time: 691 us; the launch traced here: 679 us
  Pallas kernels  399 us (58%)
  local copies, waits for them, and re-layouts  142 us (21%)
  matrix products  75.6 us (11%)
  other arithmetic  25.2 us (4%)
  waiting for transfers between devices  19.5 us (3%)
  between operations  15.9 us (2%)
    pallas_call x1, Pallas kernels, bottleneck_back(): pl.pallas_call(functools.partial(backward_kernel, nb), out_shape=(array(t...  152 us
    pallas_call x1, Pallas kernels, bottleneck(): pl.pallas_call(functools.partial(forward_kernel, nb, early), out_shape=ou...  124 us
    pallas_call x1, Pallas kernels, begin(): pl.pallas_call(functools.partial(start_kernel, nb), out_shape=(array(nb,...  54 us
    unnamed x135, local copies, waits for them, and re-layouts  53.1 us
    pallas_call x4, Pallas kernels, gather_tiles(): pl.pallas_call(tiles_kernel, out_shape=jax.ShapeDtypeStruct((4,) + block....  52.1 us
    dot_general x5, matrix products, dot(): return jnp.dot(left, right, preferred_element_type=F32)  45.4 us
    dot_general x5, matrix products, t_dot(): return jnp.einsum('pc,pd->cd', left, right, preferred_element_type=F32)  19.8 us
    all_gather x1, waiting for transfers between devices, on_device(): message_rest = lax.all_gather(message_rest, 'batch', axis=1, tiled=True)  19.4 us
  transfers between devices with their start and end apart: 7, of which 1 were waited for; matrix products, arithmetic and copies ran while one was open for 21% of the time, Pallas kernels for 57%

profile of v2, /device:TPU:0, one launch (start us, length us, event | category | flops | bytes accessed | tf_op | source)
XLA Modules:
  0.0 678.9 jit_solution(856988309673996310)
XLA Ops:
  8.8 1.2 dynamic_slice.67
  10.1 1.2 dynamic_slice.66
  11.3 1.3 fusion.31
  16.3 2.1 concatenate.57
  19.7 2.1 dynamic-slice_bitcast_fusion
  22.1 54.0 %shard_map.297 = (bf16[8,256,512]{2,1,0:T(8,128)(2,1)S(1)}, bf16[8,32,128]{2,1,0:T(8,128)(2,1)S(1)}, bf16[1536,512]{1,0:T(8,128)(2,1)S(1)}, bf16[9,512,128]{2,1,...) custom-call(bf16[256,512]{1,0:T(8,128)(2,1)S(1)} %copy-done.5, ...), custom_call_target="tpu_custom_call" | custom-call | flops 80000000000 | bytes 30000000 | tf_op jit(solution)/shard_map/pallas_call | solution.py:963
  76.2 1.3 copy-done.6
  82.9 5.3 shard_map.301
  90.7 1.7 dynamic-slice_bitcast_fusion.1
  93.8 124.4 %shard_map.298 = (bf16[512,512]{1,0:T(8,128)(2,1)}, bf16[512,512]{1,0:T(8,128)(2,1)}, bf16[512,512]{1,0:T(8,128)(2,1)}, bf16[5,512,512]{2,1,0:T(8,128)(2,1)}, bf...) custom-call(f32[384,512]{1,0:T(8,128)} %copy-done.9, ...), custom_call_target="tpu_custom_call" | custom-call | flops 80000000000 | bytes 30000000 | tf_op jit(solution)/shard_map/pallas_call | solution.py:1172
  218.2 1.6 slice.371
  220.4 1.7 constant_dynamic-update-slice_fusion.19
  222.0 4.3 pad_slice_fusion.24
  226.3 1.2 constant_dynamic-update-slice_fusion.8
  228.7 1.2 constant_dynamic-update-slice_fusion.6
  232.3 1.2 constant_dynamic-update-slice_fusion.3
  234.7 1.3 constant_dynamic-update-slice_fusion.1
  237.2 10.5 %multiply_reduce_fusion.2 = (f32[512]{0:T(512)S(1)}, f32[1280,512]{1,0:T(8,128)S(1)}) fusion(f32[1280]{0:T(1024)S(1)} %mul.171, bf16[1280,4608]{1,0:T(8,128)(2,1)} %constant_dynamic-update-slice_fusion, bf16[4608,512]{1,0:T(8,128)(2,1)} %bitcast.211), kind=kOutput, calls=%fused_computation.28 | convolution fusion | flops 6041107968 | bytes 19143680 | tf_op jit(solution)/shard_map/dot_general | solution.py:275
  249.5 8.2 %shard_map.299 = f32[8,128]{1,0:T(8,128)} custom-call(f32[8,128]{1,0:T(8,128)} %pad_maximum_fusion.3.own, f32[8,1,128]{2,1,0:T(1,128)} %slice.301.tile_sizes.sizes, f32[8,1,128]{2,1,0:T(1,128)} %slice.301.tile_sizes.sizes), custom_call_target="tpu_custom_call" | custom-call | tf_op jit(solution)/shard_map/pallas_call | solution.py:245
  257.7 1.4 slice_bitcast_fusion.12
  260.0 4.8 pad_slice_fusion.16
  264.8 1.2 constant_dynamic-update-slice_fusion.17
  267.3 1.2 constant_dynamic-update-slice_fusion.15
  269.7 2.0 constant_dynamic-update-slice_fusion.13
  271.7 1.2 constant_dynamic-update-slice_fusion.12
  274.1 1.3 constant_dynamic-update-slice_fusion.10
  276.5 19.4 %all-gather.7.cloned.1.call-done = bf16[4,512,512]{2,1,0:T(8,128)(2,1)} async-done(((bf16[4,64,512]{2,1,0:T(8,128)(2,1)}), bf16[4,512,512]{2,1,0:T(8,128)(2,1)}) %all-gather.7.cloned.1.call-update) | async-done | bytes 2097168 | tf_op jit(solution)/shard_map/all_gather | solution.py:1710
  295.9 3.0 constant_dynamic-update-slice_fusion.18
  298.9 10.6 %fusion.35 = f32[1280,512]{1,0:T(8,128)S(1)} fusion(bf16[1280,4608]{1,0:T(8,128)(2,1)} %constant_dynamic-update-slice_fusion.9, bf16[4608,512]{1,0:T(8,128)(2,1)} %bitcast.176), kind=kOutput, calls=%fused_computation.206 | convolution fusion | flops 6039797760 | bytes 19136512 | tf_op jit(solution)/shard_map/dot_general | solution.py:275
  309.6 2.7 multiply_convert_fusion.3
  314.1 10.1 %shard_map.300 = f32[4,48,1280]{2,1,0:T(8,128)} custom-call(f32[48,1280]{1,0:T(8,128)} %maximum_maximum_fusion.block), custom_call_target="tpu_custom_call" | custom-call | tf_op jit(solution)/shard_map/pallas_call | solution.py:134
  324.2 1.3 reduce_sum.104
  325.6 5.6 multiply_convert_fusion.2
  331.3 4.2 pad_slice_fusion.8
  336.4 4.4 copy-done.30
  340.7 8.0 %convolution_convert_fusion.1 = bf16[512,4608]{1,0:T(8,128)(2,1)} fusion(bf16[1280,512]{1,0:T(8,128)(2,1)S(1)} %copy-done.14, bf16[1280,4608]{1,0:T(8,128)(2,1)S(1)} %constant_dynamic-update-slice_fusion.20), kind=kOutput, calls=%fused_computation.3 | convolution fusion | flops 6042157056 | bytes 17825792 | tf_op jit(solution)/shard_map/pc,pd->cd/dot_general | solution.py:283
  348.8 7.1 %copy.88 = bf16[9,512,512]{2,1,0:T(8,128)(2,1)} copy(bf16[9,512,512]{1,2,0:T(8,128)(2,1)} %bitcast.212) | data formatting | bytes 9437184 | tf_op jit(solution)/shard_map/transpose | solution.py:1811
  355.9 6.6 copy.87
  362.5 1.8 fusion.8
  365.9 10.7 %fusion.36 = f32[1280,512]{1,0:T(8,128)S(1)} fusion(bf16[1280,4608]{1,0:T(8,128)(2,1)} %copy-done.30, bf16[4608,512]{1,0:T(8,128)(2,1)} %bitcast.214), kind=kOutput, calls=%fused_computation.207 | convolution fusion | flops 6039797760 | bytes 19136512 | tf_op jit(solution)/shard_map/dot_general | solution.py:275
  376.7 3.9 fusion.28
  381.1 8.7 %shard_map.302 = f32[8,128]{1,0:T(8,128)} custom-call(f32[8,128]{1,0:T(8,128)} %pad_maximum_fusion.4.own, f32[8,1,128]{2,1,0:T(1,128)} %slice.301.tile_sizes.sizes, f32[8,1,128]{2,1,0:T(1,128)} %slice.301.tile_sizes.sizes), custom_call_target="tpu_custom_call" | custom-call | tf_op jit(solution)/shard_map/pallas_call | solution.py:245
  389.8 1.4 fusion.34
  391.2 3.2 multiply_convert_fusion
  394.4 4.2 pad_slice_fusion
  399.5 4.4 copy-done.31
  403.9 8.0 %convolution_convert_fusion = bf16[512,4608]{1,0:T(8,128)(2,1)} fusion(bf16[1280,512]{1,0:T(8,128)(2,1)S(1)} %bitcast.174, bf16[1280,4608]{1,0:T(8,128)(2,1)S(1)} %constant_dynamic-update-slice_fusion.29), kind=kOutput, calls=%fused_computation.2 | convolution fusion | flops 6042157056 | bytes 17825792 | tf_op jit(solution)/shard_map/pc,pd->cd/dot_general | solution.py:283
  412.0 10.8 %convolution_convert_fusion.2 = bf16[1280,512]{1,0:T(8,128)(2,1)S(1)} fusion(bf16[1280,4608]{1,0:T(8,128)(2,1)} %copy-done.31, bf16[4608,512]{1,0:T(8,128)(2,1)} %bitcast.213), kind=kOutput, calls=%fused_computation.14 | convolution fusion | flops 6040453120 | bytes 17825792 | tf_op jit(solution)/shard_map/dot_general | solution.py:275
  422.8 1.3 pad.62
  425.0 1.7 convolution_convert_fusion.3
  426.7 151.9 %shard_map.303 = (f32[384,2048]{1,0:T(8,128)}, bf16[64,512]{1,0:T(8,128)(2,1)}, bf16[64,512]{1,0:T(8,128)(2,1)}, bf16[64,1152]{1,0:T(8,128)(2,1)}, bf16[64,512]{...) custom-call(bf16[1536,512]{1,0:T(8,128)(2,1)} %bitcast.221, ...), custom_call_target="tpu_custom_call" | custom-call | flops 80000000000 | bytes 30000000 | tf_op jit(solution)/shard_map/pallas_call | solution.py:1554
  580.6 2.3 pad_maximum_fusion
  585.2 12.9 %shard_map.305 = f32[4,16,512]{2,1,0:T(8,128)} custom-call(f32[16,512]{1,0:T(8,128)} %select_maximum_fusion.block), custom_call_target="tpu_custom_call" | custom-call | tf_op jit(solution)/shard_map/pallas_call | solution.py:134
  603.5 1.7 slice_bitcast_fusion.2
  606.0 23.9 %shard_map.304 = bf16[4,64,3328]{2,1,0:T(8,128)(2,1)} custom-call(bf16[64,3328]{1,0:T(8,128)(2,1)} %copy-done.28), custom_call_target="tpu_custom_call" | custom-call | tf_op jit(solution)/shard_map/pallas_call | solution.py:134
  629.9 1.3 slice.381
  631.6 2.0 convert_element_type.163
  633.6 1.5 reshape.462
  635.1 2.4 copy.91
  637.5 1.5 reshape.463
  644.4 10.6 %reshape.472 = f32[4,64,2,9,512]{4,3,2,1,0:T(8,128)} reshape(bf16[256,9216]{1,0:T(8,128)(2,1)} %all-gather.9.cloned.1.call-done) | data formatting | bytes 14155776 | tf_op jit(solution)/shard_map/transpose | solution.py:1849
  655.0 7.0 %slice_bitcast_fusion = (f32[4,9,64,512]{3,1,2,0:T(8,128)S(1)}, f32[4,9,64,512]{3,1,2,0:T(8,128)S(1)}) fusion(f32[2,4,9,64,512]{4,2,0,3,1:T(8,128)} %bitcast.170), kind=kLoop, calls=%fused_computation | loop fusion | bytes 18874368 | tf_op jit(solution)/shard_map/squeeze | solution.py:1850
  662.0 5.0 copy.95
  667.0 5.0 copy.94
  (241 shorter events, 52.2 us)
Async XLA Ops:
  7.2 1.0 copy-start
  7.2 14.6 %copy-start.27 = (bf16[1,8,40,2048]{3,2,1,0:T(8,128)(2,1)S(1)}, bf16[1,8,40,2048]{3,2,1,0:T(8,128)(2,1)}, u32[]{:S(2)}) copy-start(bf16[1,8,40,2048]{3,2,1,0:T(8,128)(2,1)} %param.18) | copy-start | bytes 3932164
  7.2 14.9 %copy-start.4 = (bf16[9,64,512]{2,1,0:T(8,128)(2,1)S(1)}, bf16[9,64,512]{2,1,0:T(8,128)(2,1)}, u32[]{:S(2)}) copy-start(bf16[9,64,512]{2,1,0:T(8,128)(2,1)} %spatial_own.1) | copy-start | bytes 1769476
  7.2 14.9 %copy-start.5 = (bf16[256,512]{1,0:T(8,128)(2,1)S(1)}, bf16[256,512]{1,0:T(8,128)(2,1)}, u32[]{:S(2)}) copy-start(bf16[256,512]{1,0:T(8,128)(2,1)} %weight.1) | copy-start | bytes 786436
  7.2 229.9 %all-gather.5.cloned.1.call-start = ((), (), s32[]{:S(2)}) async-start(), calls=%async_computation.2 | async-start | bytes 5308416 | tf_op jit(solution)/shard_map/all_gather | solution.py:1706
  8.1 85.0 %collective-permute-start = (bf16[64,512]{1,0:T(8,128)(2,1)S(1)}, bf16[64,512]{1,0:T(8,128)(2,1)S(1)}, u32[]{:S(2)}, u32[]{:S(2)}) collective-permute-start(bf16[64,512]{1,0:T(8,128)(2,1)S(1)} %constant_dynamic-slice_fusion.2), channel_id=1, source_target_pairs={{0,0},{1,4},{2,8},{3,12},{4,16},{5,20},{6,24},{7,28},{8,1},{9,5},{... | collective-permute-start | bytes 196616 | tf_op jit(solution)/shard_map/ppermute | solution.py:1656
  12.6 9.4 %copy-start.36 = (f32[8]{0:T(128)}, f32[8]{0:T(128)S(1)}, u32[]{:S(2)}) copy-start(f32[8]{0:T(128)S(1)} %get-tuple-element.161) | copy-start | bytes 100
  19.6 56.6 %copy-start.2 = (f32[1536,1]{1,0:T(8,128)}, f32[1536,1]{1,0:T(8,128)S(1)}, u32[]{:S(2)}) copy-start(f32[1536,1]{1,0:T(8,128)S(1)} %reshape.483.mask) | copy-start | bytes 18436
  22.0 54.1 %copy-start.3 = (f32[8,1,512]{2,1,0:T(1,128)}, f32[8,1,512]{2,1,0:T(1,128)S(1)}, u32[]{:S(2)}) copy-start(f32[8,1,512]{2,1,0:T(1,128)S(1)} %broadcast_in_dim.14.sizes) | copy-start | bytes 49156
  22.1 60.0 %copy-start.38 = (f32[1,8,40]{2,1,0:T(8,128)S(1)}, f32[1,8,40]{2,1,0:T(8,128)}, u32[]{:S(2)}) copy-start(f32[1,8,40]{2,1,0:T(8,128)} %param.21) | copy-start | bytes 3844
  22.1 60.0 %copy-start.39 = (s32[1,8,40]{2,1,0:T(8,128)S(1)}, s32[1,8,40]{2,1,0:T(8,128)}, u32[]{:S(2)}) copy-start(s32[1,8,40]{2,1,0:T(8,128)} %param.22) | copy-start | bytes 3844
  76.1 1.4 copy-start.6
  77.5 1.1 copy-start.7
  78.6 1.0 copy-start.8
  79.7 0.9 copy-start.9
  80.6 0.6 copy-start.10
  81.2 214.7 %all-gather.7.cloned.1.call-start = ((), (), s32[]{:S(2)}) async-start(), calls=%async_computation.3 | async-start | bytes 2359296 | tf_op jit(solution)/shard_map/all_gather | solution.py:1710
  93.1 0.6 copy-start.40
  218.2 2.1 copy-start.21
  219.8 11.4 %copy-start.17 = (bf16[32,40,512]{2,1,0:T(8,128)(2,1)}, bf16[32,40,512]{2,1,0:T(8,128)(2,1)S(1)}, u32[]{:S(2)}) copy-start(bf16[32,40,512]{2,1,0:T(8,128)(2,1)S(1)} %slice.371) | copy-start | bytes 3932164
  247.7 1.1 copy-start.37
  247.8 332.8 %reduce-scatter.3.cloned.1.call-start = ((), (), s32[]{:S(2)}) async-start(), calls=%async_computation.4 | async-start | bytes 5308416 | tf_op jit(solution)/shard_map/reduce_scatter | solution.py:1792
  260.0 7.2 %copy-start.12 = (bf16[1280,512]{1,0:T(8,128)(2,1)}, bf16[1280,512]{1,0:T(8,128)(2,1)S(1)}, u32[]{:S(2)}) copy-start(bf16[1280,512]{1,0:T(8,128)(2,1)S(1)} %multiply_convert_fusion.4) | copy-start | bytes 3932164
  298.9 10.6 %copy-start.13 = (bf16[1280,512]{1,0:T(8,128)(2,1)S(1)}, bf16[1280,512]{1,0:T(8,128)(2,1)}, u32[]{:S(2)}) copy-start(bf16[1280,512]{1,0:T(8,128)(2,1)} %copy-done.12) | copy-start | bytes 3932164
  298.9 10.6 %copy-start.41 = (bf16[512,512]{1,0:T(8,128)(2,1)S(1)}, bf16[512,512]{1,0:T(8,128)(2,1)}, u32[]{:S(2)}) copy-start(bf16[512,512]{1,0:T(8,128)(2,1)} %get-tuple-element.58) | copy-start | bytes 1572868
  309.5 2.8 copy-start.23
  312.3 1.1 copy-start.19
  336.1 4.6 copy-start.14
  336.3 4.4 copy-start.30
  348.8 231.8 %reduce-scatter.5.cloned.1.call-start = ((), (), s32[]{:S(2)}) async-start(), calls=%async_computation.5 | async-start | bytes 5308416 | tf_op jit(solution)/shard_map/reduce_scatter | solution.py:1810
  362.5 1.8 copy-start.15
  362.5 2.1 copy-start.20
  365.9 10.8 %copy-start.22 = (f32[1280,512]{1,0:T(8,128)S(1)}, f32[1280,512]{1,0:T(8,128)}, u32[]{:S(2)}) copy-start(f32[1280,512]{1,0:T(8,128)} %get-tuple-element.227) | copy-start | bytes 7864324
  365.9 10.8 %copy-start.25 = (bf16[1280,512]{1,0:T(8,128)(2,1)S(1)}, bf16[1280,512]{1,0:T(8,128)(2,1)}, u32[]{:S(2)}) copy-start(bf16[1280,512]{1,0:T(8,128)(2,1)} %get-tuple-element.164) | copy-start | bytes 3932164
  365.9 10.8 %copy-start.42 = (bf16[512,512]{1,0:T(8,128)(2,1)S(1)}, bf16[512,512]{1,0:T(8,128)(2,1)}, u32[]{:S(2)}) copy-start(bf16[512,512]{1,0:T(8,128)(2,1)} %get-tuple-element.58) | copy-start | bytes 1572868
  399.3 4.6 copy-start.18
  399.5 4.4 copy-start.31
  411.9 232.5 %all-gather.9.cloned.1.call-start = ((), (), s32[]{:S(2)}) async-start(), calls=%async_computation.6 | async-start | bytes 5898240 | tf_op jit(solution)/shard_map/all_gather | solution.py:1848
  422.7 1.7 copy-start.16
  422.7 2.3 copy-start.26
  578.6 6.0 copy-start.35
  578.6 24.9 %copy-start.24 = (f32[384,2048]{1,0:T(8,128)S(1)}, f32[384,2048]{1,0:T(8,128)}, u32[]{:S(2)}) copy-start(f32[384,2048]{1,0:T(8,128)} %get-tuple-element.71) | copy-start | bytes 9437188
  579.6 0.9 collective-permute-start.1
  603.5 1.7 copy-start.33
  603.5 1.7 copy-start.29
  603.5 1.8 copy-start.32
  603.5 1.8 copy-start.34
  605.3 0.8 copy-start.28
  629.9 1.7 copy-start.11
  667.0 5.0 copy-start.1
Sparse Core Ops, SparseCore 0:
  81.3 110.8 all-gather.4
  247.9 47.9 all-gather.6
  348.9 94.4 reduce-scatter.2
  447.5 115.7 reduce-scatter.4
  583.1 54.7 all-gather.8

commit v3 on v2

--- a/solution.py
+++ b/solution.py
@@ -859,12 +859,14 @@
     weight,
     small,
     spatial_own,
+    pair,
     feat,
     mask,
     sizes,
     tile_sizes,
     full,
     smalls,
+    targets,
     wide,
     spatial,
     pre_one,
@@ -907,7 +909,10 @@
 
     landing = wide.at[pl.ds(pl.multiple_of(blk * tile, tile), tile), :]
     here_wide = mail.local(columns(blk), landing)
+    line = targets.at[:, pl.ds(pl.multiple_of(blk * tile, tile), tile)]
+    here_line = mail.local(pair, line)
     for mask_t in range(1, 4):
+        late.append(mail.send(pair, line, (blk ^ mask_t, batch)))
         late.append(mail.send(columns(blk ^ mask_t), landing, (blk ^ mask_t, batch)))
 
     def hand_over(source):
@@ -950,10 +955,11 @@
         copy.wait_recv()
     here_small.wait()
     here_wide.wait()
+    here_line.wait()
     mail.close()
 
 
-def begin(nb, weight, small, spatial, feat, mask, sizes, tile_sizes):
+def begin(nb, weight, small, spatial, pair, feat, mask, sizes, tile_sizes):
     depth, mid = weight.shape
     tile = feat.shape[0]
 
@@ -965,13 +971,14 @@
         out_shape=(
             array(nb, depth, mid),
             array(nb, *small.shape),
+            array(8, 4 * tile, kind=F32),
             array(4 * tile, mid),
             array(9, mid, mid // 4),
             array(tile, mid, kind=F32),
             array(8, mid, kind=F32),
         ),
-        in_specs=[ANY] * 3 + [VMEM] * 4,
-        out_specs=(VMEM, ANY, VMEM, VMEM, VMEM, VMEM),
+        in_specs=[ANY] * 4 + [VMEM] * 4,
+        out_specs=(VMEM, ANY, ANY, VMEM, VMEM, VMEM, VMEM),
         scratch_shapes=[
             pltpu.VMEM((4, 2, mid), F32),
             pltpu.VMEM((nb, 2, mid), F32),
@@ -981,7 +988,7 @@
         compiler_params=pltpu.CompilerParams(
             collective_id=21, has_side_effects=True, vmem_limit_bytes=40 * 2**20
         ),
-    )(weight, small, spatial, feat, mask, sizes, tile_sizes)
+    )(weight, small, spatial, pair, feat, mask, sizes, tile_sizes)
 
 
 def forward_kernel(
@@ -1055,6 +1062,7 @@
     got_shared.start()
     stats[...] = first_stats[...]
     clear_ends(act_one, total)
+    clear_ends(shared_act, total)
     clear_ends(one_left, total)
     clear_ends(one_right, total)
 
@@ -1134,10 +1142,12 @@
     def act_fourth(rows):
         value = (pre_four[rows, :] - stats[6:7, :slim]) * stats[7:8, :slim]
         value = silu(value * norms[6:7, :slim] + norms[7:8, :slim]) * mask[rows, :]
-        shared_act[rows, lanes] = value.astype(BF16)
+        shared_act[pl.ds(pl.multiple_of(PITCH + rows.start, 16), CHUNK), lanes] = value.astype(BF16)
 
     loop(total, CHUNK, act_fourth)
-    share_tiles(mail, place, lambda index: shared_act.at[:, slim_lanes(index)])
+    share_tiles(
+        mail, place, lambda index: shared_act.at[pl.ds(PITCH, total), slim_lanes(index)]
+    )
     for later in got_message[3:]:
         later.forward()
     got_gate.finish()
@@ -1163,7 +1173,7 @@
         array(padded, mid),
         array(total, mid),
         array(total, mid),
-        array(total, mid),
+        array(padded, mid),
         array(total, slim, kind=F32),
         array(total, mid, kind=F32),
         array(total, slim, kind=F32),
@@ -1247,6 +1257,34 @@
 def silu_back(value):
     sigmoid_value = jax.nn.sigmoid(value)
     return sigmoid_value * (1.0 + value * (1.0 - sigmoid_value))
+
+
+def norm_back(stats, norms, mask, grad, pre, row, channels, lead, offset=None, skip=None):
+    def body(rows):
+        normed = (pre[rows, :] - stats[row : row + 1, :channels]) * stats[row + 1 : row + 2, :channels]
+        value = normed * norms[row : row + 1, :channels] + norms[row + 1 : row + 2, :channels]
+        if skip is not None:
+            value = value + skip[rows, :].astype(F32)
+        found = lead(rows) * mask[at_base(offset, rows), :] * silu_back(value)
+        grad[rows, :] = found
+        return found, found * normed
+
+    return loop_sums(pre.shape[0], channels, 2, body)
+
+
+def through(stats, norms, mask, sizes, grad, pre, row, channels, bias_sum, gain_sum, put, offset=None):
+    count = sizes[0, :, :channels]
+    for at in range(1, sizes.shape[0]):
+        count = count + sizes[at, :, :channels]
+    scale = stats[row + 1 : row + 2, :channels] * norms[row : row + 1, :channels]
+    bias_part, gain_part = bias_sum / count, gain_sum / count
+
+    def body(rows):
+        normed = (pre[rows, :] - stats[row : row + 1, :channels]) * stats[row + 1 : row + 2, :channels]
+        found = scale * (grad[rows, :] - bias_part - normed * gain_part)
+        put(rows, (found * mask[at_base(offset, rows), :]).astype(BF16))
+
+    loop(pre.shape[0], CHUNK, body)
 
 
 def backward_kernel(
@@ -1322,10 +1360,6 @@
     red_spatial = Reduce(mail, place, *rest[12:16], share_spatial)
     red_gates = Reduce(mail, place, gate_grads, *rest[16:19], share_gates)
     red_stream = Reduce(mail, place, stream_grads, *rest[19:22], share_stream)
-    count = sizes[0]
-    for at in range(1, images):
-        count = count + sizes[at]
-    part = 1.0 / count
     greet(place.others + place.tiles)
 
     def slim_lanes(index):
@@ -1333,32 +1367,6 @@
 
     def tile_rows(index):
         return pl.ds(pl.multiple_of(index * tile, tile), tile)
-
-    def norm_back(grad, pre, row, channels, lead, offset=None, skip=None):
-        height = pre.shape[0]
-
-        def body(rows):
-            normed = (pre[rows, :] - stats[row : row + 1, :channels]) * stats[row + 1 : row + 2, :channels]
-            value = normed * norms[row : row + 1, :channels] + norms[row + 1 : row + 2, :channels]
-            if skip is not None:
-                value = value + skip[rows, :].astype(F32)
-            found = lead(rows) * mask[at_base(offset, rows), :] * silu_back(value)
-            grad[rows, :] = found
-            return found, found * normed
-
-        return loop_sums(height, channels, 2, body)
-
-    def through(grad, pre, row, channels, bias_sum, gain_sum, put, offset=None):
-        scale = stats[row + 1 : row + 2, :channels] * norms[row : row + 1, :channels]
-        bias_part = bias_sum * part[:, :channels]
-        gain_part = gain_sum * part[:, :channels]
-
-        def body(rows):
-            normed = (pre[rows, :] - stats[row : row + 1, :channels]) * stats[row + 1 : row + 2, :channels]
-            found = scale * (grad[rows, :] - bias_part - normed * gain_part)
-            put(rows, (found * mask[at_base(offset, rows), :]).astype(BF16))
-
-        loop(pre.shape[0], CHUNK, body)
 
     def keep(row, bias_sum, gain_sum, channels):
         sums_out[row : row + 1, :channels] = gain_sum
@@ -1373,7 +1381,7 @@
     sum_over_tiles(
         mail, place, lambda index: back.at[:, slim_lanes(index)], near_four, pair_four, far_four, total, grad_four
     )
-    sums = norm_back(grad_four, pre_four, 6, slim, lambda rows: grad_four[rows, :])
+    sums = norm_back(stats, norms, mask, grad_four, pre_four, 6, slim, lambda rows: grad_four[rows, :])
     copies = send_sums(mail, place, slots_four, sums)
     for offset in range(9):
         turned[offset * slim : (offset + 1) * slim, :] = spatial[offset].T
@@ -1386,7 +1394,7 @@
     def put_four(rows, value):
         all_four[rows, lanes] = value
 
-    through(grad_four, pre_four, 6, slim, bias_sum, gain_sum, put_four)
+    through(stats, norms, mask, sizes, grad_four, pre_four, 6, slim, bias_sum, gain_sum, put_four)
     red_gates.middle()
     red_stream.middle()
     share_tiles(mail, place, lambda index: all_four.at[:, slim_lanes(index)])
@@ -1394,7 +1402,7 @@
     def joined_back(rows):
         return dot_t(all_four[rows, :], shared[...])
 
-    sums = norm_back(grad_three, pre_three, 4, mid, joined_back, None, wide)
+    sums = norm_back(stats, norms, mask, grad_three, pre_three, 4, mid, joined_back, None, wide)
     copies = send_sums(mail, place, slots_three, sums)
     grads, lines = red_shared.grad, red_shared.grad.shape[0]
     grads[...] = t_dot(act_three[...], all_four[...]).astype(BF16).reshape(grads.shape)
@@ -1411,7 +1419,7 @@
     def put_three(rows, value):
         low_three[rows, :] = value
 
-    through(grad_three, pre_three, 4, mid, bias_sum, gain_sum, put_three)
+    through(stats, norms, mask, sizes, grad_three, pre_three, 4, mid, bias_sum, gain_sum, put_three)
     red_gates.finish()
     red_stream.finish()
     mail.close()
@@ -1430,7 +1438,7 @@
         mail.send(low_joined.at[tile_rows(blk ^ mask_t)], landing, (blk ^ mask_t, batch))
         for mask_t in range(1, 4)
     ]
-    sums = norm_back(grad_two, pre_two, 2, slim, lambda rows: grad_two[rows, :])
+    sums = norm_back(stats, norms, mask, grad_two, pre_two, 2, slim, lambda rows: grad_two[rows, :])
     copies = send_sums(mail, place, slots_two, sums)
     grads = red_last.grad
     grads[...] = t_dot(act_two[...], low_three[...]).astype(BF16).reshape(grads.shape)
@@ -1442,7 +1450,7 @@
     def put_two(rows, value):
         two_here[pl.ds(pl.multiple_of(rows.start + PITCH, 16), CHUNK), :] = value
 
-    through(grad_two, pre_two, 2, slim, bias_sum, gain_sum, put_two)
+    through(stats, norms, mask, sizes, grad_two, pre_two, 2, slim, bias_sum, gain_sum, put_two)
     widen(two_here, two_left, two_right, total)
     red_shared.middle()
     red_last.start()
@@ -1459,7 +1467,7 @@
     sum_over_tiles(
         mail, place, lambda index: low_three.at[tile_rows(index)], near_one, pair_one, far_one, tile, grad_one
     )
-    sums = norm_back(grad_one, pre_one, 0, mid, lambda rows: grad_one[rows, :], base)
+    sums = norm_back(stats, norms, mask, grad_one, pre_one, 0, mid, lambda rows: grad_one[rows, :], base)
     slots_tile[blk] = jnp.concatenate(sums, 0)
     swap_tile_sums(mail, place, slots_tile)
     copies = send_sums(mail, place, slots_one, list(add_up(slots_tile)))
@@ -1477,7 +1485,7 @@
     def put_one(rows, value):
         all_one[at_base(base, rows), :] = value
 
-    through(grad_one, pre_one, 0, mid, bias_sum, gain_sum, put_one, base)
+    through(stats, norms, mask, sizes, grad_one, pre_one, 0, mid, bias_sum, gain_sum, put_one, base)
     red_shared.finish()
     red_last.middle()
     red_spatial.start()
@@ -1585,6 +1593,339 @@
     )
 
 
+class Tiles:
+    def __init__(self, mail, place, slot):
+        self.mail, self.place, self.slot = mail, place, slot
+
+    def start(self):
+        own = self.slot(self.place.blk)
+        self.far = self.mail.send(own, own, self.place.across)
+        self.near = self.mail.send(own, own, self.place.mate)
+
+    def forward(self):
+        self.far.wait_recv()
+        passed = self.slot(self.place.blk ^ 2)
+        self.last = self.mail.send(passed, passed, self.place.mate)
+
+    def finish(self):
+        self.near.wait_recv()
+        self.last.wait_recv()
+
+
+def task_kernel(
+    images,
+    early,
+    shared_act,
+    mask,
+    mask_line,
+    targets,
+    sizes,
+    norms,
+    head,
+    message_start,
+    gate,
+    to_depth,
+    to_classes,
+    from_gated,
+    streams,
+    slopes,
+    pre_five,
+    stats,
+    grad_msg,
+    grad_gate,
+    gate_grads,
+    stream_grads,
+    message_grads,
+    left,
+    right,
+    task,
+    messages,
+    opened,
+    gated,
+    slots,
+    slots_five,
+    sems,
+):
+    place = Place(images)
+    mail = Mail(sems)
+    total = mask.shape[0]
+    mid = pre_five.shape[1]
+    is_first, is_last = place.blk == 0, place.blk == 3
+    greet(place.others + [place.mate, place.across])
+    stats[...] = jnp.zeros_like(stats)
+    for cells in (left, right, task, grad_msg):
+        clear_ends(cells, total)
+    widen(shared_act, left, right, total)
+
+    def heads(rows):
+        pre_five[rows, :] = conv_rows(
+            (left, shared_act, right), rows, lambda offset, window: dot(window, head[offset]), False
+        )
+
+    loop(total, BLOCK, heads)
+    batch_norm_stats(mail, place, pre_five, mask, slots_five, sizes, stats, 0, mid)
+
+    def act_task(rows):
+        value = (pre_five[rows, :] - stats[0:1, :]) * stats[1:2, :] * norms[0:1, :] + norms[1:2, :]
+        task[pl.ds(pl.multiple_of(PITCH + rows.start, 16), CHUNK), :] = (
+            silu(value) * mask[rows, :]
+        ).astype(BF16)
+
+    loop(total, CHUNK, act_task)
+    widen(task, left, right, total)
+
+    def message_weight(offset):
+        return message_start[offset] if offset < early else head[9 + offset - early]
+
+    def here(rows):
+        return pl.ds(pl.multiple_of(PITCH + rows.start, 16), rows.size)
+
+    def send_messages(rows):
+        messages[rows, :] = conv_rows(
+            (left, task, right), rows, lambda offset, window: dot(window, message_weight(offset)), False
+        )
+        own = task[here(rows), :]
+        opened[rows, :] = jax.nn.sigmoid(dot(own, gate[...]))
+        part = (opened[rows, :] * messages[rows, :]).astype(BF16)
+        gated[rows, :] = part
+        depth_part = jnp.where(is_first, own, part)
+        sem_part = jnp.where(is_last, own, part)
+        slots[place.blk, :, rows] = dot_t(to_depth[...], depth_part) + dot_t(to_classes[...], sem_part)
+
+    loop(total, BLOCK, send_messages)
+    share_tiles(mail, place, lambda index: slots.at[index])
+    classes = to_depth.shape[0]
+    kind = lax.broadcasted_iota(jnp.int32, (classes, 2 * BLOCK), 0)
+
+    def compare(rows):
+        value = slots[0, :, rows] + slots[1, :, rows] + slots[2, :, rows] + slots[3, :, rows]
+        streams[:, rows] = value
+        is_class = (kind >= 1) & (kind <= CLASSES)
+        top = jnp.max(jnp.where(is_class, value, -jnp.inf), 0, keepdims=True)
+        power = jnp.where(is_class, jnp.exp(value - top), 0.0)
+        chance = power / jnp.sum(power, 0, keepdims=True)
+        label = targets[1:2, rows]
+        chance = chance - jnp.where((kind - 1).astype(F32) == label, 1.0, 0.0)
+        slope = jnp.where(kind == 0, value - targets[0:1, rows], jnp.where(is_class, chance, 0.0))
+        slopes[:, rows] = (slope * mask_line[0:1, rows]).astype(BF16)
+
+    loop(total, 2 * BLOCK, compare)
+    by_part = dot(slopes[...], gated[...])
+    by_task = dot(slopes[...], task[PITCH : PITCH + total, :])
+    row = lax.broadcasted_iota(jnp.int32, by_part.shape, 0)
+    use_task = ((row == 0) & is_first) | ((row > 0) & is_last)
+    found = jnp.where(use_task, by_task, by_part)
+    found = jnp.concatenate([found, jnp.zeros((LANES - classes, mid), F32)], 0)
+    stream_grads[...] = found.T.astype(BF16)
+
+    def grads(rows):
+        grad = t_dot(slopes[:, rows], from_gated[...])
+        open_part = opened[rows, :]
+        grad_msg[here(rows), :] = (grad * open_part).astype(BF16)
+        grad_gate[rows, :] = (grad * messages[rows, :] * open_part * (1.0 - open_part)).astype(BF16)
+
+    loop(total, BLOCK, grads)
+    gate_grads[...] = t_dot(task[PITCH : PITCH + total, :], grad_gate[...]).astype(BF16)
+    widen(grad_msg, left, right, total)
+    shifted = (left, grad_msg, right)
+    for offset in range(9):
+        row, col = 2 - offset // 3, 2 - offset % 3
+        window = shifted[col][PITCH * row : PITCH * row + total, :]
+        message_grads[:, offset * mid : (offset + 1) * mid] = t_dot(
+            task[PITCH : PITCH + total, :], window
+        ).astype(BF16)
+    mail.close()
+
+
+CLASSES = 40
+
+
+def one_task(nb, early, shared_act, mask, mask_line, targets, sizes, norms, weights, streams_weights):
+    total = mask.shape[0]
+    padded, mid = shared_act.shape
+    lines = streams_weights[0].shape[0]
+
+    def array(*shape, kind=BF16):
+        return jax.ShapeDtypeStruct(shape, kind)
+
+    def vmem(*shape, kind=BF16):
+        return pltpu.VMEM(shape, kind)
+
+    return pl.pallas_call(
+        functools.partial(task_kernel, nb, early),
+        out_shape=(
+            array(lines, total, kind=F32),
+            array(lines, total),
+            array(total, mid, kind=F32),
+            array(8, mid, kind=F32),
+            array(padded, mid),
+            array(total, mid),
+            array(mid, mid),
+            array(mid, LANES),
+            array(mid, 9 * mid),
+        ),
+        in_specs=[VMEM] * 12,
+        out_specs=(VMEM,) * 9,
+        scratch_shapes=[
+            vmem(padded, mid),
+            vmem(padded, mid),
+            vmem(padded, mid),
+            vmem(total, mid, kind=F32),
+            vmem(total, mid, kind=F32),
+            vmem(total, mid),
+            vmem(4, lines, total, kind=F32),
+            vmem(nb, 2, mid, kind=F32),
+            DMA((2, 32)),
+        ],
+        cost_estimate=LONG,
+        compiler_params=pltpu.CompilerParams(
+            collective_id=23, has_side_effects=True, vmem_limit_bytes=60 * 2**20
+        ),
+    )(shared_act, mask, mask_line, targets, sizes, norms, *weights, *streams_weights)
+
+
+def task_back_kernel(
+    images,
+    early,
+    shared_act,
+    mask,
+    sizes,
+    norms,
+    head,
+    message_start,
+    gate,
+    from_direct,
+    slopes,
+    pre_five,
+    stats,
+    grad_msg,
+    grad_gate,
+    back,
+    head_grads,
+    sums_out,
+    left,
+    right,
+    grad_five,
+    grad,
+    slots_five,
+    sems,
+):
+    place = Place(images)
+    mail = Mail(sems)
+    total = mask.shape[0]
+    mid = pre_five.shape[1]
+    greet(place.others)
+    sums_out[...] = jnp.zeros_like(sums_out)
+    for cells in (left, right, grad_five):
+        clear_ends(cells, total)
+    widen(grad_msg, left, right, total)
+
+    def message_weight(offset):
+        return message_start[offset] if offset < early else head[9 + offset - early]
+
+    def task_grads(rows):
+        found = conv_rows(
+            (left, grad_msg, right), rows, lambda offset, window: dot_t(window, message_weight(offset)), True
+        )
+        found = found + dot_t(grad_gate[rows, :], gate[...])
+        grad[rows, :] = found + t_dot(slopes[:, rows], from_direct[...])
+
+    loop(total, BLOCK, task_grads)
+    sums = norm_back(stats, norms, mask, grad, pre_five, 0, mid, lambda rows: grad[rows, :])
+    for copy in send_sums(mail, place, slots_five, sums):
+        copy.wait_recv()
+    bias_sum, gain_sum = add_up(slots_five)
+    sums_out[0:1, :] = gain_sum
+    sums_out[1:2, :] = bias_sum
+
+    def put(rows, value):
+        grad_five[pl.ds(pl.multiple_of(PITCH + rows.start, 16), CHUNK), :] = value
+
+    through(stats, norms, mask, sizes, grad, pre_five, 0, mid, bias_sum, gain_sum, put)
+    widen(grad_five, left, right, total)
+    shifted = (left, grad_five, right)
+
+    def head_back(rows):
+        back[rows, :] = conv_rows(
+            shifted, rows, lambda offset, window: dot_t(window, head[offset]), True
+        ).astype(BF16)
+
+    loop(total, BLOCK, head_back)
+    for offset in range(9):
+        row, col = 2 - offset // 3, 2 - offset % 3
+        window = shifted[col][PITCH * row : PITCH * row + total, :]
+        head_grads[:, offset * mid : (offset + 1) * mid] = t_dot(
+            shared_act[PITCH : PITCH + total, :], window
+        ).astype(BF16)
+    mail.close()
+
+
+def one_task_back(nb, early, shared_act, mask, sizes, norms, weights, from_direct, slopes, rest):
+    total = mask.shape[0]
+    padded, mid = shared_act.shape
+
+    def array(*shape, kind=BF16):
+        return jax.ShapeDtypeStruct(shape, kind)
+
+    def vmem(*shape, kind=BF16):
+        return pltpu.VMEM(shape, kind)
+
+    return pl.pallas_call(
+        functools.partial(task_back_kernel, nb, early),
+        out_shape=(array(total, mid), array(mid, 9 * mid), array(8, mid, kind=F32)),
+        in_specs=[VMEM] * 13,
+        out_specs=(VMEM,) * 3,
+        scratch_shapes=[
+            vmem(padded, mid),
+            vmem(padded, mid),
+            vmem(padded, mid),
+            vmem(total, mid, kind=F32),
+            vmem(nb, 2, mid, kind=F32),
+            DMA((2, 16)),
+        ],
+        cost_estimate=LONG,
+        compiler_params=pltpu.CompilerParams(
+            collective_id=24, has_side_effects=True, vmem_limit_bytes=60 * 2**20
+        ),
+    )(shared_act, mask, sizes, norms, *weights, from_direct, slopes, *rest)
+
+
+def last_kernel(shares, sums, all_shares, all_sums, sems):
+    place = Place(2)
+    mail = Mail(sems)
+    blk = place.blk
+    greet([place.mate, place.across])
+    here = [mail.local(shares, all_shares.at[blk]), mail.local(sums, all_sums.at[blk])]
+    both = []
+    for source, slots in ((sums, all_sums), (shares, all_shares)):
+        far = mail.send(source, slots.at[blk], place.across)
+        near = mail.send(source, slots.at[blk], place.mate)
+        both.append((far, near, slots))
+    for far, near, slots in both:
+        far.wait_recv()
+        passed = slots.at[blk ^ 2]
+        last = mail.send(passed, passed, place.mate)
+        near.wait_recv()
+        last.wait_recv()
+    for copy in here:
+        copy.wait()
+    mail.close()
+
+
+def gather_last(shares, sums):
+    return pl.pallas_call(
+        last_kernel,
+        out_shape=(
+            jax.ShapeDtypeStruct((4,) + shares.shape, shares.dtype),
+            jax.ShapeDtypeStruct((4,) + sums.shape, sums.dtype),
+        ),
+        in_specs=[ANY] * 2,
+        out_specs=(ANY, ANY),
+        scratch_shapes=[DMA((2, 16))],
+        compiler_params=pltpu.CompilerParams(collective_id=25, has_side_effects=True),
+    )(shares, sums)
+
+
 def on_device(
     nt,
     nb,
@@ -1656,8 +1997,10 @@
     shared_own = lax.ppermute(
         lax.dynamic_slice_in_dim(shared_weight, blk * piece, piece, 0), ("blk", "batch"), order
     )
-    full_first, smalls, wide_features, spatial, pre_one, stats = begin(
-        nb, first_weight, small, spatial_weight, feat, inside_wide, sizes, tile_sizes
+    pair = jnp.stack([depth_target[0], labels[0].astype(F32)])
+    pair = jnp.pad(pair, ((0, 6), (0, 0), (0, PITCH - cols))).reshape(8, tile_rows * PITCH)
+    full_first, smalls, targets, wide_features, spatial, pre_one, stats = begin(
+        nb, first_weight, small, spatial_weight, pair, feat, inside_wide, sizes, tile_sizes
     )
     full_first = full_first.reshape(width, mid)
     smalls = smalls.reshape(nb, room)
@@ -1700,14 +2043,16 @@
             filled(bias_four),
         ]
     )
-    head_own, stats = lax.optimization_barrier(
-        (lax.dynamic_index_in_dim(head_weights, blk, 0, False), stats)
-    )
-    head = lax.all_gather(head_own, "batch", axis=1, tiled=True)
     early = 5
-    message_rest = lax.dynamic_index_in_dim(message_weights, blk, 0, False)[early:]
-    head, message_rest = lax.optimization_barrier((head, message_rest))
-    message_rest = lax.all_gather(message_rest, "batch", axis=1, tiled=True)
+    large = jnp.concatenate(
+        [
+            lax.dynamic_index_in_dim(head_weights, blk, 0, False),
+            lax.dynamic_index_in_dim(message_weights, blk, 0, False)[early:],
+        ],
+        0,
+    )
+    large, stats = lax.optimization_barrier((large, stats))
+    large = lax.all_gather(large, "batch", axis=1, tiled=True)
     (
         last,
         shared,
@@ -1736,85 +2081,68 @@
         gate_weights,
         message_weights,
     )
-    message = jnp.concatenate([message_start, message_rest], 0)
-
-    def narrow(cells):
-        channels = cells.shape[1]
-        return cells.reshape(-1, PITCH, channels)[:, :cols].reshape(-1, channels)
-
-    def act(values, mask):
-        return (jax.nn.silu(values) * mask).astype(BF16)
-
-    shared_map = narrow(shared_act)
-    gain_task = lax.dynamic_index_in_dim(gain_mid, 3 + blk, 0, False)
-    bias_task = lax.dynamic_index_in_dim(bias_mid, 3 + blk, 0, False)
-    pre_five = dot(windows(shared_map, rows, cols, False), head.reshape(9 * mid, mid))
-    mean = jnp.sum(pre_five * inside, 0) / image_size
-    gap = pre_five - mean
-    spread = jnp.sum(gap * gap * inside, 0)
-    few = sizes[:, :, :LANES]
-    centre, spread = all_sums(mean, spread, None, few, True, False, 5)
-    inverse_five = lax.rsqrt(spread / valid_count + EPSILON)
-    normed_five = (pre_five - centre) * inverse_five
-    norm_five = normed_five * gain_task + bias_task
-    task_act = act(norm_five, inside)
-    messages = dot(windows(task_act, rows, cols, False), message.reshape(9 * mid, mid))
-    gate_open = jax.nn.sigmoid(dot(task_act, gate))
-    gated = (gate_open * messages).astype(BF16)
+
+    task_norms = jnp.stack(
+        [
+            lax.dynamic_index_in_dim(gain_mid, 3 + blk, 0, False),
+            lax.dynamic_index_in_dim(bias_mid, 3 + blk, 0, False),
+        ]
+    )
+    task_norms = jnp.pad(task_norms, ((0, 6), (0, 0)))
+    lines = -(-(1 + classes) // 16) * 16
+    stream_weight = jnp.concatenate([full_depth, full_classes], 1).T
+    stream_weight = jnp.pad(stream_weight, ((0, lines - 1 - classes), (0, 0)))
+    is_depth = jnp.arange(lines)[:, None] == 0
+    none = jnp.zeros((), BF16)
     is_first, is_last = blk == 0, blk == tasks - 1
-    depth_part = jnp.where(is_first, task_act, gated)
-    sem_part = jnp.where(is_last, task_act, gated)
-    depth_share = jnp.einsum("pc,co->op", depth_part, full_depth, preferred_element_type=F32)
-    class_share = jnp.einsum("pc,co->op", sem_part, full_classes, preferred_element_type=F32)
-    lift = -(-(1 + classes) // 8) * 8 - 1 - classes
-    shares = jnp.concatenate([depth_share, class_share, jnp.zeros((lift, pixels), F32)], 0)
-    streams = jnp.sum(gather_tiles(shares, 7), 0).T
-    depth_out = lax.dynamic_slice_in_dim(streams, blk * tile, tile, 0)[:, 0]
-    logits = lax.dynamic_slice_in_dim(streams, blk * tile, tile, 0)[:, 1 : 1 + classes]
-    targets = gather_tiles_pair(depth_target, labels, tile).reshape(pixels, 8)
-    all_depth, all_logits = streams[:, :1], streams[:, 1 : 1 + classes]
-    depth_slope = ((all_depth - targets[:, :1]) * inside).astype(BF16)
-    onehot = (targets[:, 1:2] == jnp.arange(classes, dtype=jnp.int32)[None, :].astype(F32)).astype(F32)
-    logit_slope = ((jax.nn.softmax(all_logits, axis=1) - onehot) * inside).astype(BF16)
-    grad_depth = t_dot(depth_part, depth_slope)
-    grad_classes = t_dot(sem_part, logit_slope)
-    depth_back = depth_slope.astype(F32) * full_depth.astype(F32).reshape(1, mid)
-    sem_back = dot_t(logit_slope, full_classes)
-    zero = jnp.zeros((), F32)
-    grad_gated = jnp.where(is_first, zero, depth_back) + jnp.where(is_last, zero, sem_back)
-    grad_direct = jnp.where(is_first, depth_back, zero) + jnp.where(is_last, sem_back, zero)
-
-    grad_msg = (grad_gated * gate_open).astype(BF16)
-    grad_gate = (grad_gated * messages * gate_open * (1.0 - gate_open)).astype(BF16)
-    msg_windows = windows(grad_msg, rows, cols, True)
-    gate_grads = t_dot(task_act, grad_gate).astype(BF16)
-    message_grads = t_dot(task_act, msg_windows).astype(BF16)
+    own_stream = jnp.where(is_depth, is_first, is_last)
+    to_depth = jnp.where(is_depth, stream_weight, none)
+    to_classes = jnp.where(is_depth, none, stream_weight)
+    from_gated = jnp.where(own_stream, none, stream_weight)
+    from_direct = jnp.where(own_stream, stream_weight, none)
+    mask_line = jnp.broadcast_to(inside_wide.reshape(1, -1), (8, rows * PITCH))
+    weights = (large, message_start, gate)
+    (
+        streams,
+        slopes,
+        pre_five,
+        task_stats,
+        grad_msg,
+        grad_gate,
+        gate_grads,
+        stream_grads,
+        message_grads,
+    ) = one_task(
+        nb,
+        early,
+        shared_act,
+        inside_wide,
+        mask_line,
+        targets,
+        sizes,
+        task_norms,
+        weights,
+        (to_depth, to_classes, from_gated),
+    )
+    own_streams = lax.dynamic_slice_in_dim(streams, blk * tile_rows * PITCH, tile_rows * PITCH, 1)
+    own_streams = own_streams.reshape(lines, tile_rows, PITCH)[:, :, :cols]
+    depth_out = own_streams[0]
+    logits = own_streams[1 : 1 + classes].transpose(1, 2, 0)
     share_messages = lax.psum_scatter(message_grads, "batch", scatter_dimension=0, tiled=True)
-    task_grad = (
-        grad_direct
-        + dot_t(grad_gate, gate)
-        + dot(msg_windows, message.swapaxes(1, 2).reshape(9 * mid, mid))
-    )
-    grad_norm_five = task_grad * inside * silu_slope(norm_five)
-    bias_sum_five, gain_sum_five = all_sums(
-        jnp.sum(grad_norm_five, 0), jnp.sum(grad_norm_five * normed_five, 0), None, few, False, False, 8
-    )
-    grad_pre_five = (
-        inverse_five
-        * gain_task
-        * (grad_norm_five - bias_sum_five / valid_count - normed_five * gain_sum_five / valid_count)
-        * inside
-    ).astype(BF16)
-    five_windows = windows(grad_pre_five, rows, cols, True)
-    head_grads = t_dot(shared_map, five_windows).astype(BF16)
+    back, head_grads, task_sums = one_task_back(
+        nb,
+        early,
+        shared_act,
+        inside_wide,
+        sizes,
+        task_norms,
+        weights,
+        from_direct,
+        slopes,
+        (pre_five, task_stats, grad_msg, grad_gate),
+    )
+
     share_heads = lax.psum_scatter(head_grads, "batch", scatter_dimension=0, tiled=True)
-    shared_back = dot(five_windows, head.swapaxes(1, 2).reshape(9 * mid, mid))
-
-    stream_grads = jnp.concatenate([grad_depth, grad_classes], 1)
-    stream_grads = jnp.pad(stream_grads, ((0, 0), (0, LANES - 1 - classes))).astype(BF16)
-    back = jnp.pad(
-        shared_back.astype(BF16).reshape(rows, cols, mid), ((0, 0), (0, PITCH - cols), (0, 0))
-    ).reshape(rows * PITCH, mid)
     (
         grad_input,
         share_shared,
@@ -1841,35 +2169,42 @@
     grad_input = grad_input.reshape(tile_rows, PITCH, width)[:, :cols]
 
     moved = lax.ppermute(
-        jnp.concatenate([share_first, share_shared], 1), ("blk", "batch"), [(b, a) for a, b in order]
+        jnp.concatenate([share_first, share_shared], 0), ("blk", "batch"), [(b, a) for a, b in order]
     )
     share_messages, share_heads, moved = lax.optimization_barrier((share_messages, share_heads, moved))
-    early_share = jnp.concatenate([share_messages, share_heads], 1)
-    early_all = lax.all_gather(early_share, "blk", axis=0, tiled=False).astype(F32)
-    early_all = early_all.reshape(nt, share, 2, 9, mid).transpose(2, 0, 3, 1, 4)
-    red_messages, red_heads = early_all[0], early_all[1]
-    late_share = jnp.concatenate([moved, share_last, share_spatial, share_gates, share_stream], 1)
-    late_all = gather_tiles(late_share, 12).astype(F32)
+    shares = jnp.concatenate(
+        [
+            moved,
+            share_last,
+            share_gates,
+            share_spatial.reshape(share, 9, slim).swapaxes(0, 1).reshape(-1, mid),
+            share_stream.reshape(-1, mid),
+            share_messages.reshape(share, 9, mid).swapaxes(0, 1).reshape(9 * share, mid),
+            share_heads.reshape(share, 9, mid).swapaxes(0, 1).reshape(9 * share, mid),
+        ],
+        0,
+    )
+    sums = jnp.pad(jnp.concatenate([sums_wide, task_sums[:2]], 0), ((0, 6), (0, 0)))
+    all_shares, sums = gather_last(shares, sums)
     at = 0
 
     def part(count):
         nonlocal at
-        found = late_all[:, :, at : at + count]
+        found = all_shares[:, at : at + count].astype(F32)
         at += count
         return found
 
-    red_first = part(mid).reshape(nt * share, mid)
-    red_shared = part(mid).reshape(nt * share, mid)
-    red_last = part(mid).transpose(1, 0, 2).reshape(share, width)
-    red_spatial = part(9 * slim).reshape(nt, share, 9, slim).transpose(2, 1, 0, 3).reshape(9, share, mid)
-    red_gates = part(mid)
-    streams_red = jnp.sum(part(LANES), 0)
+    red_first = part(share).reshape(nt * share, mid)
+    red_shared = part(share).reshape(nt * share, mid)
+    red_last = part(share).transpose(1, 0, 2).reshape(share, width)
+    red_gates = part(share)
+    red_spatial = part(9 * share * slim // mid).reshape(nt, 9, share, slim)
+    red_spatial = red_spatial.transpose(1, 2, 0, 3).reshape(9, share, mid)
+    streams_red = jnp.sum(part(share * LANES // mid).reshape(nt, share, LANES), 0)
     red_depth = streams_red[:, 0]
     red_classes = streams_red[:, 1 : 1 + classes]
-
-    sums = jnp.concatenate([sums_wide, gain_sum_five[None], bias_sum_five[None]], 0)
-    sums = jnp.pad(sums, ((0, 6), (0, 0)))
-    sums = gather_tiles(sums, 13)
+    red_messages = part(9 * share).reshape(nt, 9, share, mid)
+    red_heads = part(9 * share).reshape(nt, 9, share, mid)
     two_gain, two_bias = sums[:, 2, :slim].reshape(1, mid), sums[:, 3, :slim].reshape(1, mid)
     four_gain, four_bias = sums[:, 6, :slim].reshape(1, mid), sums[:, 7, :slim].reshape(1, mid)
     mid_gains = jnp.concatenate([sums[0, 0:1], two_gain, four_gain, sums[:, 8]], 0)

time: 691 us -> 610 us (0.88); the launches traced: 679 us -> 606 us
  Pallas kernels: 399 us -> 495 us
  local copies, waits for them, and re-layouts: 142 us -> 48.2 us
  matrix products: 75.6 us -> 0 us
    pallas_call x6 -> x3, Pallas kernels: 69 us -> 164 us  [the longest x1 63.9 us: one_task(): pl.pallas_call(functools.partial(task_kernel, nb, early), out_shape=(arra...]
    dot_general x14 -> x0, matrix products: 75.6 us -> none  [the longest x5 45.4 us: dot(): return jnp.dot(left, right, preferred_element_type=F32)]
    unnamed x135 -> x55, local copies, waits for them, and re-layouts: 53.1 us -> 10.6 us
    transpose x5 -> x3, local copies, waits for them, and re-layouts: 27.5 us -> 0.77 us  [the longest x1 0.36 us: on_device(): share_messages.reshape(share, 9, mid).swapaxes(0, 1).reshape(9 * share, mid)]
    reduce_scatter x1, waiting for transfers between devices: 0.02 us -> 24.7 us  [on_device(): lax.psum_scatter(head_grads, 'batch', scatter_dimension=0, tiled=True)]
    all_gather x3 -> x1, waiting for transfers between devices: 19.4 us -> 0.02 us  [on_device(): large = lax.all_gather(large, 'batch', axis=1, tiled=True)]
    slice x11 -> x3, local copies, waits for them, and re-layouts: 22.3 us -> 5.55 us  [the longest x1 4.23 us: part(): found = all_shares[:, at:at + count].astype(F32)]
    pallas_call x1, Pallas kernels: 124 us -> 137 us  [bottleneck(): pl.pallas_call(functools.partial(forward_kernel, nb, early), out_shape=ou...]
  transfers between devices with their start and end apart: 7 -> 5, of which waited for: 1 -> 1; matrix products, arithmetic and copies ran while one was open for 21% -> 2% of each run, Pallas kernels for 57% -> 54%
where the time goes in v3:
time: 610 us; the launch traced here: 606 us
  Pallas kernels  495 us (81%)
  local copies, waits for them, and re-layouts  48.2 us (8%)
  waiting for transfers between devices  24.8 us (4%)
  other arithmetic  21.7 us (4%)
  between operations  14.7 us (2%)
    pallas_call x1, Pallas kernels, bottleneck_back(): pl.pallas_call(functools.partial(backward_kernel, nb), out_shape=(array(t...  142 us
    pallas_call x1, Pallas kernels, bottleneck(): pl.pallas_call(functools.partial(forward_kernel, nb, early), out_shape=ou...  137 us
    pallas_call x1, Pallas kernels, one_task(): pl.pallas_call(functools.partial(task_kernel, nb, early), out_shape=(arra...  63.9 us
    pallas_call x1, Pallas kernels, begin(): pl.pallas_call(functools.partial(start_kernel, nb), out_shape=(array(nb,...  51.8 us
    pallas_call x1, Pallas kernels, gather_last(): pl.pallas_call(last_kernel, out_shape=(jax.ShapeDtypeStruct((4,) + shares...  51.1 us
    pallas_call x1, Pallas kernels, one_task_back(): pl.pallas_call(functools.partial(task_back_kernel, nb, early), out_shape=...  48.5 us
    reduce_scatter x1, waiting for transfers between devices, on_device(): lax.psum_scatter(head_grads, 'batch', scatter_dimension=0, tiled=True)  24.7 us
  transfers between devices with their start and end apart: 5, of which 1 were waited for; matrix products, arithmetic and copies ran while one was open for 2% of the time, Pallas kernels for 54%

profile of v3, /device:TPU:0, one launch (start us, length us, event | category | flops | bytes accessed | tf_op | source)
XLA Modules:
  0.0 605.7 jit_solution(13142323678266577906)
XLA Ops:
  7.2 1.3 dynamic_slice.66
  8.5 1.2 dynamic_slice.65
  9.8 0.7 multiply_convert_fusion
  10.4 0.8 reshape.240
  11.2 0.8 reshape.241
  12.0 0.8 copy.55
  12.9 2.1 concatenate.24
  15.0 0.7 convert_element_type.84
  15.6 0.7 select_maximum_fusion.1
  16.4 0.7 iota_compare_fusion.5
  17.1 0.7 iota_compare_fusion.6
  18.4 1.6 pad.39
  20.1 1.2 dynamic-slice_bitcast_fusion
  21.3 1.0 dynamic-slice_bitcast_fusion.1
  22.3 1.0 pad_maximum_fusion
  23.4 0.9 copy-done.5
  24.4 51.8 %shard_map.297 = (bf16[8,256,512]{2,1,0:T(8,128)(2,1)S(1)}, bf16[8,32,128]{2,1,0:T(8,128)(2,1)S(1)}, f32[8,1536]{1,0:T(8,128)S(1)}, bf16[1536,512]{1,0:T(8,128)(...) custom-call(bf16[256,512]{1,0:T(8,128)(2,1)S(1)} %copy-done.5, ...), custom_call_target="tpu_custom_call" | custom-call | flops 80000000000 | bytes 30000000 | tf_op jit(solution)/shard_map/pallas_call | solution.py:969
  76.2 1.3 copy-done.6
  77.5 1.1 copy-done.7
  78.6 1.0 copy-done.8
  79.7 0.9 copy-done.9
  80.6 0.6 copy-done.11
  81.3 0.7 collective-permute-start
  83.6 0.6 stack.45.norms
  84.3 0.7 broadcast_select_fusion
  85.1 0.6 select_maximum_fusion.2.norms
  85.7 0.6 copy-done.19
  86.3 137.1 %shard_map.298 = (bf16[512,512]{1,0:T(8,128)(2,1)}, bf16[512,512]{1,0:T(8,128)(2,1)}, bf16[512,512]{1,0:T(8,128)(2,1)}, bf16[5,512,512]{2,1,0:T(8,128)(2,1)}, bf...) custom-call(f32[384,512]{1,0:T(8,128)} %copy-done.9, ...), custom_call_target="tpu_custom_call" | custom-call | flops 80000000000 | bytes 30000000 | tf_op jit(solution)/shard_map/pallas_call | solution.py:1182
  223.5 0.6 broadcast_in_dim.62.mask_line
  224.1 63.9 %shard_map.299 = (f32[48,1536]{1,0:T(8,128)}, bf16[48,1536]{1,0:T(8,128)(2,1)}, f32[1536,512]{1,0:T(8,128)}, f32[8,512]{1,0:T(8,128)}, bf16[1632,512]{1,0:T(8,12...) custom-call(bf16[1632,512]{1,0:T(8,128)(2,1)} %get-tuple-element.68., ...), custom_call_target="tpu_custom_call" | custom-call | flops 80000000000 | bytes 30000000 | tf_op jit(solution)/shard_map/pallas_call | solution.py:1754
  288.1 48.5 %shard_map.300 = (bf16[1536,512]{1,0:T(8,128)(2,1)}, bf16[512,4608]{1,0:T(8,128)(2,1)}, f32[8,512]{1,0:T(8,128)}) custom-call(bf16[1632,512]{1,0:T(8,128)(2,1)} %get-tuple-element.68.shared_act, f32[1536,1]{1,0:T(8,128)} %copy-done.2, f32[8,1,512]{2,1,0:T(1,128)} %copy-done.3, f32[8,512]{1,0:T(8,128)} %select_maximum_fusion.2.norms, ...), custom_call_target="tpu_custom_call" | custom-call | flops 80000000000 | bytes 30000000 | tf_op jit(solution)/shard_map/pallas_call | solution.py:1873
  336.6 0.9 constant_dynamic-slice_fusion
  337.7 142.4 %shard_map.301 = (f32[384,2048]{1,0:T(8,128)}, bf16[64,512]{1,0:T(8,128)(2,1)}, bf16[64,512]{1,0:T(8,128)(2,1)}, bf16[64,1152]{1,0:T(8,128)(2,1)}, bf16[64,512]{...) custom-call(bf16[1536,512]{1,0:T(8,128)(2,1)} %get-tuple-element.79.back, ...), custom_call_target="tpu_custom_call" | custom-call | flops 80000000000 | bytes 30000000 | tf_op jit(solution)/shard_map/pallas_call | solution.py:1562
  480.1 0.9 pad_maximum_fusion.1
  481.0 0.7 collective-permute-start.1
  481.7 3.6 slice_bitcast_fusion
  485.9 0.8 copy.69
  487.0 0.7 slice.166
  487.7 0.6 select_maximum_fusion.sums
  488.3 24.7 %reduce-scatter.5.cloned.1.call-done = bf16[64,4608]{1,0:T(8,128)(2,1)} async-done(((bf16[512,4608]{1,0:T(8,128)(2,1)}), bf16[64,4608]{1,0:T(8,128)(2,1)}) %reduce-scatter.5.cloned.1.call-update) | async-done | bytes 589840 | tf_op jit(solution)/shard_map/reduce_scatter | solution.py:2145
  513.0 1.4 reshape.261
  514.8 1.4 reshape.263
  517.3 1.1 copy-done.13
  518.4 51.1 %shard_map.302 = (bf16[4,1568,512]{2,1,0:T(8,128)(2,1)}, f32[4,16,512]{2,1,0:T(8,128)}) custom-call(bf16[1568,512]{1,0:T(8,128)(2,1)} %copy-done.13, f32[16,512]{1,0:T(8,128)} %select_maximum_fusion.sums), custom_call_target="tpu_custom_call" | custom-call | tf_op jit(solution)/shard_map/pallas_call | solution.py:1916
  569.5 2.2 slice_convert_fusion.1
  571.7 2.2 slice_convert_fusion
  573.9 4.2 fusion.11
  578.2 0.9 convert_reduce_fusion
  579.0 0.6 slice_reduce_fusion
  579.7 0.8 slice_bitcast_fusion.6
  580.5 0.9 slice_bitcast_fusion.4
  581.5 1.0 fusion.12
  582.4 0.9 bitcast_convert_fusion.1
  583.3 2.3 reshape.299
  585.6 2.4 copy_bitcast_fusion
  588.0 0.8 copy.74
  588.9 0.9 bitcast_convert_fusion
  589.8 2.8 convert.20
  592.6 2.9 convert.21
  595.4 0.7 copy.70
  596.1 0.6 dynamic_slice.85
  596.8 0.6 dynamic_slice.86
  597.4 0.7 fusion.5
  598.1 0.7 fusion.2
  (110 shorter events, 5.4 us)
Async XLA Ops:
  7.2 74.1 %copy-start = (bf16[256,512]{1,0:T(8,128)(2,1)S(1)}, bf16[256,512]{1,0:T(8,128)(2,1)}, u32[]{:S(2)}) copy-start(bf16[256,512]{1,0:T(8,128)(2,1)} %param.26) | copy-start | bytes 786436
  7.2 216.3 %all-gather.2.cloned.1.call-start = ((), (), s32[]{:S(2)}) async-start(), calls=%async_computation.2 | async-start | bytes 7667712 | tf_op jit(solution)/shard_map/all_gather | solution.py:2055
  18.2 5.2 copy-start.2
  20.1 3.3 copy-start.4
  23.3 52.9 %copy-start.3 = (f32[8,1,512]{2,1,0:T(1,128)}, f32[8,1,512]{2,1,0:T(1,128)S(1)}, u32[]{:S(2)}) copy-start(f32[8,1,512]{2,1,0:T(1,128)S(1)} %broadcast_in_dim.60.sizes) | copy-start | bytes 49156
  23.4 1.0 copy-start.5
  76.2 1.3 copy-start.6
  77.5 1.1 copy-start.7
  78.6 1.0 copy-start.8
  79.7 0.9 copy-start.9
  80.6 0.6 copy-start.11
  81.2 142.3 %copy-start.10 = (f32[8,1536]{1,0:T(8,128)}, f32[8,1536]{1,0:T(8,128)S(1)}, u32[]{:S(2)}) copy-start(f32[8,1536]{1,0:T(8,128)S(1)} %get-tuple-element.69.targets) | copy-start | bytes 147460
  81.2 407.1 %reduce-scatter.3.cloned.1.call-start = ((), (), s32[]{:S(2)}) async-start(), calls=%async_computation.3 | async-start | bytes 5308416 | tf_op jit(solution)/shard_map/reduce_scatter | solution.py:2131
  81.3 4.4 collective-permute-start
  85.7 0.6 copy-start.19
  288.0 225.0 %reduce-scatter.5.cloned.1.call-start = ((), (), s32[]{:S(2)}) async-start(), calls=%async_computation.4 | async-start | bytes 5308416 | tf_op jit(solution)/shard_map/reduce_scatter | solution.py:2145
  481.0 7.3 %collective-permute-start.1 = (bf16[128,512]{1,0:T(8,128)(2,1)S(1)}, bf16[128,512]{1,0:T(8,128)(2,1)S(1)}, u32[]{:S(2)}, u32[]{:S(2)}) collective-permute-start(bf16[128,512]{1,0:T(8,128)(2,1)S(1)} %pad_maximum_fusion.1), channel_id=1, source_target_pairs={{0,0},{4,1},{8,2},{12,3},{16,4},{20,5},{24,6},{28,7},{1,8},{5,9},{... | collective-permute-start | bytes 393224 | tf_op jit(solution)/shard_map/ppermute | solution.py:2171
  481.7 5.0 copy-start.14
  485.3 1.7 copy-start.18
  485.3 2.4 copy-start.17
  514.8 2.3 copy-start.15
  516.2 0.8 copy-start.16
  517.2 1.2 copy-start.13
  589.8 2.8 copy-start.12
  592.6 6.2 %copy-start.1 = (bf16[256,512]{1,0:T(8,128)(2,1)S(1)}, bf16[256,512]{1,0:T(8,128)(2,1)}, u32[]{:S(2)}) copy-start(bf16[256,512]{1,0:T(8,128)(2,1)} %param.26) | copy-start | bytes 786436
Sparse Core Ops, SparseCore 0:
  81.3 141.7 all-gather.1
  288.1 108.0 reduce-scatter.2
  399.9 113.0 reduce-scatter.4

commit v4 on v3

--- a/solution.py
+++ b/solution.py
@@ -640,10 +640,11 @@
     def __init__(self, sems):
         self.sems, self.used, self.open = sems, 0, []
 
-    def send(self, src, dst, peer):
+    def send(self, src, dst, peer, keep=True):
         copy = send(src, dst, self.sems.at[0, self.used], self.sems.at[1, self.used], peer)
         self.used += 1
-        self.open.append(copy.wait_send)
+        if keep:
+            self.open.append(copy.wait_send)
         return copy
 
     def local(self, src, dst):
@@ -697,13 +698,14 @@
 
 def share_tiles(mail, place, slot):
     own = slot(place.blk)
-    far = mail.send(own, own, place.across)
-    near = mail.send(own, own, place.mate)
+    far = mail.send(own, own, place.across, False)
+    near = mail.send(own, own, place.mate, False)
     far.wait_recv()
     passed = slot(place.blk ^ 2)
-    last = mail.send(passed, passed, place.mate)
-    near.wait_recv()
-    last.wait_recv()
+    last = mail.send(passed, passed, place.mate, False)
+    near.wait()
+    last.wait()
+    far.wait_send()
 
 
 def loop(total, step, body):
@@ -751,9 +753,11 @@
     return total[0:1, :], total[1:2, :]
 
 
-def swap_sums(mail, place, slots):
+def swap_sums(mail, place, slots, meanwhile=None):
     own = slots.at[place.batch]
     copies = [mail.send(own, own, peer) for peer in place.others]
+    if meanwhile is not None:
+        meanwhile()
     for copy in copies:
         copy.wait_recv()
 
@@ -786,11 +790,11 @@
     return pl.ds(pl.multiple_of(base + rows.start, CHUNK), rows.size)
 
 
-def batch_norm_stats(mail, place, pre, mask, slots, sizes, stats, row, channels):
+def batch_norm_stats(mail, place, pre, mask, slots, sizes, stats, row, channels, meanwhile=None):
     total = pre.shape[0]
     mean, spread = local_stats(pre, mask, None, total, channels, sizes[place.batch, :, :channels])
     slots[place.batch] = jnp.concatenate([mean, spread], 0)
-    swap_sums(mail, place, slots)
+    swap_sums(mail, place, slots, meanwhile)
     keep_stats(slots, sizes, stats, row, channels)
 
 
@@ -832,7 +836,7 @@
     return total
 
 
-def sum_over_tiles(mail, place, part, near_in, pair, far_in, total, out):
+def sum_over_tiles(mail, place, part, near_in, pair, far_in, total, out, meanwhile=None):
     far_first = mail.send(part(place.blk ^ 3), near_in.at[0], place.mate)
     near_next = mail.send(part(place.blk ^ 1), near_in.at[1], place.mate)
     far_first.wait_recv()
@@ -843,6 +847,8 @@
 
     loop(total, CHUNK, pairs)
     far = mail.send(pair, far_in, place.across)
+    if meanwhile is not None:
+        meanwhile()
     near_next.wait_recv()
     far.wait_recv()
 
@@ -947,9 +953,8 @@
     swap_tile_sums(mail, place, slots_tile)
     mean, spread, _ = merge(slots_tile, tile_sizes, mid)
     slots_one[batch] = jnp.concatenate([mean, spread], 0)
-    swap_sums(mail, place, slots_one)
+    swap_sums(mail, place, slots_one, got_spatial.forward)
     keep_stats(slots_one, sizes, stats, 0, mid)
-    got_spatial.forward()
     got_spatial.finish()
     for copy in late:
         copy.wait_recv()
@@ -1087,9 +1092,13 @@
         )
 
     loop(total, BLOCK, conv_two)
-    batch_norm_stats(mail, place, pre_two, mask, slots_two, sizes, stats, 2, slim)
-    got_gate.start()
-    got_message[0].start()
+
+    def after_two():
+        got_gate.start()
+        got_message[0].start()
+        got_message[1].start()
+
+    batch_norm_stats(mail, place, pre_two, mask, slots_two, sizes, stats, 2, slim, after_two)
 
     def act_second(rows):
         value = (pre_two[rows, :] - stats[2:3, :slim]) * stats[3:4, :slim]
@@ -1106,10 +1115,14 @@
         pre_three[rows, :] = dot(act_two[rows, :], last[...])
 
     loop(total, BLOCK, expand)
-    batch_norm_stats(mail, place, pre_three, mask, slots_three, sizes, stats, 4, mid)
-    got_message[0].forward()
-    got_message[1].start()
-    got_message[2].start()
+
+    def after_three():
+        got_message[0].forward()
+        got_message[1].forward()
+        got_message[2].start()
+        got_message[3].start()
+
+    batch_norm_stats(mail, place, pre_three, mask, slots_three, sizes, stats, 4, mid, after_three)
     got_shared.finish()
 
     def act_third(rows):
@@ -1133,11 +1146,14 @@
         total,
         pre_four,
     )
-    got_message[1].forward()
-    batch_norm_stats(mail, place, pre_four, mask, slots_four, sizes, stats, 6, slim)
-    got_message[2].forward()
-    for later in got_message[3:]:
-        later.start()
+
+    def after_four():
+        got_message[2].forward()
+        got_message[3].forward()
+        for later in got_message[4:]:
+            later.start()
+
+    batch_norm_stats(mail, place, pre_four, mask, slots_four, sizes, stats, 6, slim, after_four)
 
     def act_fourth(rows):
         value = (pre_four[rows, :] - stats[6:7, :slim]) * stats[7:8, :slim]
@@ -1148,7 +1164,7 @@
     share_tiles(
         mail, place, lambda index: shared_act.at[pl.ds(PITCH, total), slim_lanes(index)]
     )
-    for later in got_message[3:]:
+    for later in got_message[4:]:
         later.forward()
     got_gate.finish()
     for one in got_message:
@@ -1203,6 +1219,29 @@
     )(pre_one, stats, spatial, wide, mask, norms, sizes, last, shared, gate, message)
 
 
+class Tiles:
+    def __init__(self, mail, place, slot, own=None):
+        self.mail, self.place, self.slot, self.own = mail, place, slot, own
+
+    def start(self):
+        own, here = self.own, self.slot(self.place.blk)
+        if own is None:
+            own = here
+        else:
+            self.mail.open.append(self.mail.local(own, here).wait)
+        self.far = self.mail.send(own, here, self.place.across)
+        self.near = self.mail.send(own, here, self.place.mate)
+
+    def forward(self):
+        self.far.wait_recv()
+        passed = self.slot(self.place.blk ^ 2)
+        self.last = self.mail.send(passed, passed, self.place.mate)
+
+    def end(self):
+        self.near.wait_recv()
+        self.last.wait_recv()
+
+
 class Reduce:
     def __init__(self, mail, place, grad, from_side, summed, from_line, out):
         self.mail, self.place = mail, place
@@ -1214,14 +1253,22 @@
     def start(self):
         self.from_x = self.mail.send(self.grad.at[:, 1 - self.side], self.from_side, self.place.side)
 
-    def middle(self):
-        place = self.place
+    def own_half(self, at):
+        return self.grad[at, self.side]
+
+    def add_side(self):
         self.from_x.wait_recv()
         lines = self.from_side.shape[0]
         for at in range(lines):
-            self.summed[at] = (
-                self.grad[at, self.side].astype(F32) + self.from_side[at].astype(F32)
-            ).astype(BF16)
+            self.summed[at] = (self.own_half(at).astype(F32) + self.from_side[at].astype(F32)).astype(BF16)
+
+    def middle(self):
+        self.add_side()
+        self.send_lines()
+
+    def send_lines(self):
+        place = self.place
+        lines = self.summed.shape[0]
         self.copies = [
             self.mail.send(
                 self.summed.at[self.line ^ mask],
@@ -1237,6 +1284,122 @@
             copy.wait_recv()
             total = total + self.from_line[at].astype(F32)
         self.out[...] = total.astype(BF16)
+
+
+class ReduceFar(Reduce):
+    def start(self):
+        super().start()
+        self.fetch = self.mail.local(self.grad.at[:, self.side], self.summed)
+
+    def own_half(self, at):
+        if at == 0:
+            self.fetch.wait()
+        return self.summed[at]
+
+
+class Owners:
+    def __init__(self, mail, place, result, slots):
+        self.mail, self.place, self.result, self.slots = mail, place, result, slots
+        self.base = mail.used
+        mail.used += 5
+        self.owner = 2 * place.blk + lax.div(place.batch, 4)
+        self.quarter = lax.rem(place.batch, 4)
+        self.at_home = self.owner == place.batch
+
+    def copy(self, mask):
+        place, mail = self.place, self.mail
+        return pltpu.make_async_remote_copy(
+            src_ref=self.result,
+            dst_ref=self.slots.at[self.quarter],
+            send_sem=mail.sems.at[0, self.base + mask],
+            recv_sem=mail.sems.at[1, self.base + self.quarter],
+            device_id=(place.blk ^ mask, self.owner),
+            device_id_type=MESH,
+        )
+
+    def local(self):
+        return pltpu.make_async_copy(
+            self.result, self.slots.at[self.quarter], self.mail.sems.at[0, self.base + 4]
+        )
+
+    def start(self):
+        for mask in range(1, 4):
+            self.copy(mask).start()
+
+        @pl.when(self.at_home)
+        def _():
+            self.local().start()
+
+        @pl.when(jnp.logical_not(self.at_home))
+        def _():
+            self.copy(0).start()
+
+    def forward(self):
+        for mask in range(1, 4):
+            self.copy(mask).wait_send()
+
+        @pl.when(self.at_home)
+        def _():
+            self.local().wait()
+
+        @pl.when(jnp.logical_not(self.at_home))
+        def _():
+            self.copy(0).wait_send()
+
+    def end(self):
+        place, mail = self.place, self.mail
+        for quarter in range(4):
+            source = 4 * lax.rem(place.batch, 2) + quarter
+            at_home = (lax.div(place.batch, 2) == place.blk) & (source == place.batch)
+
+            @pl.when(jnp.logical_not(at_home))
+            def _():
+                pltpu.make_async_remote_copy(
+                    src_ref=self.result,
+                    dst_ref=self.slots.at[quarter],
+                    send_sem=mail.sems.at[0, self.base],
+                    recv_sem=mail.sems.at[1, self.base + quarter],
+                    device_id=place.mate,
+                    device_id_type=MESH,
+                ).wait_recv()
+
+
+def greet_owners(place):
+    barrier = pltpu.get_barrier_semaphore()
+    regular = [place.mate, place.across]
+    for peer in regular:
+        pl.semaphore_signal(barrier, inc=1, device_id=peer, device_id_type=MESH)
+    for quarter in range(4):
+        source = (lax.div(place.batch, 2), 4 * lax.rem(place.batch, 2) + quarter)
+        at_home = (source[0] == place.blk) & (source[1] == place.batch)
+
+        @pl.when(jnp.logical_not(at_home))
+        def _():
+            pl.semaphore_signal(barrier, inc=1, device_id=source, device_id_type=MESH)
+
+    owner = 2 * place.blk + lax.div(place.batch, 4)
+
+    @pl.when(owner == place.batch)
+    def _():
+        pl.semaphore_wait(barrier, len(regular) + 3)
+
+    @pl.when(owner != place.batch)
+    def _():
+        pl.semaphore_wait(barrier, len(regular) + 4)
+
+
+class Job:
+    def __init__(self, reduce, tiles):
+        self.steps = []
+        if reduce is not None:
+            self.steps += [reduce.start, reduce.middle, reduce.finish]
+        if tiles is not None:
+            self.steps += [tiles.start, tiles.forward, tiles.end]
+
+
+def step(*jobs):
+    for job in jobs:
+        job.steps.pop(0)()
 
 
 def reduce_scratch(lines, share, columns, own):
@@ -1308,14 +1471,19 @@
     first,
     gate_grads,
     stream_grads,
+    message_share,
+    head_grads,
+    task_sums,
     grad_input,
     share_shared,
-    share_last,
-    share_spatial,
     share_first,
-    share_gates,
-    share_stream,
-    sums_out,
+    all_last,
+    all_spatial,
+    all_gates,
+    all_stream,
+    all_heads,
+    all_messages,
+    all_sums,
     near_four,
     pair_four,
     far_four,
@@ -1355,11 +1523,37 @@
     slim = pre_two.shape[1]
     base = blk * tile
     red_shared = Reduce(mail, place, *rest[0:4], share_shared)
-    red_last = Reduce(mail, place, *rest[4:8], share_last)
+    red_last = Reduce(mail, place, *rest[4:8], all_last.at[blk])
     red_first = Reduce(mail, place, *rest[8:12], share_first)
-    red_spatial = Reduce(mail, place, *rest[12:16], share_spatial)
-    red_gates = Reduce(mail, place, gate_grads, *rest[16:19], share_gates)
-    red_stream = Reduce(mail, place, stream_grads, *rest[19:22], share_stream)
+    red_spatial = Reduce(mail, place, *rest[12:16], all_spatial.at[blk])
+    red_gates = Reduce(mail, place, gate_grads, *rest[16:19], all_gates.at[blk])
+    red_stream = Reduce(mail, place, stream_grads, *rest[19:22], all_stream.at[blk])
+    share = share_shared.shape[0]
+    results, sums_out, at = rest[22], rest[23], 24
+    heads, messages = [], []
+
+    def tiles_of(slots, first_row, count, own):
+        rows_at = pl.ds(first_row, count)
+        return Tiles(mail, place, lambda index: slots.at[index, rows_at], own)
+
+    def slots_of(slots):
+        return Tiles(mail, place, lambda index: slots.at[index])
+
+    for offset in range(9):
+        result = results.at[offset]
+        reduce = ReduceFar(mail, place, head_grads.at[offset], *rest[at : at + 3], result)
+        at += 3
+        heads.append(Job(reduce, tiles_of(all_heads, offset * share, share, result)))
+    early = message_share.shape[0] // share
+    ends = [0, early // 3, 2 * early // 3, early]
+    for begin_at, end_at in zip(ends[:-1], ends[1:]):
+        count = (end_at - begin_at) * share
+        own = message_share.at[pl.ds(begin_at * share, count)]
+        messages.append(Job(None, tiles_of(all_messages, begin_at * share, count, own)))
+    job_shared, job_first = Job(red_shared, None), Job(red_first, None)
+    job_sums = Job(None, Tiles(mail, place, lambda index: all_sums.at[index], sums_out))
+    job_last, job_spatial = Job(red_last, slots_of(all_last)), Job(red_spatial, slots_of(all_spatial))
+    job_gates, job_stream = Job(red_gates, slots_of(all_gates)), Job(red_stream, slots_of(all_stream))
     greet(place.others + place.tiles)
 
     def slim_lanes(index):
@@ -1373,16 +1567,18 @@
         sums_out[row + 1 : row + 2, :channels] = bias_sum
 
     sums_out[...] = jnp.zeros_like(sums_out)
+    sums_out[8:10, :] = task_sums[0:2, :]
     for cells in (two_left, two_here, two_right):
         clear_ends(cells, total)
-    red_gates.start()
-    red_stream.start()
+    step(heads[0], heads[1], job_gates, job_stream)
 
     sum_over_tiles(
         mail, place, lambda index: back.at[:, slim_lanes(index)], near_four, pair_four, far_four, total, grad_four
     )
     sums = norm_back(stats, norms, mask, grad_four, pre_four, 6, slim, lambda rows: grad_four[rows, :])
     copies = send_sums(mail, place, slots_four, sums)
+    step(heads[0], heads[1], job_gates, job_stream)
+    step(heads[2], heads[3], heads[4])
     for offset in range(9):
         turned[offset * slim : (offset + 1) * slim, :] = spatial[offset].T
     for copy in copies:
@@ -1395,17 +1591,21 @@
         all_four[rows, lanes] = value
 
     through(stats, norms, mask, sizes, grad_four, pre_four, 6, slim, bias_sum, gain_sum, put_four)
-    red_gates.middle()
-    red_stream.middle()
     share_tiles(mail, place, lambda index: all_four.at[:, slim_lanes(index)])
+    step(messages[0])
 
     def joined_back(rows):
         return dot_t(all_four[rows, :], shared[...])
 
     sums = norm_back(stats, norms, mask, grad_three, pre_three, 4, mid, joined_back, None, wide)
     copies = send_sums(mail, place, slots_three, sums)
+    step(heads[2], heads[3], heads[4])
+    step(heads[5], heads[6])
+    step(heads[0], heads[1], job_gates, job_stream)
+    step(messages[0])
     grads, lines = red_shared.grad, red_shared.grad.shape[0]
     grads[...] = t_dot(act_three[...], all_four[...]).astype(BF16).reshape(grads.shape)
+    step(job_shared)
 
     def lower(rows):
         low_joined[rows, :] = grad_three[rows, :].astype(BF16)
@@ -1420,10 +1620,6 @@
         low_three[rows, :] = value
 
     through(stats, norms, mask, sizes, grad_three, pre_three, 4, mid, bias_sum, gain_sum, put_three)
-    red_gates.finish()
-    red_stream.finish()
-    mail.close()
-    red_shared.start()
 
     def two_part(rows):
         all_four[rows, :] = dot_t(low_three[rows, :], last[...]).astype(BF16)
@@ -1432,6 +1628,7 @@
     sum_over_tiles(
         mail, place, lambda index: all_four.at[:, slim_lanes(index)], near_two, pair_two, far_two, total, grad_two
     )
+    step(messages[1])
     landing = joined_rows.at[:, pl.ds(pl.multiple_of(blk * mid, mid), mid)]
     joined_here = mail.local(low_joined.at[tile_rows(blk)], landing)
     joined_copies = [
@@ -1440,8 +1637,12 @@
     ]
     sums = norm_back(stats, norms, mask, grad_two, pre_two, 2, slim, lambda rows: grad_two[rows, :])
     copies = send_sums(mail, place, slots_two, sums)
+    step(heads[5], heads[6], job_shared)
+    step(heads[7], heads[8])
+    step(heads[2], heads[3], heads[4])
     grads = red_last.grad
     grads[...] = t_dot(act_two[...], low_three[...]).astype(BF16).reshape(grads.shape)
+    step(job_last)
     for copy in copies:
         copy.wait_recv()
     bias_sum, gain_sum = add_up(slots_two)
@@ -1452,8 +1653,6 @@
 
     through(stats, norms, mask, sizes, grad_two, pre_two, 2, slim, bias_sum, gain_sum, put_two)
     widen(two_here, two_left, two_right, total)
-    red_shared.middle()
-    red_last.start()
     shifted = (two_left, two_here, two_right)
 
     def one_part(rows):
@@ -1464,19 +1663,36 @@
         low_three[rows, :] = dot(strip[...], turned[...]).astype(BF16)
 
     loop(total, BLOCK, one_part)
+
+    def spatial_grads():
+        grads = red_spatial.grad
+        for offset in range(9):
+            row, col = 2 - offset // 3, 2 - offset % 3
+            window = shifted[col][PITCH * row : PITCH * row + total, :]
+            found = t_dot(act_one[PITCH : PITCH + total, :], window).astype(BF16)
+            grads[:, :, :, offset * slim : (offset + 1) * slim] = found.reshape(grads.shape[:3] + (slim,))
+        step(job_spatial)
+
     sum_over_tiles(
-        mail, place, lambda index: low_three.at[tile_rows(index)], near_one, pair_one, far_one, tile, grad_one
-    )
+        mail,
+        place,
+        lambda index: low_three.at[tile_rows(index)],
+        near_one,
+        pair_one,
+        far_one,
+        tile,
+        grad_one,
+        spatial_grads,
+    )
+    step(messages[1])
+    step(messages[2])
+    step(heads[0], heads[1], job_gates, job_stream)
     sums = norm_back(stats, norms, mask, grad_one, pre_one, 0, mid, lambda rows: grad_one[rows, :], base)
     slots_tile[blk] = jnp.concatenate(sums, 0)
     swap_tile_sums(mail, place, slots_tile)
     copies = send_sums(mail, place, slots_one, list(add_up(slots_tile)))
-    grads = red_spatial.grad
-    for offset in range(9):
-        row, col = 2 - offset // 3, 2 - offset % 3
-        window = shifted[col][PITCH * row : PITCH * row + total, :]
-        found = t_dot(act_one[PITCH : PITCH + total, :], window).astype(BF16)
-        grads[:, :, :, offset * slim : (offset + 1) * slim] = found.reshape(grads.shape[:3] + (slim,))
+    step(heads[7], heads[8], job_last, job_spatial)
+    step(heads[5], heads[6], job_shared)
     for copy in copies:
         copy.wait_recv()
     bias_sum, gain_sum = add_up(slots_one)
@@ -1486,14 +1702,13 @@
         all_one[at_base(base, rows), :] = value
 
     through(stats, norms, mask, sizes, grad_one, pre_one, 0, mid, bias_sum, gain_sum, put_one, base)
-    red_shared.finish()
-    red_last.middle()
-    red_spatial.start()
     share_tiles(mail, place, lambda index: all_one.at[tile_rows(index)])
     grads = red_first.grad
     grads[...] = t_dot(wide[...], all_one[...]).astype(BF16).reshape(grads.shape)
-    red_first.start()
-    red_spatial.middle()
+    step(job_first)
+    step(messages[2], job_sums)
+    step(heads[0], heads[1], job_gates, job_stream)
+    step(heads[2], heads[3], heads[4], heads[5], heads[6])
     joined_here.wait()
     for copy in joined_copies:
         copy.wait_recv()
@@ -1503,14 +1718,18 @@
         grad_input[rows, :] = dot_t(own, first[...]) + joined_rows[rows, :].astype(F32)
 
     loop(tile, tile // 3, input_grads)
-    red_last.finish()
-    red_first.middle()
-    red_spatial.finish()
-    red_first.finish()
+    step(job_first)
+    step(heads[2], heads[3], heads[4], heads[5], heads[6], job_sums)
+    step(heads[7], heads[8], job_last, job_spatial)
+    step(heads[7], heads[8], job_last, job_spatial)
+    step(job_first)
+    step(heads[7], heads[8], job_last, job_spatial)
+    for job in messages + heads + [job_gates, job_stream, job_last, job_spatial, job_sums]:
+        step(job)
     mail.close()
 
 
-def bottleneck_back(nb, back, pres, stats, norms, mask, sizes, wide, acts, weights, gate_grads, stream_grads):
+def bottleneck_back(nb, back, pres, stats, norms, mask, sizes, wide, acts, weights, gate_grads, stream_grads, task_grads):
     tile, total = pres[0].shape[0], mask.shape[0]
     mid = pres[0].shape[1]
     slim = mid // 4
@@ -1558,21 +1777,27 @@
         scratch += reduce_scratch(lines, share, columns, True)
     for columns in (mid, LANES):
         scratch += reduce_scratch(lines, share, columns, False)
-    scratch.append(DMA((2, 128)))
+    message_share, head_grads, task_sums = task_grads
+    scratch += [vmem(9, share, mid), vmem(16, mid, kind=F32)]
+    for _ in range(9):
+        scratch += reduce_scratch(lines, share, mid, False)
+    scratch.append(DMA((2, 256)))
     return pl.pallas_call(
         functools.partial(backward_kernel, nb),
         out_shape=(
             array(tile, width, kind=F32),
             array(share, mid),
             array(share, mid),
-            array(share, 9 * slim),
-            array(share, mid),
-            array(share, mid),
-            array(share, LANES),
-            array(8, mid, kind=F32),
+            array(4, share, mid),
+            array(4, share, 9 * slim),
+            array(4, share, mid),
+            array(4, share, LANES),
+            array(4, 9 * share, mid),
+            array(4, message_share.shape[0], mid),
+            array(4, 16, mid, kind=F32),
         ),
-        in_specs=[VMEM] * 19,
-        out_specs=(VMEM,) * 8,
+        in_specs=[VMEM] * 19 + [ANY] * 2 + [VMEM],
+        out_specs=(VMEM,) * 7 + (ANY, ANY, VMEM),
         scratch_shapes=scratch,
         cost_estimate=LONG,
         compiler_params=pltpu.CompilerParams(
@@ -1590,26 +1815,44 @@
         *weights,
         gate_grads.reshape(lines, 2, share, mid),
         stream_grads.reshape(lines, 2, share, LANES),
-    )
-
-
-class Tiles:
-    def __init__(self, mail, place, slot):
-        self.mail, self.place, self.slot = mail, place, slot
-
-    def start(self):
-        own = self.slot(self.place.blk)
-        self.far = self.mail.send(own, own, self.place.across)
-        self.near = self.mail.send(own, own, self.place.mate)
-
-    def forward(self):
-        self.far.wait_recv()
-        passed = self.slot(self.place.blk ^ 2)
-        self.last = self.mail.send(passed, passed, self.place.mate)
-
-    def finish(self):
-        self.near.wait_recv()
-        self.last.wait_recv()
+        message_share,
+        head_grads.reshape(9, lines, 2, share, mid),
+        task_sums,
+    )
+
+
+def finish_kernel(images, first, shared, rest, first_rows, shared_rows, all_rest, sems):
+    place = Place(images)
+    mail = Mail(sems)
+    greet_owners(place)
+    jobs = [
+        Tiles(mail, place, lambda index: all_rest.at[index], rest),
+        Owners(mail, place, first, first_rows),
+        Owners(mail, place, shared, shared_rows),
+    ]
+    for job in jobs:
+        job.start()
+    for job in jobs:
+        job.forward()
+    for job in jobs:
+        job.end()
+    mail.close()
+
+
+def finish(nb, first, shared, rest):
+    share, mid = first.shape
+    return pl.pallas_call(
+        functools.partial(finish_kernel, nb),
+        out_shape=(
+            jax.ShapeDtypeStruct((4, share, mid), BF16),
+            jax.ShapeDtypeStruct((4, share, mid), BF16),
+            jax.ShapeDtypeStruct((4,) + rest.shape, BF16),
+        ),
+        in_specs=[ANY] * 3,
+        out_specs=(ANY,) * 3,
+        scratch_shapes=[DMA((2, 32))],
+        compiler_params=pltpu.CompilerParams(collective_id=26, has_side_effects=True),
+    )(first, shared, rest)
 
 
 def task_kernel(
@@ -1627,6 +1870,7 @@
     to_depth,
     to_classes,
     from_gated,
+    message_own,
     streams,
     slopes,
     pre_five,
@@ -1636,6 +1880,8 @@
     gate_grads,
     stream_grads,
     message_grads,
+    message_rest,
+    message_end,
     left,
     right,
     task,
@@ -1652,6 +1898,19 @@
     mid = pre_five.shape[1]
     is_first, is_last = place.blk == 0, place.blk == 3
     greet(place.others + [place.mate, place.across])
+    late = message_end.shape[0]
+    share = message_own.shape[2]
+    got = [
+        Spread(
+            mail,
+            place,
+            message_own.at[place.blk, 9 - late + at],
+            lambda index, at=at: message_end.at[at, pl.ds(pl.multiple_of(index * share, share), share), :],
+        )
+        for at in range(late)
+    ]
+    for one in got[: late // 2]:
+        one.start()
     stats[...] = jnp.zeros_like(stats)
     for cells in (left, right, task, grad_msg):
         clear_ends(cells, total)
@@ -1663,7 +1922,16 @@
         )
 
     loop(total, BLOCK, heads)
-    batch_norm_stats(mail, place, pre_five, mask, slots_five, sizes, stats, 0, mid)
+
+    def behind():
+        for one in got[: late // 2]:
+            one.forward()
+        for one in got[late // 2 :]:
+            one.start()
+
+    batch_norm_stats(mail, place, pre_five, mask, slots_five, sizes, stats, 0, mid, behind)
+    for one in got[late // 2 :]:
+        one.forward()
 
     def act_task(rows):
         value = (pre_five[rows, :] - stats[0:1, :]) * stats[1:2, :] * norms[0:1, :] + norms[1:2, :]
@@ -1673,9 +1941,13 @@
 
     loop(total, CHUNK, act_task)
     widen(task, left, right, total)
+    for one in got:
+        one.finish()
 
     def message_weight(offset):
-        return message_start[offset] if offset < early else head[9 + offset - early]
+        if offset < early:
+            return message_start[offset]
+        return head[9 + offset - early] if offset < 9 - late else message_end[offset - 9 + late]
 
     def here(rows):
         return pl.ds(pl.multiple_of(PITCH + rows.start, 16), rows.size)
@@ -1731,16 +2003,18 @@
     for offset in range(9):
         row, col = 2 - offset // 3, 2 - offset % 3
         window = shifted[col][PITCH * row : PITCH * row + total, :]
-        message_grads[:, offset * mid : (offset + 1) * mid] = t_dot(
-            task[PITCH : PITCH + total, :], window
-        ).astype(BF16)
+        found = t_dot(task[PITCH : PITCH + total, :], window).astype(BF16)
+        if offset < early:
+            message_grads[offset] = found
+        else:
+            message_rest[:, (offset - early) * mid : (offset - early + 1) * mid] = found
     mail.close()
 
 
 CLASSES = 40
 
 
-def one_task(nb, early, shared_act, mask, mask_line, targets, sizes, norms, weights, streams_weights):
+def one_task(nb, early, late, shared_act, mask, mask_line, targets, sizes, norms, weights, streams_weights, own):
     total = mask.shape[0]
     padded, mid = shared_act.shape
     lines = streams_weights[0].shape[0]
@@ -1762,10 +2036,12 @@
             array(total, mid),
             array(mid, mid),
             array(mid, LANES),
-            array(mid, 9 * mid),
+            array(early, mid, mid),
+            array(mid, (9 - early) * mid),
+            array(late, mid, mid),
         ),
-        in_specs=[VMEM] * 12,
-        out_specs=(VMEM,) * 9,
+        in_specs=[VMEM] * 12 + [ANY],
+        out_specs=(VMEM,) * 11,
         scratch_shapes=[
             vmem(padded, mid),
             vmem(padded, mid),
@@ -1775,13 +2051,13 @@
             vmem(total, mid),
             vmem(4, lines, total, kind=F32),
             vmem(nb, 2, mid, kind=F32),
-            DMA((2, 32)),
+            DMA((2, 64)),
         ],
         cost_estimate=LONG,
         compiler_params=pltpu.CompilerParams(
             collective_id=23, has_side_effects=True, vmem_limit_bytes=60 * 2**20
         ),
-    )(shared_act, mask, mask_line, targets, sizes, norms, *weights, *streams_weights)
+    )(shared_act, mask, mask_line, targets, sizes, norms, *weights, *streams_weights, own)
 
 
 def task_back_kernel(
@@ -1794,34 +2070,52 @@
     head,
     message_start,
     gate,
+    message_end,
     from_direct,
     slopes,
     pre_five,
     stats,
     grad_msg,
     grad_gate,
+    message_grads,
     back,
     head_grads,
+    message_done,
     sums_out,
     left,
     right,
     grad_five,
     grad,
     slots_five,
-    sems,
+    *rest,
 ):
     place = Place(images)
-    mail = Mail(sems)
+    mail = Mail(rest[-1])
+    sums_of = [
+        Reduce(
+            mail,
+            place,
+            message_grads.at[offset],
+            *rest[3 * offset : 3 * offset + 3],
+            message_done.at[offset],
+        )
+        for offset in range(early)
+    ]
     total = mask.shape[0]
+    late = message_end.shape[0]
     mid = pre_five.shape[1]
     greet(place.others)
     sums_out[...] = jnp.zeros_like(sums_out)
+    sums_of[0].start()
+    sums_of[1].start()
     for cells in (left, right, grad_five):
         clear_ends(cells, total)
     widen(grad_msg, left, right, total)
 
     def message_weight(offset):
-        return message_start[offset] if offset < early else head[9 + offset - early]
+        if offset < early:
+            return message_start[offset]
+        return head[9 + offset - early] if offset < 9 - late else message_end[offset - 9 + late]
 
     def task_grads(rows):
         found = conv_rows(
@@ -1832,7 +2126,12 @@
 
     loop(total, BLOCK, task_grads)
     sums = norm_back(stats, norms, mask, grad, pre_five, 0, mid, lambda rows: grad[rows, :])
-    for copy in send_sums(mail, place, slots_five, sums):
+    copies = send_sums(mail, place, slots_five, sums)
+    sums_of[0].middle()
+    sums_of[1].middle()
+    for one in sums_of[2:]:
+        one.start()
+    for copy in copies:
         copy.wait_recv()
     bias_sum, gain_sum = add_up(slots_five)
     sums_out[0:1, :] = gain_sum
@@ -1851,18 +2150,23 @@
         ).astype(BF16)
 
     loop(total, BLOCK, head_back)
+    for one in sums_of[2:]:
+        one.middle()
+    sums_of[0].finish()
+    sums_of[1].finish()
     for offset in range(9):
         row, col = 2 - offset // 3, 2 - offset % 3
         window = shifted[col][PITCH * row : PITCH * row + total, :]
-        head_grads[:, offset * mid : (offset + 1) * mid] = t_dot(
-            shared_act[PITCH : PITCH + total, :], window
-        ).astype(BF16)
+        head_grads[offset] = t_dot(shared_act[PITCH : PITCH + total, :], window).astype(BF16)
+    for one in sums_of[2:]:
+        one.finish()
     mail.close()
 
 
 def one_task_back(nb, early, shared_act, mask, sizes, norms, weights, from_direct, slopes, rest):
     total = mask.shape[0]
     padded, mid = shared_act.shape
+    lines, share = nb // 2, mid // nb
 
     def array(*shape, kind=BF16):
         return jax.ShapeDtypeStruct(shape, kind)
@@ -1872,17 +2176,23 @@
 
     return pl.pallas_call(
         functools.partial(task_back_kernel, nb, early),
-        out_shape=(array(total, mid), array(mid, 9 * mid), array(8, mid, kind=F32)),
-        in_specs=[VMEM] * 13,
-        out_specs=(VMEM,) * 3,
+        out_shape=(
+            array(total, mid),
+            array(9, mid, mid),
+            array(early, share, mid),
+            array(8, mid, kind=F32),
+        ),
+        in_specs=[VMEM] * 15,
+        out_specs=(VMEM,) * 4,
         scratch_shapes=[
             vmem(padded, mid),
             vmem(padded, mid),
             vmem(padded, mid),
             vmem(total, mid, kind=F32),
             vmem(nb, 2, mid, kind=F32),
-            DMA((2, 16)),
-        ],
+        ]
+        + early * reduce_scratch(lines, share, mid, False)
+        + [DMA((2, 48))],
         cost_estimate=LONG,
         compiler_params=pltpu.CompilerParams(
             collective_id=24, has_side_effects=True, vmem_limit_bytes=60 * 2**20
@@ -2043,11 +2353,11 @@
             filled(bias_four),
         ]
     )
-    early = 5
+    early, late = 5, 4
     large = jnp.concatenate(
         [
             lax.dynamic_index_in_dim(head_weights, blk, 0, False),
-            lax.dynamic_index_in_dim(message_weights, blk, 0, False)[early:],
+            lax.dynamic_index_in_dim(message_weights, blk, 0, False)[early : 9 - late],
         ],
         0,
     )
@@ -2112,9 +2422,12 @@
         gate_grads,
         stream_grads,
         message_grads,
+        message_rest,
+        message_end,
     ) = one_task(
         nb,
         early,
+        late,
         shared_act,
         inside_wide,
         mask_line,
@@ -2123,35 +2436,39 @@
         task_norms,
         weights,
         (to_depth, to_classes, from_gated),
+        message_weights,
     )
     own_streams = lax.dynamic_slice_in_dim(streams, blk * tile_rows * PITCH, tile_rows * PITCH, 1)
     own_streams = own_streams.reshape(lines, tile_rows, PITCH)[:, :, :cols]
     depth_out = own_streams[0]
     logits = own_streams[1 : 1 + classes].transpose(1, 2, 0)
-    share_messages = lax.psum_scatter(message_grads, "batch", scatter_dimension=0, tiled=True)
-    back, head_grads, task_sums = one_task_back(
+    rest_share = lax.psum_scatter(message_rest, "batch", scatter_dimension=0, tiled=True)
+    message_grads = message_grads.reshape(early, nb // 2, 2, share, mid)
+    back, head_grads, message_done, task_sums = one_task_back(
         nb,
         early,
         shared_act,
         inside_wide,
         sizes,
         task_norms,
-        weights,
+        weights + (message_end,),
         from_direct,
         slopes,
-        (pre_five, task_stats, grad_msg, grad_gate),
-    )
-
-    share_heads = lax.psum_scatter(head_grads, "batch", scatter_dimension=0, tiled=True)
+        (pre_five, task_stats, grad_msg, grad_gate, message_grads),
+    )
+    message_share = message_done.reshape(early * share, mid)
+
     (
         grad_input,
         share_shared,
-        share_last,
-        share_spatial,
         share_first,
-        share_gates,
-        share_stream,
-        sums_wide,
+        all_last,
+        all_spatial,
+        all_gates,
+        all_stream,
+        all_heads,
+        all_messages,
+        sums,
     ) = bottleneck_back(
         nb,
         back,
@@ -2165,46 +2482,26 @@
         (spatial, last, shared, full_first),
         gate_grads,
         stream_grads,
+        (message_share, head_grads, task_sums),
     )
     grad_input = grad_input.reshape(tile_rows, PITCH, width)[:, :cols]
 
-    moved = lax.ppermute(
-        jnp.concatenate([share_first, share_shared], 0), ("blk", "batch"), [(b, a) for a, b in order]
-    )
-    share_messages, share_heads, moved = lax.optimization_barrier((share_messages, share_heads, moved))
-    shares = jnp.concatenate(
-        [
-            moved,
-            share_last,
-            share_gates,
-            share_spatial.reshape(share, 9, slim).swapaxes(0, 1).reshape(-1, mid),
-            share_stream.reshape(-1, mid),
-            share_messages.reshape(share, 9, mid).swapaxes(0, 1).reshape(9 * share, mid),
-            share_heads.reshape(share, 9, mid).swapaxes(0, 1).reshape(9 * share, mid),
-        ],
-        0,
-    )
-    sums = jnp.pad(jnp.concatenate([sums_wide, task_sums[:2]], 0), ((0, 6), (0, 0)))
-    all_shares, sums = gather_last(shares, sums)
-    at = 0
-
-    def part(count):
-        nonlocal at
-        found = all_shares[:, at : at + count].astype(F32)
-        at += count
-        return found
-
-    red_first = part(share).reshape(nt * share, mid)
-    red_shared = part(share).reshape(nt * share, mid)
-    red_last = part(share).transpose(1, 0, 2).reshape(share, width)
-    red_gates = part(share)
-    red_spatial = part(9 * share * slim // mid).reshape(nt, 9, share, slim)
-    red_spatial = red_spatial.transpose(1, 2, 0, 3).reshape(9, share, mid)
-    streams_red = jnp.sum(part(share * LANES // mid).reshape(nt, share, LANES), 0)
+    rest_share, share_first = lax.optimization_barrier((rest_share, share_first))
+    rest_share = rest_share.reshape(share, 9 - early, mid).swapaxes(0, 1).reshape((9 - early) * share, mid)
+    red_first, red_shared, all_rest = finish(nb, share_first, share_shared, rest_share)
+    red_first = red_first.astype(F32).reshape(nt * share, mid)
+    red_shared = red_shared.astype(F32).reshape(nt * share, mid)
+    red_messages = jnp.concatenate(
+        [all_messages.reshape(nt, early, share, mid), all_rest.reshape(nt, 9 - early, share, mid)], 1
+    ).astype(F32)
+    red_last = all_last.astype(F32).transpose(1, 0, 2).reshape(share, width)
+    red_gates = all_gates.astype(F32)
+    red_spatial = all_spatial.astype(F32).reshape(nt, share, 9, slim)
+    red_spatial = red_spatial.transpose(2, 1, 0, 3).reshape(9, share, mid)
+    streams_red = jnp.sum(all_stream.astype(F32), 0)
     red_depth = streams_red[:, 0]
     red_classes = streams_red[:, 1 : 1 + classes]
-    red_messages = part(9 * share).reshape(nt, 9, share, mid)
-    red_heads = part(9 * share).reshape(nt, 9, share, mid)
+    red_heads = all_heads.astype(F32).reshape(nt, 9, share, mid)
     two_gain, two_bias = sums[:, 2, :slim].reshape(1, mid), sums[:, 3, :slim].reshape(1, mid)
     four_gain, four_bias = sums[:, 6, :slim].reshape(1, mid), sums[:, 7, :slim].reshape(1, mid)
     mid_gains = jnp.concatenate([sums[0, 0:1], two_gain, four_gain, sums[:, 8]], 0)

time: 610 us -> 579 us (0.949)
  the two profiles are of different devices: /device:TPU:0 before, /device:TPU:2 now
where the time goes in v4:
time: 579 us; the launch traced here: 571 us
  Pallas kernels  496 us (86%)
  local copies, waits for them, and re-layouts  36 us (6%)
  other arithmetic  19.5 us (3%)
  between operations  14.8 us (3%)
    pallas_call x1, Pallas kernels, bottleneck_back(): pl.pallas_call(functools.partial(backward_kernel, nb), out_shape=(array(t...  159 us
    pallas_call x1, Pallas kernels, bottleneck(): pl.pallas_call(functools.partial(forward_kernel, nb, early), out_shape=ou...  125 us
    pallas_call x1, Pallas kernels, one_task(): pl.pallas_call(functools.partial(task_kernel, nb, early), out_shape=(arra...  81.4 us
    pallas_call x1, Pallas kernels, one_task_back(): pl.pallas_call(functools.partial(task_back_kernel, nb, early), out_shape=...  61 us
    pallas_call x1, Pallas kernels, begin(): pl.pallas_call(functools.partial(start_kernel, nb), out_shape=(array(nb,...  39.5 us
    pallas_call x1, Pallas kernels, finish(): pl.pallas_call(functools.partial(finish_kernel, nb), out_shape=(jax.Shape...  29.9 us
  transfers between devices with their start and end apart: 3, of which 0 were waited for; matrix products, arithmetic and copies ran while one was open for 7% of the time, Pallas kernels for 67%

profile of v4, /device:TPU:2, one launch (start us, length us, event | category | flops | bytes accessed | tf_op | source)
XLA Modules:
  0.0 570.6 jit_solution(16887018469680582912)
XLA Ops:
  7.2 0.9 copy-done
  8.1 4.5 collective-permute-start
  12.6 1.2 dynamic_slice.63
  13.9 1.2 dynamic_slice.62
  15.1 0.7 multiply_convert_fusion
  15.8 0.8 reshape.231
  16.5 0.8 reshape.232
  17.3 0.8 copy.76
  18.1 0.1 reshape.233
  18.2 2.1 concatenate.15
  20.3 0.7 convert_element_type.84
  21.0 0.7 select_maximum_fusion
  21.8 0.7 iota_compare_fusion.4
  22.4 0.7 iota_compare_fusion.5
  23.2 0.4 reshape.287.mask
  23.5 0.1 convert_reduce_fusion.1
  23.7 0.1 reduce_sum.26
  23.7 1.6 pad.35
  25.3 0.1 reduce_sum.27
  25.4 1.9 dynamic-slice_bitcast_fusion
  27.5 39.5 %shard_map.297 = (bf16[8,256,512]{2,1,0:T(8,128)(2,1)S(1)}, bf16[8,32,128]{2,1,0:T(8,128)(2,1)S(1)}, f32[8,1536]{1,0:T(8,128)S(1)}, bf16[1536,512]{1,0:T(8,128)(...) custom-call(bf16[256,512]{1,0:T(8,128)(2,1)S(1)} %copy-done.5, ...), custom_call_target="tpu_custom_call" | custom-call | flops 80000000000 | bytes 30000000 | tf_op jit(solution)/shard_map/pallas_call | solution.py:974
  67.1 1.3 copy-done.6
  68.4 1.1 copy-done.7
  69.5 1.0 copy-done.8
  70.5 0.9 copy-done.9
  71.4 0.6 copy-done.10
  72.0 0.6 copy-done.11
  73.2 0.1 slice.155
  73.9 0.2 reshape.241
  74.1 0.1 copy.81
  74.2 0.1 reshape.240
  74.4 0.6 stack.45.norms
  75.1 0.7 broadcast_select_fusion
  75.8 0.6 select_maximum_fusion.1.norms
  76.5 124.7 %shard_map.298 = (bf16[512,512]{1,0:T(8,128)(2,1)}, bf16[512,512]{1,0:T(8,128)(2,1)}, bf16[512,512]{1,0:T(8,128)(2,1)}, bf16[5,512,512]{2,1,0:T(8,128)(2,1)}, bf...) custom-call(f32[384,512]{1,0:T(8,128)} %copy-done.9, ...), custom_call_target="tpu_custom_call" | custom-call | flops 80000000000 | bytes 30000000 | tf_op jit(solution)/shard_map/pallas_call | solution.py:1198
  201.2 0.6 broadcast_in_dim.62.mask_line
  201.8 81.4 %shard_map.299 = (f32[48,1536]{1,0:T(8,128)}, bf16[48,1536]{1,0:T(8,128)(2,1)}, f32[1536,512]{1,0:T(8,128)}, f32[8,512]{1,0:T(8,128)}, bf16[1632,512]{1,0:T(8,12...) custom-call(bf16[1632,512]{1,0:T(8,128)(2,1)} %get-tuple-element.73., ...), custom_call_target="tpu_custom_call" | custom-call | flops 80000000000 | bytes 30000000 | tf_op jit(solution)/shard_map/pallas_call | solution.py:2028
  283.2 61.0 %shard_map.300 = (bf16[1536,512]{1,0:T(8,128)(2,1)}, bf16[9,512,512]{2,1,0:T(8,128)(2,1)}, bf16[5,64,512]{2,1,0:T(8,128)(2,1)}, f32[8,512]{1,0:T(8,128)}) custom-call(bf16[1632,512]{1,0:T(8,128)(2,1)} %get-tuple-element.73.shared_act, f32[1536,1]{1,0:T(8,128)} %copy-done.2, f32[8,1,512]{2,1,0:T(1,128)} %copy-done.3, f32[8,512]{1,0:T(8,128)} %select_maximum_fusion.1.norms, ...), custom_call_target="tpu_custom_call" | custom-call | flops 80000000000 | bytes 30000000 | tf_op jit(solution)/shard_map/pallas_call | solution.py:2177
  344.3 159.1 %shard_map.301 = (f32[384,2048]{1,0:T(8,128)}, bf16[64,512]{1,0:T(8,128)(2,1)}, bf16[64,512]{1,0:T(8,128)(2,1)}, bf16[4,64,512]{2,1,0:T(8,128)(2,1)}, bf16[4,64,...) custom-call(bf16[1536,512]{1,0:T(8,128)(2,1)} %get-tuple-element.86., ...), custom_call_target="tpu_custom_call" | custom-call | flops 80000000000 | bytes 30000000 | tf_op jit(solution)/shard_map/pallas_call | solution.py:1785
  503.4 0.9 constant_dynamic-slice_fusion
  504.3 0.1 reshape.242
  504.4 0.6 slice.156
  505.0 0.8 copy.88
  505.8 1.3 reshape.286
  507.2 0.8 copy.86
  507.9 1.5 reshape.274
  509.5 0.8 copy.93
  510.3 4.6 convert.19
  515.0 0.9 convert_element_type.99
  515.9 0.7 copy.89
  516.6 1.0 fusion.11
  517.6 0.6 dynamic_slice.81
  518.2 0.6 dynamic_slice.82
  518.9 0.8 slice_bitcast_fusion.6
  519.7 0.9 slice_bitcast_fusion.4
  520.6 0.7 fusion.5
  521.3 0.7 fusion.2
  522.0 0.6 slice_reduce_fusion
  522.6 1.7 slice_bitcast_fusion
  524.3 1.8 copy.101
  526.0 29.9 %shard_map.302 = (bf16[4,64,512]{2,1,0:T(8,128)(2,1)}, bf16[4,64,512]{2,1,0:T(8,128)(2,1)}, bf16[4,256,512]{2,1,0:T(8,128)(2,1)}) custom-call(bf16[64,512]{1,0:T(8,128)(2,1)} %get-tuple-element.105.first, bf16[64,512]{1,0:T(8,128)(2,1)} %get-tuple-element.106.shared, bf16[256,512]{1,0:T(8,128)(2,1)} %bitcast.100), custom_call_target="tpu_custom_call" | custom-call | tf_op jit(solution)/shard_map/pallas_call | solution.py:1844
  556.0 1.8 bitcast_convert_fusion.1
  557.8 1.8 bitcast_convert_fusion
  559.6 3.8 maximum_convert_fusion
  (79 shorter events, 1.9 us)
Async XLA Ops:
  7.2 1.0 copy-start
  7.2 194.0 %all-gather.2.cloned.1.call-start = ((), (), s32[]{:S(2)}) async-start(), calls=%async_computation.1 | async-start | bytes 5308416 | tf_op jit(solution)/shard_map/all_gather | solution.py:2365
  8.1 68.3 %collective-permute-start = (bf16[64,512]{1,0:T(8,128)(2,1)S(1)}, bf16[64,512]{1,0:T(8,128)(2,1)}, u32[]{:S(2)}, u32[]{:S(2)}) collective-permute-start(bf16[64,512]{1,0:T(8,128)(2,1)S(1)} %constant_dynamic-slice_fusion.3), channel_id=1, source_target_pairs={{0,0},{1,4},{2,8},{3,12},{4,16},{5,20},{6,24},{7,28},{8,1},{9,5},{... | collective-permute-start | bytes 196616 | tf_op jit(solution)/shard_map/ppermute | solution.py:2307
  23.1 4.4 copy-start.4
  23.1 4.4 copy-start.5
  23.5 43.5 %copy-start.2 = (f32[1536,1]{1,0:T(8,128)}, f32[1536,1]{1,0:T(8,128)S(1)}, u32[]{:S(2)}) copy-start(f32[1536,1]{1,0:T(8,128)S(1)} %reshape.287.mask) | copy-start | bytes 18436
  27.4 39.6 %copy-start.3 = (f32[8,1,512]{2,1,0:T(1,128)}, f32[8,1,512]{2,1,0:T(1,128)S(1)}, u32[]{:S(2)}) copy-start(f32[8,1,512]{2,1,0:T(1,128)S(1)} %broadcast_in_dim.60.sizes) | copy-start | bytes 49156
  67.0 1.3 copy-start.6
  68.4 1.1 copy-start.7
  69.5 1.0 copy-start.8
  70.5 0.9 copy-start.9
  71.4 0.6 copy-start.10
  72.0 0.6 copy-start.11
  72.7 451.6 %reduce-scatter.2.cloned.1.call-start = ((), (), s32[]{:S(2)}) async-start(), calls=%async_computation.2 | async-start | bytes 2359296 | tf_op jit(solution)/shard_map/reduce_scatter | solution.py:2445
  507.2 2.3 copy-start.15
  510.3 4.6 copy-start.14
  510.3 5.5 copy-start.16
  510.3 12.3 %copy-start.12 = (f32[384,2048]{1,0:T(8,128)S(1)}, f32[384,2048]{1,0:T(8,128)}, u32[]{:S(2)}) copy-start(f32[384,2048]{1,0:T(8,128)} %get-tuple-element.102) | copy-start | bytes 9437188
  524.3 35.3 %copy-start.13 = (bf16[4,320,512]{2,1,0:T(8,128)(2,1)S(1)}, bf16[4,320,512]{2,1,0:T(8,128)(2,1)}, u32[]{:S(2)}) copy-start(bf16[4,320,512]{2,1,0:T(8,128)(2,1)} %get-tuple-element.113) | copy-start | bytes 3932164
  559.6 3.8 copy-start.1
Sparse Core Ops, SparseCore 0:
  72.8 122.3 all-gather.1
  283.4 77.2 reduce-scatter.1

commit v5 on v4

--- a/solution.py
+++ b/solution.py
@@ -708,21 +708,58 @@
     far.wait_send()
 
 
-def loop(total, step, body):
+def loop(total, step, body, base=0):
     def run(at, carry):
-        body(pl.ds(pl.multiple_of(at * step, step), step))
+        body(pl.ds(pl.multiple_of(base + at * step, step), step))
         return carry
 
     lax.fori_loop(0, total // step, run, 0)
+
+
+PIECES = 3
+
+
+def pieces_of(total):
+    size = total // PIECES
+    return [(at * size, size) for at in range(PIECES)]
+
+
+def share_pieces(mail, place, slot, total, produce=None, consume=None, meanwhile=None):
+    pieces = pieces_of(total)
+    far, near, last = [], [], []
+    for first, size in pieces:
+        if produce is not None:
+            produce(first, size)
+        own = slot(place.blk, first, size)
+        far.append(mail.send(own, own, place.across, False))
+        near.append(mail.send(own, own, place.mate, False))
+    if meanwhile is not None:
+        meanwhile()
+
+    def use(at):
+        near[at].wait_recv()
+        last[at].wait_recv()
+        if consume is not None:
+            consume(*pieces[at])
+
+    for at, (first, size) in enumerate(pieces):
+        far[at].wait_recv()
+        passed = slot(place.blk ^ 2, first, size)
+        last.append(mail.send(passed, passed, place.mate, False))
+        if at > 0:
+            use(at - 1)
+    use(len(pieces) - 1)
+    for copy in far + near + last:
+        copy.wait_send()
 
 
 def folded(values):
     return jnp.sum(values.reshape(values.shape[0] // 8, 8, values.shape[1]), 0)
 
 
-def loop_sums(total, channels, count, body):
+def loop_sums(total, channels, count, body, base=0):
     def run(at, carry):
-        found = body(pl.ds(pl.multiple_of(at * CHUNK, CHUNK), CHUNK))
+        found = body(pl.ds(pl.multiple_of(base + at * CHUNK, CHUNK), CHUNK))
         return tuple(kept + folded(one) for kept, one in zip(carry, found))
 
     start = tuple(jnp.zeros((8, channels), F32) for _ in range(count))
@@ -836,28 +873,42 @@
     return total
 
 
-def sum_over_tiles(mail, place, part, near_in, pair, far_in, total, out, meanwhile=None):
-    far_first = mail.send(part(place.blk ^ 3), near_in.at[0], place.mate)
-    near_next = mail.send(part(place.blk ^ 1), near_in.at[1], place.mate)
-    far_first.wait_recv()
+def sum_over_tiles(mail, place, part, near_in, pair, far_in, total, out, meanwhile=None, produce=None):
     mine_far, mine = part(place.blk ^ 2), part(place.blk)
+    pieces = pieces_of(total)
+    near_far, near_own, far = [], [], []
 
     def pairs(rows):
         pair[rows, :] = (mine_far[rows, :].astype(F32) + near_in[0, rows, :].astype(F32)).astype(BF16)
 
-    loop(total, CHUNK, pairs)
-    far = mail.send(pair, far_in, place.across)
+    def pass_on(at):
+        first, size = pieces[at]
+        near_far[at].wait_recv()
+        loop(size, CHUNK, pairs, first)
+        here = pl.ds(first, size)
+        far.append(mail.send(pair.at[here], far_in.at[here], place.across))
+
+    for at, (first, size) in enumerate(pieces):
+        if produce is not None:
+            produce(first, size)
+        here = pl.ds(first, size)
+        near_far.append(mail.send(part(place.blk ^ 3).at[here], near_in.at[0, here], place.mate))
+        near_own.append(mail.send(part(place.blk ^ 1).at[here], near_in.at[1, here], place.mate))
+        if at > 0:
+            pass_on(at - 1)
+    pass_on(len(pieces) - 1)
     if meanwhile is not None:
         meanwhile()
-    near_next.wait_recv()
-    far.wait_recv()
 
     def finish(rows):
         out[rows, :] = (
             mine[rows, :].astype(F32) + near_in[1, rows, :].astype(F32) + far_in[rows, :].astype(F32)
         )
 
-    loop(total, CHUNK, finish)
+    for at, (first, size) in enumerate(pieces):
+        near_own[at].wait_recv()
+        far[at].wait_recv()
+        loop(size, CHUNK, finish, first)
 
 
 def start_kernel(
@@ -1076,9 +1127,14 @@
         value = silu(value) * mask[at_base(base, rows), :]
         act_one[pl.ds(pl.multiple_of(PITCH + base + rows.start, 16), CHUNK), :] = value.astype(BF16)
 
-    loop(tile, CHUNK, act_first)
-    share_tiles(
-        mail, place, lambda index: act_one.at[pl.ds(pl.multiple_of(PITCH + index * tile, 16), tile), :]
+    share_pieces(
+        mail,
+        place,
+        lambda index, first, size: act_one.at[
+            pl.ds(pl.multiple_of(PITCH + index * tile + first, 16), size), :
+        ],
+        tile,
+        lambda first, size: loop(size, CHUNK, act_first, first),
     )
     widen(act_one, one_left, one_right, total)
     got_last.forward()
@@ -1105,16 +1161,20 @@
         value = silu(value * norms[2:3, :slim] + norms[3:4, :slim]) * mask[rows, :]
         act_two[rows, lanes] = value.astype(BF16)
 
-    loop(total, CHUNK, act_second)
-    share_tiles(mail, place, lambda index: act_two.at[:, slim_lanes(index)])
-
     got_last.finish()
-    got_gate.forward()
 
     def expand(rows):
         pre_three[rows, :] = dot(act_two[rows, :], last[...])
 
-    loop(total, BLOCK, expand)
+    share_pieces(
+        mail,
+        place,
+        lambda index, first, size: act_two.at[pl.ds(first, size), slim_lanes(index)],
+        total,
+        lambda first, size: loop(size, CHUNK, act_second, first),
+        lambda first, size: loop(size, BLOCK, expand, first),
+    )
+    got_gate.forward()
 
     def after_three():
         got_message[0].forward()
@@ -1135,7 +1195,6 @@
     def reduce(rows):
         parts[rows, :] = dot(act_three[rows, :], shared[...]).astype(BF16)
 
-    loop(total, BLOCK, reduce)
     sum_over_tiles(
         mail,
         place,
@@ -1145,6 +1204,8 @@
         far_in,
         total,
         pre_four,
+        None,
+        lambda first, size: loop(size, BLOCK, reduce, first),
     )
 
     def after_four():
@@ -1160,9 +1221,12 @@
         value = silu(value * norms[6:7, :slim] + norms[7:8, :slim]) * mask[rows, :]
         shared_act[pl.ds(pl.multiple_of(PITCH + rows.start, 16), CHUNK), lanes] = value.astype(BF16)
 
-    loop(total, CHUNK, act_fourth)
-    share_tiles(
-        mail, place, lambda index: shared_act.at[pl.ds(PITCH, total), slim_lanes(index)]
+    share_pieces(
+        mail,
+        place,
+        lambda index, first, size: shared_act.at[pl.ds(PITCH + first, size), slim_lanes(index)],
+        total,
+        lambda first, size: loop(size, CHUNK, act_fourth, first),
     )
     for later in got_message[4:]:
         later.forward()
@@ -1399,7 +1463,8 @@
 
 def step(*jobs):
     for job in jobs:
-        job.steps.pop(0)()
+        if job.steps:
+            job.steps.pop(0)()
 
 
 def reduce_scratch(lines, share, columns, own):
@@ -1422,7 +1487,7 @@
     return sigmoid_value * (1.0 + value * (1.0 - sigmoid_value))
 
 
-def norm_back(stats, norms, mask, grad, pre, row, channels, lead, offset=None, skip=None):
+def norm_back(stats, norms, mask, grad, pre, row, channels, lead, offset=None, skip=None, rows_of=None):
     def body(rows):
         normed = (pre[rows, :] - stats[row : row + 1, :channels]) * stats[row + 1 : row + 2, :channels]
         value = normed * norms[row : row + 1, :channels] + norms[row + 1 : row + 2, :channels]
@@ -1432,10 +1497,11 @@
         grad[rows, :] = found
         return found, found * normed
 
-    return loop_sums(pre.shape[0], channels, 2, body)
-
-
-def through(stats, norms, mask, sizes, grad, pre, row, channels, bias_sum, gain_sum, put, offset=None):
+    first, size = (0, pre.shape[0]) if rows_of is None else rows_of
+    return loop_sums(size, channels, 2, body, first)
+
+
+def through(stats, norms, mask, sizes, grad, pre, row, channels, bias_sum, gain_sum, put, offset=None, rows_of=None):
     count = sizes[0, :, :channels]
     for at in range(1, sizes.shape[0]):
         count = count + sizes[at, :, :channels]
@@ -1447,7 +1513,8 @@
         found = scale * (grad[rows, :] - bias_part - normed * gain_part)
         put(rows, (found * mask[at_base(offset, rows), :]).astype(BF16))
 
-    loop(pre.shape[0], CHUNK, body)
+    first, size = (0, pre.shape[0]) if rows_of is None else rows_of
+    loop(size, CHUNK, body, first)
 
 
 def backward_kernel(
@@ -1539,11 +1606,13 @@
     def slots_of(slots):
         return Tiles(mail, place, lambda index: slots.at[index])
 
-    for offset in range(9):
+    kept = head_grads.shape[0]
+    for offset in range(kept):
         result = results.at[offset]
         reduce = ReduceFar(mail, place, head_grads.at[offset], *rest[at : at + 3], result)
         at += 3
         heads.append(Job(reduce, tiles_of(all_heads, offset * share, share, result)))
+    heads += [Job(None, None)] * (9 - kept)
     early = message_share.shape[0] // share
     ends = [0, early // 3, 2 * early // 3, early]
     for begin_at, end_at in zip(ends[:-1], ends[1:]):
@@ -1590,14 +1659,33 @@
     def put_four(rows, value):
         all_four[rows, lanes] = value
 
-    through(stats, norms, mask, sizes, grad_four, pre_four, 6, slim, bias_sum, gain_sum, put_four)
-    share_tiles(mail, place, lambda index: all_four.at[:, slim_lanes(index)])
-    step(messages[0])
-
     def joined_back(rows):
         return dot_t(all_four[rows, :], shared[...])
 
-    sums = norm_back(stats, norms, mask, grad_three, pre_three, 4, mid, joined_back, None, wide)
+    sums = []
+
+    def make_four(first, size):
+        through(
+            stats, norms, mask, sizes, grad_four, pre_four, 6, slim, bias_sum, gain_sum, put_four, None, (first, size)
+        )
+
+    def use_four(first, size):
+        sums.append(
+            norm_back(
+                stats, norms, mask, grad_three, pre_three, 4, mid, joined_back, None, wide, (first, size)
+            )
+        )
+
+    share_pieces(
+        mail,
+        place,
+        lambda index, first, size: all_four.at[pl.ds(first, size), slim_lanes(index)],
+        total,
+        make_four,
+        use_four,
+    )
+    step(messages[0])
+    sums = [sum(one[1:], one[0]) for one in zip(*sums)]
     copies = send_sums(mail, place, slots_three, sums)
     step(heads[2], heads[3], heads[4])
     step(heads[5], heads[6])
@@ -1619,14 +1707,26 @@
     def put_three(rows, value):
         low_three[rows, :] = value
 
-    through(stats, norms, mask, sizes, grad_three, pre_three, 4, mid, bias_sum, gain_sum, put_three)
-
     def two_part(rows):
         all_four[rows, :] = dot_t(low_three[rows, :], last[...]).astype(BF16)
 
-    loop(total, BLOCK, two_part)
+    def make_two(first, size):
+        through(
+            stats, norms, mask, sizes, grad_three, pre_three, 4, mid, bias_sum, gain_sum, put_three, None, (first, size)
+        )
+        loop(size, BLOCK, two_part, first)
+
     sum_over_tiles(
-        mail, place, lambda index: all_four.at[:, slim_lanes(index)], near_two, pair_two, far_two, total, grad_two
+        mail,
+        place,
+        lambda index: all_four.at[:, slim_lanes(index)],
+        near_two,
+        pair_two,
+        far_two,
+        total,
+        grad_two,
+        None,
+        make_two,
     )
     step(messages[1])
     landing = joined_rows.at[:, pl.ds(pl.multiple_of(blk * mid, mid), mid)]
@@ -1701,23 +1801,39 @@
     def put_one(rows, value):
         all_one[at_base(base, rows), :] = value
 
-    through(stats, norms, mask, sizes, grad_one, pre_one, 0, mid, bias_sum, gain_sum, put_one, base)
-    share_tiles(mail, place, lambda index: all_one.at[tile_rows(index)])
+    def make_one(first, size):
+        through(
+            stats, norms, mask, sizes, grad_one, pre_one, 0, mid, bias_sum, gain_sum, put_one, base, (first, size)
+        )
+
+    def inputs_back():
+        joined_here.wait()
+        for copy in joined_copies:
+            copy.wait_recv()
+
+        def input_grads(rows):
+            own = all_one[pl.ds(pl.multiple_of(base + rows.start, CHUNK), rows.size), :]
+            grad_input[rows, :] = dot_t(own, first[...]) + joined_rows[rows, :].astype(F32)
+
+        loop(tile, tile // 3, input_grads)
+
+    share_pieces(
+        mail,
+        place,
+        lambda index, first, size: all_one.at[
+            pl.ds(pl.multiple_of(index * tile + first, CHUNK), size), :
+        ],
+        tile,
+        make_one,
+        None,
+        inputs_back,
+    )
     grads = red_first.grad
     grads[...] = t_dot(wide[...], all_one[...]).astype(BF16).reshape(grads.shape)
     step(job_first)
     step(messages[2], job_sums)
     step(heads[0], heads[1], job_gates, job_stream)
     step(heads[2], heads[3], heads[4], heads[5], heads[6])
-    joined_here.wait()
-    for copy in joined_copies:
-        copy.wait_recv()
-
-    def input_grads(rows):
-        own = all_one[pl.ds(pl.multiple_of(base + rows.start, CHUNK), rows.size), :]
-        grad_input[rows, :] = dot_t(own, first[...]) + joined_rows[rows, :].astype(F32)
-
-    loop(tile, tile // 3, input_grads)
     step(job_first)
     step(heads[2], heads[3], heads[4], heads[5], heads[6], job_sums)
     step(heads[7], heads[8], job_last, job_spatial)
@@ -1778,8 +1894,9 @@
     for columns in (mid, LANES):
         scratch += reduce_scratch(lines, share, columns, False)
     message_share, head_grads, task_sums = task_grads
-    scratch += [vmem(9, share, mid), vmem(16, mid, kind=F32)]
-    for _ in range(9):
+    kept = head_grads.shape[0]
+    scratch += [vmem(kept, share, mid), vmem(16, mid, kind=F32)]
+    for _ in range(kept):
         scratch += reduce_scratch(lines, share, mid, False)
     scratch.append(DMA((2, 256)))
     return pl.pallas_call(
@@ -1792,7 +1909,7 @@
             array(4, share, 9 * slim),
             array(4, share, mid),
             array(4, share, LANES),
-            array(4, 9 * share, mid),
+            array(4, kept * share, mid),
             array(4, message_share.shape[0], mid),
             array(4, 16, mid, kind=F32),
         ),
@@ -1816,7 +1933,7 @@
         gate_grads.reshape(lines, 2, share, mid),
         stream_grads.reshape(lines, 2, share, LANES),
         message_share,
-        head_grads.reshape(9, lines, 2, share, mid),
+        head_grads.reshape(kept, lines, 2, share, mid),
         task_sums,
     )
 
@@ -2080,6 +2197,7 @@
     message_grads,
     back,
     head_grads,
+    head_rest,
     message_done,
     sums_out,
     left,
@@ -2157,13 +2275,18 @@
     for offset in range(9):
         row, col = 2 - offset // 3, 2 - offset % 3
         window = shifted[col][PITCH * row : PITCH * row + total, :]
-        head_grads[offset] = t_dot(shared_act[PITCH : PITCH + total, :], window).astype(BF16)
+        found = t_dot(shared_act[PITCH : PITCH + total, :], window).astype(BF16)
+        kept = head_grads.shape[0]
+        if offset < kept:
+            head_grads[offset] = found
+        else:
+            head_rest[:, (offset - kept) * mid : (offset - kept + 1) * mid] = found
     for one in sums_of[2:]:
         one.finish()
     mail.close()
 
 
-def one_task_back(nb, early, shared_act, mask, sizes, norms, weights, from_direct, slopes, rest):
+def one_task_back(nb, early, kept, shared_act, mask, sizes, norms, weights, from_direct, slopes, rest):
     total = mask.shape[0]
     padded, mid = shared_act.shape
     lines, share = nb // 2, mid // nb
@@ -2178,12 +2301,13 @@
         functools.partial(task_back_kernel, nb, early),
         out_shape=(
             array(total, mid),
-            array(9, mid, mid),
+            array(kept, mid, mid),
+            array(mid, (9 - kept) * mid),
             array(early, share, mid),
             array(8, mid, kind=F32),
         ),
         in_specs=[VMEM] * 15,
-        out_specs=(VMEM,) * 4,
+        out_specs=(VMEM,) * 5,
         scratch_shapes=[
             vmem(padded, mid),
             vmem(padded, mid),
@@ -2444,9 +2568,11 @@
     logits = own_streams[1 : 1 + classes].transpose(1, 2, 0)
     rest_share = lax.psum_scatter(message_rest, "batch", scatter_dimension=0, tiled=True)
     message_grads = message_grads.reshape(early, nb // 2, 2, share, mid)
-    back, head_grads, message_done, task_sums = one_task_back(
+    kept = 7
+    back, head_grads, head_rest, message_done, task_sums = one_task_back(
         nb,
         early,
+        kept,
         shared_act,
         inside_wide,
         sizes,
@@ -2457,6 +2583,7 @@
         (pre_five, task_stats, grad_msg, grad_gate, message_grads),
     )
     message_share = message_done.reshape(early * share, mid)
+    head_share = lax.psum_scatter(head_rest, "batch", scatter_dimension=0, tiled=True)
 
     (
         grad_input,
@@ -2486,13 +2613,16 @@
     )
     grad_input = grad_input.reshape(tile_rows, PITCH, width)[:, :cols]
 
-    rest_share, share_first = lax.optimization_barrier((rest_share, share_first))
-    rest_share = rest_share.reshape(share, 9 - early, mid).swapaxes(0, 1).reshape((9 - early) * share, mid)
+    rest_share, head_share, share_first = lax.optimization_barrier((rest_share, head_share, share_first))
+    rest_share = jnp.concatenate([rest_share, head_share], 1)
+    left = 18 - early - kept
+    rest_share = rest_share.reshape(share, left, mid).swapaxes(0, 1).reshape(left * share, mid)
     red_first, red_shared, all_rest = finish(nb, share_first, share_shared, rest_share)
     red_first = red_first.astype(F32).reshape(nt * share, mid)
     red_shared = red_shared.astype(F32).reshape(nt * share, mid)
+    all_rest = all_rest.reshape(nt, left, share, mid)
     red_messages = jnp.concatenate(
-        [all_messages.reshape(nt, early, share, mid), all_rest.reshape(nt, 9 - early, share, mid)], 1
+        [all_messages.reshape(nt, early, share, mid), all_rest[:, : 9 - early]], 1
     ).astype(F32)
     red_last = all_last.astype(F32).transpose(1, 0, 2).reshape(share, width)
     red_gates = all_gates.astype(F32)
@@ -2501,7 +2631,9 @@
     streams_red = jnp.sum(all_stream.astype(F32), 0)
     red_depth = streams_red[:, 0]
     red_classes = streams_red[:, 1 : 1 + classes]
-    red_heads = all_heads.astype(F32).reshape(nt, 9, share, mid)
+    red_heads = jnp.concatenate(
+        [all_heads.reshape(nt, kept, share, mid), all_rest[:, 9 - early :]], 1
+    ).astype(F32)
     two_gain, two_bias = sums[:, 2, :slim].reshape(1, mid), sums[:, 3, :slim].reshape(1, mid)
     four_gain, four_bias = sums[:, 6, :slim].reshape(1, mid), sums[:, 7, :slim].reshape(1, mid)
     mid_gains = jnp.concatenate([sums[0, 0:1], two_gain, four_gain, sums[:, 8]], 0)

time: 579 us -> 559 us (0.965)
  Pallas kernels: 496 us -> 475 us
    pallas_call x1, Pallas kernels: 159 us -> 145 us  [bottleneck_back(): pl.pallas_call(functools.partial(backward_kernel, nb), out_shape=(array(t...]
  transfers between devices with their start and end apart: 3 -> 4, of which waited for: 0 -> 0; matrix products, arithmetic and copies ran while one was open for 7% -> 7% of each run, Pallas kernels for 67% -> 56%
where the time goes in v5:
time: 559 us; the launch traced here: 550 us
  Pallas kernels  475 us (85%)
  local copies, waits for them, and re-layouts  40 us (7%)
  other arithmetic  15.2 us (3%)
  between operations  14.6 us (3%)
    pallas_call x1, Pallas kernels, bottleneck_back(): pl.pallas_call(functools.partial(backward_kernel, nb), out_shape=(array(t...  145 us
    pallas_call x1, Pallas kernels, bottleneck(): pl.pallas_call(functools.partial(forward_kernel, nb, early), out_shape=ou...  123 us
    pallas_call x1, Pallas kernels, one_task(): pl.pallas_call(functools.partial(task_kernel, nb, early), out_shape=(arra...  79.6 us
    pallas_call x1, Pallas kernels, one_task_back(): pl.pallas_call(functools.partial(task_back_kernel, nb, early), out_shape=...  59.5 us
    pallas_call x1, Pallas kernels, begin(): pl.pallas_call(functools.partial(start_kernel, nb), out_shape=(array(nb,...  39.5 us
    pallas_call x1, Pallas kernels, finish(): pl.pallas_call(functools.partial(finish_kernel, nb), out_shape=(jax.Shape...  28.4 us
  transfers between devices with their start and end apart: 4, of which 0 were waited for; matrix products, arithmetic and copies ran while one was open for 7% of the time, Pallas kernels for 56%

profile of v5, /device:TPU:2, one launch (start us, length us, event | category | flops | bytes accessed | tf_op | source)
XLA Modules:
  0.0 550.1 jit_solution(1751595816599485282)
XLA Ops:
  7.2 0.9 copy-done
  8.1 4.5 collective-permute-start
  12.6 1.2 dynamic_slice.63
  13.9 1.2 dynamic_slice.62
  15.1 0.7 multiply_convert_fusion
  15.8 0.8 reshape.228
  16.5 0.8 reshape.229
  17.3 0.8 copy.76
  18.2 2.1 concatenate.21
  20.3 0.7 convert_element_type.86
  21.0 0.7 select_maximum_fusion
  21.8 0.7 iota_compare_fusion.4
  22.4 0.7 iota_compare_fusion.5
  23.2 0.4 reshape.281.mask
  23.5 0.1 convert_reduce_fusion.1
  23.7 1.6 pad.35
  25.3 0.1 reduce_sum.27
  25.4 1.9 dynamic-slice_bitcast_fusion
  27.5 39.5 %shard_map.297 = (bf16[8,256,512]{2,1,0:T(8,128)(2,1)S(1)}, bf16[8,32,128]{2,1,0:T(8,128)(2,1)S(1)}, f32[8,1536]{1,0:T(8,128)S(1)}, bf16[1536,512]{1,0:T(8,128)(...) custom-call(bf16[256,512]{1,0:T(8,128)(2,1)S(1)} %copy-done.5, ...), custom_call_target="tpu_custom_call" | custom-call | flops 80000000000 | bytes 30000000 | tf_op jit(solution)/shard_map/pallas_call | solution.py:1025
  67.1 1.3 copy-done.6
  68.4 1.1 copy-done.7
  69.5 1.0 copy-done.8
  70.5 0.9 copy-done.9
  71.4 0.6 copy-done.10
  72.0 0.6 copy-done.11
  73.9 0.2 reshape.238
  74.4 0.6 stack.45.norms
  75.1 0.8 broadcast_select_fusion
  75.9 0.6 select_maximum_fusion.1.norms
  76.5 122.9 %shard_map.298 = (bf16[512,512]{1,0:T(8,128)(2,1)}, bf16[512,512]{1,0:T(8,128)(2,1)}, bf16[512,512]{1,0:T(8,128)(2,1)}, bf16[5,512,512]{2,1,0:T(8,128)(2,1)}, bf...) custom-call(f32[384,512]{1,0:T(8,128)} %copy-done.9, ...), custom_call_target="tpu_custom_call" | custom-call | flops 80000000000 | bytes 30000000 | tf_op jit(solution)/shard_map/pallas_call | solution.py:1262
  199.4 0.6 broadcast_in_dim.62.mask_line
  200.0 79.6 %shard_map.299 = (f32[48,1536]{1,0:T(8,128)}, bf16[48,1536]{1,0:T(8,128)(2,1)}, f32[1536,512]{1,0:T(8,128)}, f32[8,512]{1,0:T(8,128)}, bf16[1632,512]{1,0:T(8,12...) custom-call(bf16[1632,512]{1,0:T(8,128)(2,1)} %get-tuple-element.75., ...), custom_call_target="tpu_custom_call" | custom-call | flops 80000000000 | bytes 30000000 | tf_op jit(solution)/shard_map/pallas_call | solution.py:2145
  279.6 59.5 %shard_map.300 = (bf16[1536,512]{1,0:T(8,128)(2,1)}, bf16[7,512,512]{2,1,0:T(8,128)(2,1)}, bf16[512,1024]{1,0:T(8,128)(2,1)}, bf16[5,64,512]{2,1,0:T(8,128)(2,1)}, f32[8,512]{1,0:T(8,128)}) custom-call(bf16[1632,512]{1,0:T(8,128)(2,1)} %get-tuple-element.75.shared_act, f32[1536,1]{1,0:T(8,128)} %copy-done.2, f32[8,1,512]{2,1,0:T(1,128)} %copy-done.3, ...), custom_call_target="tpu_custom_call" | custom-call | flops 80000000000 | bytes 30000000 | tf_op jit(solution)/shard_map/pallas_call | solution.py:2300
  339.2 0.7 reduce-scatter.3.cloned.1.call-update
  339.9 145.0 %shard_map.301 = (f32[384,2048]{1,0:T(8,128)}, bf16[64,512]{1,0:T(8,128)(2,1)}, bf16[64,512]{1,0:T(8,128)(2,1)}, bf16[4,64,512]{2,1,0:T(8,128)(2,1)}, bf16[4,64,...) custom-call(bf16[1536,512]{1,0:T(8,128)(2,1)} %get-tuple-element.88., ...), custom_call_target="tpu_custom_call" | custom-call | flops 80000000000 | bytes 30000000 | tf_op jit(solution)/shard_map/pallas_call | solution.py:1902
  484.9 0.9 constant_dynamic-slice_fusion
  485.8 0.1 reshape.239
  485.9 0.6 slice.164
  486.5 0.8 copy.88
  487.3 1.3 reshape.280
  488.7 0.8 copy.86
  489.5 1.5 reshape.270
  491.0 0.8 copy.92
  491.9 0.9 convert_element_type.102
  492.8 0.7 copy.89
  493.5 1.0 fusion.11
  494.5 0.6 dynamic_slice.81
  495.1 0.6 dynamic_slice.82
  495.8 0.8 slice_bitcast_fusion.6
  496.6 0.9 slice_bitcast_fusion.4
  497.4 0.7 fusion.5
  498.1 0.7 fusion.2
  498.8 0.6 slice_reduce_fusion
  499.4 3.5 slice_bitcast_fusion
  502.9 1.0 pad_maximum_fusion
  504.0 0.5 reshape.249
  504.5 0.9 copy.85
  505.3 28.4 %shard_map.302 = (bf16[4,64,512]{2,1,0:T(8,128)(2,1)}, bf16[4,64,512]{2,1,0:T(8,128)(2,1)}, bf16[4,384,512]{2,1,0:T(8,128)(2,1)}) custom-call(bf16[64,512]{1,0:T(8,128)(2,1)} %get-tuple-element.108.first, bf16[64,512]{1,0:T(8,128)(2,1)} %get-tuple-element.109.shared, bf16[384,512]{1,0:T(8,128)(2,1)} %bitcast.92), custom_call_target="tpu_custom_call" | custom-call | tf_op jit(solution)/shard_map/pallas_call | solution.py:1961
  533.8 1.2 slice.167
  535.0 1.3 slice.168
  536.3 0.9 bitcast_convert_fusion.1
  537.2 0.9 bitcast_convert_fusion
  538.1 2.5 maximum_convert_fusion
  540.6 2.5 maximum_convert_fusion.1
  (90 shorter events, 2.4 us)
Async XLA Ops:
  7.2 1.0 copy-start
  7.2 192.2 %all-gather.2.cloned.1.call-start = ((), (), s32[]{:S(2)}) async-start(), calls=%async_computation.2 | async-start | bytes 5308416 | tf_op jit(solution)/shard_map/all_gather | solution.py:2489
  8.1 68.3 %collective-permute-start = (bf16[64,512]{1,0:T(8,128)(2,1)S(1)}, bf16[64,512]{1,0:T(8,128)(2,1)}, u32[]{:S(2)}, u32[]{:S(2)}) collective-permute-start(bf16[64,512]{1,0:T(8,128)(2,1)S(1)} %constant_dynamic-slice_fusion.3), channel_id=1, source_target_pairs={{0,0},{1,4},{2,8},{3,12},{4,16},{5,20},{6,24},{7,28},{8,1},{9,5},{... | collective-permute-start | bytes 196616 | tf_op jit(solution)/shard_map/ppermute | solution.py:2431
  23.1 4.4 copy-start.4
  23.1 4.4 copy-start.5
  23.5 43.5 %copy-start.2 = (f32[1536,1]{1,0:T(8,128)}, f32[1536,1]{1,0:T(8,128)S(1)}, u32[]{:S(2)}) copy-start(f32[1536,1]{1,0:T(8,128)S(1)} %reshape.281.mask) | copy-start | bytes 18436
  27.4 39.6 %copy-start.3 = (f32[8,1,512]{2,1,0:T(1,128)}, f32[8,1,512]{2,1,0:T(1,128)S(1)}, u32[]{:S(2)}) copy-start(f32[8,1,512]{2,1,0:T(1,128)S(1)} %broadcast_in_dim.60.sizes) | copy-start | bytes 49156
  67.1 1.3 copy-start.6
  68.4 1.1 copy-start.7
  69.5 1.0 copy-start.8
  70.5 0.9 copy-start.9
  71.4 0.6 copy-start.10
  72.0 0.6 copy-start.11
  72.7 430.3 %reduce-scatter.5.cloned.1.call-start = ((), (), s32[]{:S(2)}) async-start(), calls=%async_computation.4 | async-start | bytes 1179648 | tf_op jit(solution)/shard_map/reduce_scatter | solution.py:2586
  339.2 163.8 %reduce-scatter.3.cloned.1.call-start = ((), (), s32[]{:S(2)}) async-start(), calls=%async_computation.3 | async-start | bytes 2359296 | tf_op jit(solution)/shard_map/reduce_scatter | solution.py:2569
  489.4 1.5 copy-start.15
  489.5 2.4 copy-start.14
  489.5 3.3 copy-start.18
  533.8 2.6 copy-start.17
  533.8 3.5 copy-start.16
  533.8 4.3 copy-start.12
  538.1 2.5 copy-start.13
  540.6 2.5 copy-start.1
Sparse Core Ops, SparseCore 0:
  72.8 124.1 all-gather.1
  339.3 68.7 reduce-scatter.4
  412.1 74.6 reduce-scatter.2

commit v6 on v5

--- a/solution.py
+++ b/solution.py
@@ -917,6 +917,7 @@
     small,
     spatial_own,
     pair,
+    head_all,
     feat,
     mask,
     sizes,
@@ -928,6 +929,7 @@
     spatial,
     pre_one,
     stats,
+    head_own,
     slots_tile,
     slots_one,
     sems,
@@ -945,6 +947,7 @@
     greet(place.others + place.tiles)
     here = mail.local(weight, full.at[batch])
     here_small = mail.local(small, smalls.at[batch])
+    here_head = mail.local(head_all.at[blk], head_own)
     z_copies, x_copies, arrived, late = {}, [], [], []
     for peer in place.others:
         late.append(mail.send(small, smalls.at[batch], peer))
@@ -1012,10 +1015,11 @@
     here_small.wait()
     here_wide.wait()
     here_line.wait()
+    here_head.wait()
     mail.close()
 
 
-def begin(nb, weight, small, spatial, pair, feat, mask, sizes, tile_sizes):
+def begin(nb, weight, small, spatial, pair, heads, feat, mask, sizes, tile_sizes):
     depth, mid = weight.shape
     tile = feat.shape[0]
 
@@ -1032,9 +1036,10 @@
             array(9, mid, mid // 4),
             array(tile, mid, kind=F32),
             array(8, mid, kind=F32),
+            array(*heads.shape[1:]),
         ),
-        in_specs=[ANY] * 4 + [VMEM] * 4,
-        out_specs=(VMEM, ANY, ANY, VMEM, VMEM, VMEM, VMEM),
+        in_specs=[ANY] * 5 + [VMEM] * 4,
+        out_specs=(VMEM, ANY, ANY, VMEM, VMEM, VMEM, VMEM, ANY),
         scratch_shapes=[
             pltpu.VMEM((4, 2, mid), F32),
             pltpu.VMEM((nb, 2, mid), F32),
@@ -1044,7 +1049,7 @@
         compiler_params=pltpu.CompilerParams(
             collective_id=21, has_side_effects=True, vmem_limit_bytes=40 * 2**20
         ),
-    )(weight, small, spatial, pair, feat, mask, sizes, tile_sizes)
+    )(weight, small, spatial, pair, heads, feat, mask, sizes, tile_sizes)
 
 
 def forward_kernel(
@@ -1274,7 +1279,7 @@
             pltpu.VMEM((nb, 2, slim), F32),
             pltpu.VMEM((nb, 2, mid), F32),
             pltpu.VMEM((nb, 2, slim), F32),
-            DMA((2, 128)),
+            DMA((2, 192)),
         ],
         cost_estimate=LONG,
         compiler_params=pltpu.CompilerParams(
@@ -1359,97 +1364,6 @@
         if at == 0:
             self.fetch.wait()
         return self.summed[at]
-
-
-class Owners:
-    def __init__(self, mail, place, result, slots):
-        self.mail, self.place, self.result, self.slots = mail, place, result, slots
-        self.base = mail.used
-        mail.used += 5
-        self.owner = 2 * place.blk + lax.div(place.batch, 4)
-        self.quarter = lax.rem(place.batch, 4)
-        self.at_home = self.owner == place.batch
-
-    def copy(self, mask):
-        place, mail = self.place, self.mail
-        return pltpu.make_async_remote_copy(
-            src_ref=self.result,
-            dst_ref=self.slots.at[self.quarter],
-            send_sem=mail.sems.at[0, self.base + mask],
-            recv_sem=mail.sems.at[1, self.base + self.quarter],
-            device_id=(place.blk ^ mask, self.owner),
-            device_id_type=MESH,
-        )
-
-    def local(self):
-        return pltpu.make_async_copy(
-            self.result, self.slots.at[self.quarter], self.mail.sems.at[0, self.base + 4]
-        )
-
-    def start(self):
-        for mask in range(1, 4):
-            self.copy(mask).start()
-
-        @pl.when(self.at_home)
-        def _():
-            self.local().start()
-
-        @pl.when(jnp.logical_not(self.at_home))
-        def _():
-            self.copy(0).start()
-
-    def forward(self):
-        for mask in range(1, 4):
-            self.copy(mask).wait_send()
-
-        @pl.when(self.at_home)
-        def _():
-            self.local().wait()
-
-        @pl.when(jnp.logical_not(self.at_home))
-        def _():
-            self.copy(0).wait_send()
-
-    def end(self):
-        place, mail = self.place, self.mail
-        for quarter in range(4):
-            source = 4 * lax.rem(place.batch, 2) + quarter
-            at_home = (lax.div(place.batch, 2) == place.blk) & (source == place.batch)
-
-            @pl.when(jnp.logical_not(at_home))
-            def _():
-                pltpu.make_async_remote_copy(
-                    src_ref=self.result,
-                    dst_ref=self.slots.at[quarter],
-                    send_sem=mail.sems.at[0, self.base],
-                    recv_sem=mail.sems.at[1, self.base + quarter],
-                    device_id=place.mate,
-                    device_id_type=MESH,
-                ).wait_recv()
-
-
-def greet_owners(place):
-    barrier = pltpu.get_barrier_semaphore()
-    regular = [place.mate, place.across]
-    for peer in regular:
-        pl.semaphore_signal(barrier, inc=1, device_id=peer, device_id_type=MESH)
-    for quarter in range(4):
-        source = (lax.div(place.batch, 2), 4 * lax.rem(place.batch, 2) + quarter)
-        at_home = (source[0] == place.blk) & (source[1] == place.batch)
-
-        @pl.when(jnp.logical_not(at_home))
-        def _():
-            pl.semaphore_signal(barrier, inc=1, device_id=source, device_id_type=MESH)
-
-    owner = 2 * place.blk + lax.div(place.batch, 4)
-
-    @pl.when(owner == place.batch)
-    def _():
-        pl.semaphore_wait(barrier, len(regular) + 3)
-
-    @pl.when(owner != place.batch)
-    def _():
-        pl.semaphore_wait(barrier, len(regular) + 4)
 
 
 class Job:
@@ -1941,17 +1855,69 @@
 def finish_kernel(images, first, shared, rest, first_rows, shared_rows, all_rest, sems):
     place = Place(images)
     mail = Mail(sems)
-    greet_owners(place)
-    jobs = [
-        Tiles(mail, place, lambda index: all_rest.at[index], rest),
-        Owners(mail, place, first, first_rows),
-        Owners(mail, place, shared, shared_rows),
-    ]
+    blk, batch = place.blk, place.batch
+    target = (lax.rem(batch, 4), 2 * blk + lax.div(batch, 4))
+    source = (lax.div(batch, 2), 4 * lax.rem(batch, 2) + blk)
+    stays = (target[0] == blk) & (target[1] == batch)
+    moves = jnp.logical_not(stays)
+    barrier = pltpu.get_barrier_semaphore()
+    for peer in (place.mate, place.across):
+        pl.semaphore_signal(barrier, inc=1, device_id=peer, device_id_type=MESH)
+
+    @pl.when(moves)
+    def _():
+        pl.semaphore_signal(barrier, inc=1, device_id=source, device_id_type=MESH)
+        pl.semaphore_wait(barrier, 3)
+
+    @pl.when(stays)
+    def _():
+        pl.semaphore_wait(barrier, 2)
+
+    def hop(at, own, slots):
+        return pltpu.make_async_remote_copy(
+            src_ref=own,
+            dst_ref=slots.at[target[0]],
+            send_sem=sems.at[0, at],
+            recv_sem=sems.at[1, at],
+            device_id=target,
+            device_id_type=MESH,
+        )
+
+    def stay(at, own, slots):
+        return pltpu.make_async_copy(own, slots.at[blk], sems.at[0, at])
+
+    mail.used = 2
+    pairs = [(0, first, first_rows), (1, shared, shared_rows)]
+
+    @pl.when(moves)
+    def _():
+        for pair in pairs:
+            hop(*pair).start()
+
+    @pl.when(stays)
+    def _():
+        for pair in pairs:
+            stay(*pair).start()
+
+    tiles = Tiles(mail, place, lambda index: all_rest.at[index], rest)
+    tiles.start()
+    jobs = [Tiles(mail, place, lambda index, slots=slots: slots.at[index]) for _, _, slots in pairs]
+
+    @pl.when(moves)
+    def _():
+        for pair in pairs:
+            hop(*pair).wait()
+
+    @pl.when(stays)
+    def _():
+        for pair in pairs:
+            stay(*pair).wait()
+
     for job in jobs:
         job.start()
-    for job in jobs:
+    for job in [tiles] + jobs:
         job.forward()
-    for job in jobs:
+    for job in [tiles] + jobs:
         job.end()
     mail.close()
 
@@ -2026,7 +1992,7 @@
         )
         for at in range(late)
     ]
-    for one in got[: late // 2]:
+    for one in got[: (late + 1) // 2]:
         one.start()
     stats[...] = jnp.zeros_like(stats)
     for cells in (left, right, task, grad_msg):
@@ -2041,13 +2007,13 @@
     loop(total, BLOCK, heads)
 
     def behind():
-        for one in got[: late // 2]:
+        for one in got[: (late + 1) // 2]:
             one.forward()
-        for one in got[late // 2 :]:
+        for one in got[(late + 1) // 2 :]:
             one.start()
 
     batch_norm_stats(mail, place, pre_five, mask, slots_five, sizes, stats, 0, mid, behind)
-    for one in got[late // 2 :]:
+    for one in got[(late + 1) // 2 :]:
         one.forward()
 
     def act_task(rows):
@@ -2433,8 +2399,8 @@
     )
     pair = jnp.stack([depth_target[0], labels[0].astype(F32)])
     pair = jnp.pad(pair, ((0, 6), (0, 0), (0, PITCH - cols))).reshape(8, tile_rows * PITCH)
-    full_first, smalls, targets, wide_features, spatial, pre_one, stats = begin(
-        nb, first_weight, small, spatial_weight, pair, feat, inside_wide, sizes, tile_sizes
+    full_first, smalls, targets, wide_features, spatial, pre_one, stats, large = begin(
+        nb, first_weight, small, spatial_weight, pair, head_weights, feat, inside_wide, sizes, tile_sizes
     )
     full_first = full_first.reshape(width, mid)
     smalls = smalls.reshape(nb, room)
@@ -2477,15 +2443,7 @@
             filled(bias_four),
         ]
     )
-    early, late = 5, 4
-    large = jnp.concatenate(
-        [
-            lax.dynamic_index_in_dim(head_weights, blk, 0, False),
-            lax.dynamic_index_in_dim(message_weights, blk, 0, False)[early : 9 - late],
-        ],
-        0,
-    )
-    large, stats = lax.optimization_barrier((large, stats))
+    early, late = 4, 5
     large = lax.all_gather(large, "batch", axis=1, tiled=True)
     (
         last,

time: 559 us -> 549 us (0.982)
  the two profiles are of different devices: /device:TPU:2 before, /device:TPU:0 now
where the time goes in v6:
time: 549 us; the launch traced here: 540 us
  Pallas kernels  465 us (85%)
  local copies, waits for them, and re-layouts  40 us (7%)
  other arithmetic  15.3 us (3%)
  between operations  14.6 us (3%)
    pallas_call x1, Pallas kernels, bottleneck_back(): pl.pallas_call(functools.partial(backward_kernel, nb), out_shape=(array(t...  145 us
    pallas_call x1, Pallas kernels, bottleneck(): pl.pallas_call(functools.partial(forward_kernel, nb, early), out_shape=ou...  117 us
    pallas_call x1, Pallas kernels, one_task(): pl.pallas_call(functools.partial(task_kernel, nb, early), out_shape=(arra...  85.5 us
    pallas_call x1, Pallas kernels, one_task_back(): pl.pallas_call(functools.partial(task_back_kernel, nb, early), out_shape=...  52.7 us
    pallas_call x1, Pallas kernels, begin(): pl.pallas_call(functools.partial(start_kernel, nb), out_shape=(array(nb,...  45 us
    pallas_call x1, Pallas kernels, finish(): pl.pallas_call(functools.partial(finish_kernel, nb), out_shape=(jax.Shape...  20.1 us
  transfers between devices with their start and end apart: 4, of which 1 were waited for; matrix products, arithmetic and copies ran while one was open for 6% of the time, Pallas kernels for 57%

profile of v6, /device:TPU:0, one launch (start us, length us, event | category | flops | bytes accessed | tf_op | source)
XLA Modules:
  0.0 540.3 jit_solution(16638175940658660518)
XLA Ops:
  7.3 0.9 copy-done
  8.1 1.3 collective-permute-start
  9.4 1.2 dynamic_slice.59
  10.7 1.2 dynamic_slice.58
  11.9 0.7 multiply_convert_fusion
  12.6 0.8 reshape.228
  13.3 0.8 reshape.229
  14.1 0.8 copy.76
  15.0 2.1 concatenate.21
  17.1 0.7 convert_element_type.86
  17.8 0.7 select_maximum_fusion
  18.6 0.7 iota_compare_fusion.4
  19.2 0.7 iota_compare_fusion.5
  19.9 0.4 reshape.281.mask
  20.5 1.6 pad.35
  22.1 0.1 reduce_sum.27
  22.4 1.7 copy-done.4
  24.1 45.0 %shard_map.297 = (bf16[8,256,512]{2,1,0:T(8,128)(2,1)S(1)}, bf16[8,32,128]{2,1,0:T(8,128)(2,1)S(1)}, f32[8,1536]{1,0:T(8,128)S(1)}, bf16[1536,512]{1,0:T(8,128)(...) custom-call(bf16[256,512]{1,0:T(8,128)(2,1)S(1)} %copy-done.6, ...), custom_call_target="tpu_custom_call" | custom-call | flops 80000000000 | bytes 30000000 | tf_op jit(solution)/shard_map/pallas_call | solution.py:1029
  69.1 1.3 copy-done.7
  70.4 1.1 copy-done.8
  71.5 1.0 copy-done.9
  72.5 0.9 copy-done.10
  73.4 0.6 copy-done.11
  74.0 0.6 copy-done.12
  75.9 0.2 reshape.238
  76.4 0.6 stack.45.norms
  77.1 0.7 broadcast_select_fusion
  77.9 0.6 select_maximum_fusion.1.norms
  78.5 116.7 %shard_map.298 = (bf16[512,512]{1,0:T(8,128)(2,1)}, bf16[512,512]{1,0:T(8,128)(2,1)}, bf16[512,512]{1,0:T(8,128)(2,1)}, bf16[4,512,512]{2,1,0:T(8,128)(2,1)}, bf...) custom-call(f32[384,512]{1,0:T(8,128)} %copy-done.10, ...), custom_call_target="tpu_custom_call" | custom-call | flops 80000000000 | bytes 30000000 | tf_op jit(solution)/shard_map/pallas_call | solution.py:1267
  195.2 3.1 all-gather.2.cloned.1.call-done.head
  198.3 0.6 broadcast_in_dim.62.mask_line
  199.0 85.5 %shard_map.299 = (f32[48,1536]{1,0:T(8,128)}, bf16[48,1536]{1,0:T(8,128)(2,1)}, f32[1536,512]{1,0:T(8,128)}, f32[8,512]{1,0:T(8,128)}, bf16[1632,512]{1,0:T(8,12...) custom-call(bf16[1632,512]{1,0:T(8,128)(2,1)} %get-tuple-element.73., ...), custom_call_target="tpu_custom_call" | custom-call | flops 80000000000 | bytes 30000000 | tf_op jit(solution)/shard_map/pallas_call | solution.py:2111
  284.4 52.7 %shard_map.300 = (bf16[1536,512]{1,0:T(8,128)(2,1)}, bf16[7,512,512]{2,1,0:T(8,128)(2,1)}, bf16[512,1024]{1,0:T(8,128)(2,1)}, bf16[4,64,512]{2,1,0:T(8,128)(2,1)}, f32[8,512]{1,0:T(8,128)}) custom-call(bf16[1632,512]{1,0:T(8,128)(2,1)} %get-tuple-element.73.shared_act, f32[1536,1]{1,0:T(8,128)} %copy-done.2, f32[8,1,512]{2,1,0:T(1,128)} %copy-done.3, ...), custom_call_target="tpu_custom_call" | custom-call | flops 80000000000 | bytes 30000000 | tf_op jit(solution)/shard_map/pallas_call | solution.py:2266
  337.2 0.7 reduce-scatter.3.cloned.1.call-update
  337.9 145.2 %shard_map.301 = (f32[384,2048]{1,0:T(8,128)}, bf16[64,512]{1,0:T(8,128)(2,1)}, bf16[64,512]{1,0:T(8,128)(2,1)}, bf16[4,64,512]{2,1,0:T(8,128)(2,1)}, bf16[4,64,...) custom-call(bf16[1536,512]{1,0:T(8,128)(2,1)} %get-tuple-element.86., ...), custom_call_target="tpu_custom_call" | custom-call | flops 80000000000 | bytes 30000000 | tf_op jit(solution)/shard_map/pallas_call | solution.py:1816
  483.1 0.9 constant_dynamic-slice_fusion
  484.0 0.1 reshape.239
  484.1 0.6 slice.164
  484.7 0.8 copy.88
  485.5 1.3 reshape.280
  486.8 0.8 copy.86
  487.6 1.5 reshape.270
  489.2 0.8 copy.92
  490.0 0.9 convert_element_type.102
  491.0 0.7 copy.89
  491.7 1.0 fusion.11
  492.6 0.6 dynamic_slice.76
  493.3 0.6 dynamic_slice.77
  493.9 0.8 slice_bitcast_fusion.6
  494.7 0.9 slice_bitcast_fusion.4
  495.6 0.7 fusion.5
  496.3 0.7 fusion.2
  496.9 0.6 slice_reduce_fusion
  497.6 3.5 slice_bitcast_fusion
  501.1 1.1 pad_maximum_fusion
  502.2 0.5 reshape.249
  502.7 0.9 copy.85
  503.7 20.1 %shard_map.302 = (bf16[4,64,512]{2,1,0:T(8,128)(2,1)}, bf16[4,64,512]{2,1,0:T(8,128)(2,1)}, bf16[4,448,512]{2,1,0:T(8,128)(2,1)}) custom-call(bf16[64,512]{1,0:T(8,128)(2,1)} %get-tuple-element.106.first, bf16[64,512]{1,0:T(8,128)(2,1)} %get-tuple-element.107.shared, bf16[448,512]{1,0:T(8,128)(2,1)} %bitcast.92), custom_call_target="tpu_custom_call" | custom-call | tf_op jit(solution)/shard_map/pallas_call | solution.py:1927
  523.8 1.1 slice.167
  525.0 1.6 slice.168
  526.6 0.9 bitcast_convert_fusion.1
  527.4 0.9 bitcast_convert_fusion
  528.3 2.5 maximum_convert_fusion
  530.8 2.5 maximum_convert_fusion.1
  (91 shorter events, 2.5 us)
Async XLA Ops:
  7.2 1.0 copy-start
  7.2 15.2 %copy-start.6 = (bf16[256,512]{1,0:T(8,128)(2,1)S(1)}, bf16[256,512]{1,0:T(8,128)(2,1)}, u32[]{:S(2)}) copy-start(bf16[256,512]{1,0:T(8,128)(2,1)} %weight.1) | copy-start | bytes 786436
  7.2 15.2 %copy-start.5 = (bf16[9,64,512]{2,1,0:T(8,128)(2,1)S(1)}, bf16[9,64,512]{2,1,0:T(8,128)(2,1)}, u32[]{:S(2)}) copy-start(bf16[9,64,512]{2,1,0:T(8,128)(2,1)} %spatial_own.1) | copy-start | bytes 1769476
  7.2 191.1 %all-gather.2.cloned.1.call-start = ((), (), s32[]{:S(2)}) async-start(), calls=%async_computation.2 | async-start | bytes 5308416 | tf_op jit(solution)/shard_map/all_gather | solution.py:2447
  8.1 70.3 %collective-permute-start = (bf16[64,512]{1,0:T(8,128)(2,1)S(1)}, bf16[64,512]{1,0:T(8,128)(2,1)}, u32[]{:S(2)}, u32[]{:S(2)}) collective-permute-start(bf16[64,512]{1,0:T(8,128)(2,1)S(1)} %constant_dynamic-slice_fusion.3), channel_id=1, source_target_pairs={{0,0},{1,4},{2,8},{3,12},{4,16},{5,20},{6,24},{7,28},{8,1},{9,5},{... | collective-permute-start | bytes 196616 | tf_op jit(solution)/shard_map/ppermute | solution.py:2397
  20.3 48.7 %copy-start.2 = (f32[1536,1]{1,0:T(8,128)}, f32[1536,1]{1,0:T(8,128)S(1)}, u32[]{:S(2)}) copy-start(f32[1536,1]{1,0:T(8,128)S(1)} %reshape.281.mask) | copy-start | bytes 18436
  22.3 46.8 %copy-start.3 = (f32[8,1,512]{2,1,0:T(1,128)}, f32[8,1,512]{2,1,0:T(1,128)S(1)}, u32[]{:S(2)}) copy-start(f32[8,1,512]{2,1,0:T(1,128)S(1)} %broadcast_in_dim.60.sizes) | copy-start | bytes 49156
  22.4 1.7 copy-start.4
  69.1 1.3 copy-start.7
  70.4 1.1 copy-start.8
  71.5 1.0 copy-start.9
  72.5 0.9 copy-start.10
  73.4 0.6 copy-start.11
  74.0 0.6 copy-start.12
  74.7 426.4 %reduce-scatter.5.cloned.1.call-start = ((), (), s32[]{:S(2)}) async-start(), calls=%async_computation.4 | async-start | bytes 1179648 | tf_op jit(solution)/shard_map/reduce_scatter | solution.py:2544
  337.1 164.0 %reduce-scatter.3.cloned.1.call-start = ((), (), s32[]{:S(2)}) async-start(), calls=%async_computation.3 | async-start | bytes 2949120 | tf_op jit(solution)/shard_map/reduce_scatter | solution.py:2527
  487.6 1.5 copy-start.16
  487.6 2.4 copy-start.15
  487.6 3.3 copy-start.19
  523.8 2.7 copy-start.18
  523.8 3.6 copy-start.17
  525.0 3.3 copy-start.13
  528.3 2.5 copy-start.14
  530.8 2.5 copy-start.1
Sparse Core Ops, SparseCore 0:
  74.8 123.5 all-gather.1
  337.2 68.8 reduce-scatter.4
  410.1 81.9 reduce-scatter.2

commit v7 on v6

--- a/solution.py
+++ b/solution.py
@@ -861,9 +861,9 @@
     cells[PITCH + total : 2 * PITCH + total, :] = zeros
 
 
-def conv_rows(shifted, rows, weight, back):
+def conv_rows(shifted, rows, weight, back, offsets=range(9)):
     total = None
-    for offset in range(9):
+    for offset in offsets:
         row, col = offset // 3, offset % 3
         if back:
             row, col = 2 - row, 2 - col
@@ -2024,8 +2024,6 @@
 
     loop(total, CHUNK, act_task)
     widen(task, left, right, total)
-    for one in got:
-        one.finish()
 
     def message_weight(offset):
         if offset < early:
@@ -2035,12 +2033,29 @@
     def here(rows):
         return pl.ds(pl.multiple_of(PITCH + rows.start, 16), rows.size)
 
+    def start_messages(rows):
+        messages[rows, :] = conv_rows(
+            (left, task, right),
+            rows,
+            lambda offset, window: dot(window, message_weight(offset)),
+            False,
+            range(9 - late),
+        )
+        opened[rows, :] = jax.nn.sigmoid(dot(task[here(rows), :], gate[...]))
+
+    loop(total, BLOCK, start_messages)
+    for one in got:
+        one.finish()
+
     def send_messages(rows):
-        messages[rows, :] = conv_rows(
-            (left, task, right), rows, lambda offset, window: dot(window, message_weight(offset)), False
+        messages[rows, :] += conv_rows(
+            (left, task, right),
+            rows,
+            lambda offset, window: dot(window, message_weight(offset)),
+            False,
+            range(9 - late, 9),
         )
         own = task[here(rows), :]
-        opened[rows, :] = jax.nn.sigmoid(dot(own, gate[...]))
         part = (opened[rows, :] * messages[rows, :]).astype(BF16)
         gated[rows, :] = part
         depth_part = jnp.where(is_first, own, part)

time: 549 us -> 545 us (level)
  no operation moved by 1% of the time
where the time goes in v7:
time: 545 us; the launch traced here: 536 us
  Pallas kernels  461 us (85%)
  local copies, waits for them, and re-layouts  40 us (7%)
  other arithmetic  15.3 us (3%)
  between operations  14.6 us (3%)
    pallas_call x1, Pallas kernels, bottleneck_back(): pl.pallas_call(functools.partial(backward_kernel, nb), out_shape=(array(t...  144 us
    pallas_call x1, Pallas kernels, bottleneck(): pl.pallas_call(functools.partial(forward_kernel, nb, early), out_shape=ou...  117 us
    pallas_call x1, Pallas kernels, one_task(): pl.pallas_call(functools.partial(task_kernel, nb, early), out_shape=(arra...  81.4 us
    pallas_call x1, Pallas kernels, one_task_back(): pl.pallas_call(functools.partial(task_back_kernel, nb, early), out_shape=...  53.1 us
    pallas_call x1, Pallas kernels, begin(): pl.pallas_call(functools.partial(start_kernel, nb), out_shape=(array(nb,...  45 us
    pallas_call x1, Pallas kernels, finish(): pl.pallas_call(functools.partial(finish_kernel, nb), out_shape=(jax.Shape...  20.9 us
  transfers between devices with their start and end apart: 4, of which 1 were waited for; matrix products, arithmetic and copies ran while one was open for 6% of the time, Pallas kernels for 57%

profile of v7, /device:TPU:0, one launch (start us, length us, event | category | flops | bytes accessed | tf_op | source)
XLA Modules:
  0.0 536.5 jit_solution(17584733704325889265)
XLA Ops:
  7.3 0.9 copy-done
  8.1 1.3 collective-permute-start
  9.4 1.2 dynamic_slice.59
  10.7 1.2 dynamic_slice.58
  11.9 0.7 multiply_convert_fusion
  12.6 0.8 reshape.228
  13.3 0.8 reshape.229
  14.1 0.8 copy.76
  15.0 2.1 concatenate.21
  17.1 0.7 convert_element_type.86
  17.8 0.7 select_maximum_fusion
  18.6 0.7 iota_compare_fusion.4
  19.2 0.7 iota_compare_fusion.5
  19.9 0.4 reshape.281.mask
  20.5 1.6 pad.35
  22.1 0.1 reduce_sum.27
  22.4 1.7 copy-done.4
  24.1 45.0 %shard_map.297 = (bf16[8,256,512]{2,1,0:T(8,128)(2,1)S(1)}, bf16[8,32,128]{2,1,0:T(8,128)(2,1)S(1)}, f32[8,1536]{1,0:T(8,128)S(1)}, bf16[1536,512]{1,0:T(8,128)(...) custom-call(bf16[256,512]{1,0:T(8,128)(2,1)S(1)} %copy-done.6, ...), custom_call_target="tpu_custom_call" | custom-call | flops 80000000000 | bytes 30000000 | tf_op jit(solution)/shard_map/pallas_call | solution.py:1029
  69.1 1.3 copy-done.7
  70.4 1.1 copy-done.8
  71.5 1.0 copy-done.9
  72.5 0.9 copy-done.10
  73.4 0.6 copy-done.11
  74.0 0.6 copy-done.12
  75.9 0.2 reshape.238
  76.4 0.6 stack.45.norms
  77.1 0.7 broadcast_select_fusion
  77.9 0.6 select_maximum_fusion.1.norms
  78.5 116.7 %shard_map.298 = (bf16[512,512]{1,0:T(8,128)(2,1)}, bf16[512,512]{1,0:T(8,128)(2,1)}, bf16[512,512]{1,0:T(8,128)(2,1)}, bf16[4,512,512]{2,1,0:T(8,128)(2,1)}, bf...) custom-call(f32[384,512]{1,0:T(8,128)} %copy-done.10, ...), custom_call_target="tpu_custom_call" | custom-call | flops 80000000000 | bytes 30000000 | tf_op jit(solution)/shard_map/pallas_call | solution.py:1267
  195.2 3.1 all-gather.2.cloned.1.call-done.head
  198.3 0.6 broadcast_in_dim.62.mask_line
  199.0 81.4 %shard_map.299 = (f32[48,1536]{1,0:T(8,128)}, bf16[48,1536]{1,0:T(8,128)(2,1)}, f32[1536,512]{1,0:T(8,128)}, f32[8,512]{1,0:T(8,128)}, bf16[1632,512]{1,0:T(8,12...) custom-call(bf16[1632,512]{1,0:T(8,128)(2,1)} %get-tuple-element.73., ...), custom_call_target="tpu_custom_call" | custom-call | flops 80000000000 | bytes 30000000 | tf_op jit(solution)/shard_map/pallas_call | solution.py:2126
  280.3 53.1 %shard_map.300 = (bf16[1536,512]{1,0:T(8,128)(2,1)}, bf16[7,512,512]{2,1,0:T(8,128)(2,1)}, bf16[512,1024]{1,0:T(8,128)(2,1)}, bf16[4,64,512]{2,1,0:T(8,128)(2,1)}, f32[8,512]{1,0:T(8,128)}) custom-call(bf16[1632,512]{1,0:T(8,128)(2,1)} %get-tuple-element.73.shared_act, f32[1536,1]{1,0:T(8,128)} %copy-done.2, f32[8,1,512]{2,1,0:T(1,128)} %copy-done.3, ...), custom_call_target="tpu_custom_call" | custom-call | flops 80000000000 | bytes 30000000 | tf_op jit(solution)/shard_map/pallas_call | solution.py:2281
  333.5 0.7 reduce-scatter.3.cloned.1.call-update
  334.2 144.3 %shard_map.301 = (f32[384,2048]{1,0:T(8,128)}, bf16[64,512]{1,0:T(8,128)(2,1)}, bf16[64,512]{1,0:T(8,128)(2,1)}, bf16[4,64,512]{2,1,0:T(8,128)(2,1)}, bf16[4,64,...) custom-call(bf16[1536,512]{1,0:T(8,128)(2,1)} %get-tuple-element.86., ...), custom_call_target="tpu_custom_call" | custom-call | flops 80000000000 | bytes 30000000 | tf_op jit(solution)/shard_map/pallas_call | solution.py:1816
  478.5 0.9 constant_dynamic-slice_fusion
  479.4 0.1 reshape.239
  479.6 0.6 slice.164
  480.2 0.8 copy.88
  480.9 1.3 reshape.280
  482.3 0.8 copy.86
  483.1 1.5 reshape.270
  484.6 0.8 copy.92
  485.5 0.9 convert_element_type.102
  486.4 0.7 copy.89
  487.1 1.0 fusion.11
  488.1 0.6 dynamic_slice.76
  488.7 0.6 dynamic_slice.77
  489.4 0.8 slice_bitcast_fusion.6
  490.2 0.9 slice_bitcast_fusion.4
  491.1 0.7 fusion.5
  491.7 0.7 fusion.2
  492.4 0.6 slice_reduce_fusion
  493.0 3.5 slice_bitcast_fusion
  496.6 1.1 pad_maximum_fusion
  497.6 0.5 reshape.249
  498.2 0.9 copy.85
  499.1 20.9 %shard_map.302 = (bf16[4,64,512]{2,1,0:T(8,128)(2,1)}, bf16[4,64,512]{2,1,0:T(8,128)(2,1)}, bf16[4,448,512]{2,1,0:T(8,128)(2,1)}) custom-call(bf16[64,512]{1,0:T(8,128)(2,1)} %get-tuple-element.106.first, bf16[64,512]{1,0:T(8,128)(2,1)} %get-tuple-element.107.shared, bf16[448,512]{1,0:T(8,128)(2,1)} %bitcast.92), custom_call_target="tpu_custom_call" | custom-call | tf_op jit(solution)/shard_map/pallas_call | solution.py:1927
  520.0 1.1 slice.167
  521.2 1.6 slice.168
  522.8 0.9 bitcast_convert_fusion.1
  523.6 0.9 bitcast_convert_fusion
  524.5 2.5 maximum_convert_fusion
  527.0 2.5 maximum_convert_fusion.1
  (91 shorter events, 2.5 us)
Async XLA Ops:
  7.2 1.0 copy-start
  7.2 15.2 %copy-start.6 = (bf16[256,512]{1,0:T(8,128)(2,1)S(1)}, bf16[256,512]{1,0:T(8,128)(2,1)}, u32[]{:S(2)}) copy-start(bf16[256,512]{1,0:T(8,128)(2,1)} %weight.1) | copy-start | bytes 786436
  7.2 15.2 %copy-start.5 = (bf16[9,64,512]{2,1,0:T(8,128)(2,1)S(1)}, bf16[9,64,512]{2,1,0:T(8,128)(2,1)}, u32[]{:S(2)}) copy-start(bf16[9,64,512]{2,1,0:T(8,128)(2,1)} %spatial_own.1) | copy-start | bytes 1769476
  7.2 191.1 %all-gather.2.cloned.1.call-start = ((), (), s32[]{:S(2)}) async-start(), calls=%async_computation.2 | async-start | bytes 5308416 | tf_op jit(solution)/shard_map/all_gather | solution.py:2462
  8.1 70.3 %collective-permute-start = (bf16[64,512]{1,0:T(8,128)(2,1)S(1)}, bf16[64,512]{1,0:T(8,128)(2,1)}, u32[]{:S(2)}, u32[]{:S(2)}) collective-permute-start(bf16[64,512]{1,0:T(8,128)(2,1)S(1)} %constant_dynamic-slice_fusion.3), channel_id=1, source_target_pairs={{0,0},{1,4},{2,8},{3,12},{4,16},{5,20},{6,24},{7,28},{8,1},{9,5},{... | collective-permute-start | bytes 196616 | tf_op jit(solution)/shard_map/ppermute | solution.py:2412
  20.3 48.7 %copy-start.2 = (f32[1536,1]{1,0:T(8,128)}, f32[1536,1]{1,0:T(8,128)S(1)}, u32[]{:S(2)}) copy-start(f32[1536,1]{1,0:T(8,128)S(1)} %reshape.281.mask) | copy-start | bytes 18436
  22.3 46.8 %copy-start.3 = (f32[8,1,512]{2,1,0:T(1,128)}, f32[8,1,512]{2,1,0:T(1,128)S(1)}, u32[]{:S(2)}) copy-start(f32[8,1,512]{2,1,0:T(1,128)S(1)} %broadcast_in_dim.60.sizes) | copy-start | bytes 49156
  22.4 1.7 copy-start.4
  69.1 1.3 copy-start.7
  70.4 1.1 copy-start.8
  71.5 1.0 copy-start.9
  72.5 0.9 copy-start.10
  73.4 0.6 copy-start.11
  74.0 0.6 copy-start.12
  74.7 421.9 %reduce-scatter.5.cloned.1.call-start = ((), (), s32[]{:S(2)}) async-start(), calls=%async_computation.4 | async-start | bytes 1179648 | tf_op jit(solution)/shard_map/reduce_scatter | solution.py:2559
  333.4 163.1 %reduce-scatter.3.cloned.1.call-start = ((), (), s32[]{:S(2)}) async-start(), calls=%async_computation.3 | async-start | bytes 2949120 | tf_op jit(solution)/shard_map/reduce_scatter | solution.py:2542
  483.1 1.5 copy-start.16
  483.1 2.4 copy-start.15
  483.1 3.3 copy-start.19
  520.0 2.7 copy-start.18
  520.0 3.6 copy-start.17
  521.2 3.3 copy-start.13
  524.5 2.5 copy-start.14
  527.0 2.5 copy-start.1
Sparse Core Ops, SparseCore 0:
  74.8 123.5 all-gather.1
  333.6 68.5 reduce-scatter.4
  406.0 82.0 reduce-scatter.2

commit v8 on v7

--- a/solution.py
+++ b/solution.py
@@ -1698,13 +1698,13 @@
         grad_one,
         spatial_grads,
     )
-    step(messages[1])
-    step(messages[2])
-    step(heads[0], heads[1], job_gates, job_stream)
     sums = norm_back(stats, norms, mask, grad_one, pre_one, 0, mid, lambda rows: grad_one[rows, :], base)
     slots_tile[blk] = jnp.concatenate(sums, 0)
     swap_tile_sums(mail, place, slots_tile)
     copies = send_sums(mail, place, slots_one, list(add_up(slots_tile)))
+    step(messages[1])
+    step(messages[2])
+    step(heads[0], heads[1], job_gates, job_stream)
     step(heads[7], heads[8], job_last, job_spatial)
     step(heads[5], heads[6], job_shared)
     for copy in copies:

time: 545 us -> 542 us (level)
  no operation moved by 1% of the time
where the time goes in v8:
time: 542 us; the launch traced here: 533 us
  Pallas kernels  458 us (85%)
  local copies, waits for them, and re-layouts  40 us (7%)
  other arithmetic  15.3 us (3%)
  between operations  14.6 us (3%)
    pallas_call x1, Pallas kernels, bottleneck_back(): pl.pallas_call(functools.partial(backward_kernel, nb), out_shape=(array(t...  141 us
    pallas_call x1, Pallas kernels, bottleneck(): pl.pallas_call(functools.partial(forward_kernel, nb, early), out_shape=ou...  117 us
    pallas_call x1, Pallas kernels, one_task(): pl.pallas_call(functools.partial(task_kernel, nb, early), out_shape=(arra...  81.4 us
    pallas_call x1, Pallas kernels, one_task_back(): pl.pallas_call(functools.partial(task_back_kernel, nb, early), out_shape=...  53.1 us
    pallas_call x1, Pallas kernels, begin(): pl.pallas_call(functools.partial(start_kernel, nb), out_shape=(array(nb,...  45 us
    pallas_call x1, Pallas kernels, finish(): pl.pallas_call(functools.partial(finish_kernel, nb), out_shape=(jax.Shape...  20.4 us
  transfers between devices with their start and end apart: 4, of which 1 were waited for; matrix products, arithmetic and copies ran while one was open for 6% of the time, Pallas kernels for 57%

profile of v8, /device:TPU:0, one launch (start us, length us, event | category | flops | bytes accessed | tf_op | source)
XLA Modules:
  0.0 532.8 jit_solution(14675389634499533949)
XLA Ops:
  7.3 0.9 copy-done
  8.1 1.3 collective-permute-start
  9.4 1.2 dynamic_slice.59
  10.7 1.2 dynamic_slice.58
  11.9 0.7 multiply_convert_fusion
  12.6 0.8 reshape.228
  13.3 0.8 reshape.229
  14.1 0.8 copy.76
  15.0 2.1 concatenate.21
  17.1 0.7 convert_element_type.86
  17.8 0.7 select_maximum_fusion
  18.6 0.7 iota_compare_fusion.4
  19.2 0.7 iota_compare_fusion.5
  19.9 0.4 reshape.281.mask
  20.5 1.6 pad.35
  22.1 0.1 reduce_sum.27
  22.4 1.7 copy-done.4
  24.1 45.0 %shard_map.297 = (bf16[8,256,512]{2,1,0:T(8,128)(2,1)S(1)}, bf16[8,32,128]{2,1,0:T(8,128)(2,1)S(1)}, f32[8,1536]{1,0:T(8,128)S(1)}, bf16[1536,512]{1,0:T(8,128)(...) custom-call(bf16[256,512]{1,0:T(8,128)(2,1)S(1)} %copy-done.6, ...), custom_call_target="tpu_custom_call" | custom-call | flops 80000000000 | bytes 30000000 | tf_op jit(solution)/shard_map/pallas_call | solution.py:1029
  69.1 1.3 copy-done.7
  70.4 1.1 copy-done.8
  71.5 1.0 copy-done.9
  72.5 0.9 copy-done.10
  73.4 0.6 copy-done.11
  74.0 0.6 copy-done.12
  75.9 0.2 reshape.238
  76.4 0.6 stack.45.norms
  77.1 0.7 broadcast_select_fusion
  77.9 0.6 select_maximum_fusion.1.norms
  78.5 116.7 %shard_map.298 = (bf16[512,512]{1,0:T(8,128)(2,1)}, bf16[512,512]{1,0:T(8,128)(2,1)}, bf16[512,512]{1,0:T(8,128)(2,1)}, bf16[4,512,512]{2,1,0:T(8,128)(2,1)}, bf...) custom-call(f32[384,512]{1,0:T(8,128)} %copy-done.10, ...), custom_call_target="tpu_custom_call" | custom-call | flops 80000000000 | bytes 30000000 | tf_op jit(solution)/shard_map/pallas_call | solution.py:1267
  195.2 3.1 all-gather.2.cloned.1.call-done.head
  198.3 0.6 broadcast_in_dim.62.mask_line
  199.0 81.4 %shard_map.299 = (f32[48,1536]{1,0:T(8,128)}, bf16[48,1536]{1,0:T(8,128)(2,1)}, f32[1536,512]{1,0:T(8,128)}, f32[8,512]{1,0:T(8,128)}, bf16[1632,512]{1,0:T(8,12...) custom-call(bf16[1632,512]{1,0:T(8,128)(2,1)} %get-tuple-element.73., ...), custom_call_target="tpu_custom_call" | custom-call | flops 80000000000 | bytes 30000000 | tf_op jit(solution)/shard_map/pallas_call | solution.py:2126
  280.3 53.1 %shard_map.300 = (bf16[1536,512]{1,0:T(8,128)(2,1)}, bf16[7,512,512]{2,1,0:T(8,128)(2,1)}, bf16[512,1024]{1,0:T(8,128)(2,1)}, bf16[4,64,512]{2,1,0:T(8,128)(2,1)}, f32[8,512]{1,0:T(8,128)}) custom-call(bf16[1632,512]{1,0:T(8,128)(2,1)} %get-tuple-element.73.shared_act, f32[1536,1]{1,0:T(8,128)} %copy-done.2, f32[8,1,512]{2,1,0:T(1,128)} %copy-done.3, ...), custom_call_target="tpu_custom_call" | custom-call | flops 80000000000 | bytes 30000000 | tf_op jit(solution)/shard_map/pallas_call | solution.py:2281
  333.5 0.7 reduce-scatter.3.cloned.1.call-update
  334.2 141.1 %shard_map.301 = (f32[384,2048]{1,0:T(8,128)}, bf16[64,512]{1,0:T(8,128)(2,1)}, bf16[64,512]{1,0:T(8,128)(2,1)}, bf16[4,64,512]{2,1,0:T(8,128)(2,1)}, bf16[4,64,...) custom-call(bf16[1536,512]{1,0:T(8,128)(2,1)} %get-tuple-element.86., ...), custom_call_target="tpu_custom_call" | custom-call | flops 80000000000 | bytes 30000000 | tf_op jit(solution)/shard_map/pallas_call | solution.py:1816
  475.3 0.9 constant_dynamic-slice_fusion
  476.2 0.1 reshape.239
  476.3 0.6 slice.164
  476.9 0.8 copy.88
  477.7 1.3 reshape.280
  479.1 0.8 copy.86
  479.9 1.5 reshape.270
  481.4 0.8 copy.92
  482.2 0.9 convert_element_type.102
  483.2 0.7 copy.89
  483.9 1.0 fusion.11
  484.9 0.6 dynamic_slice.76
  485.5 0.6 dynamic_slice.77
  486.1 0.8 slice_bitcast_fusion.6
  486.9 0.9 slice_bitcast_fusion.4
  487.8 0.7 fusion.5
  488.5 0.7 fusion.2
  489.2 0.6 slice_reduce_fusion
  489.8 3.6 slice_bitcast_fusion
  493.4 1.1 pad_maximum_fusion
  494.4 0.5 reshape.249
  495.0 0.9 copy.85
  495.9 20.4 %shard_map.302 = (bf16[4,64,512]{2,1,0:T(8,128)(2,1)}, bf16[4,64,512]{2,1,0:T(8,128)(2,1)}, bf16[4,448,512]{2,1,0:T(8,128)(2,1)}) custom-call(bf16[64,512]{1,0:T(8,128)(2,1)} %get-tuple-element.106.first, bf16[64,512]{1,0:T(8,128)(2,1)} %get-tuple-element.107.shared, bf16[448,512]{1,0:T(8,128)(2,1)} %bitcast.92), custom_call_target="tpu_custom_call" | custom-call | tf_op jit(solution)/shard_map/pallas_call | solution.py:1927
  516.3 1.1 slice.167
  517.5 1.6 slice.168
  519.0 0.9 bitcast_convert_fusion.1
  519.9 0.9 bitcast_convert_fusion
  520.8 2.5 maximum_convert_fusion
  523.3 2.5 maximum_convert_fusion.1
  (91 shorter events, 2.5 us)
Async XLA Ops:
  7.2 1.0 copy-start
  7.2 15.2 %copy-start.6 = (bf16[256,512]{1,0:T(8,128)(2,1)S(1)}, bf16[256,512]{1,0:T(8,128)(2,1)}, u32[]{:S(2)}) copy-start(bf16[256,512]{1,0:T(8,128)(2,1)} %weight.1) | copy-start | bytes 786436
  7.2 15.2 %copy-start.5 = (bf16[9,64,512]{2,1,0:T(8,128)(2,1)S(1)}, bf16[9,64,512]{2,1,0:T(8,128)(2,1)}, u32[]{:S(2)}) copy-start(bf16[9,64,512]{2,1,0:T(8,128)(2,1)} %spatial_own.1) | copy-start | bytes 1769476
  7.2 191.1 %all-gather.2.cloned.1.call-start = ((), (), s32[]{:S(2)}) async-start(), calls=%async_computation.2 | async-start | bytes 5308416 | tf_op jit(solution)/shard_map/all_gather | solution.py:2462
  8.1 70.3 %collective-permute-start = (bf16[64,512]{1,0:T(8,128)(2,1)S(1)}, bf16[64,512]{1,0:T(8,128)(2,1)}, u32[]{:S(2)}, u32[]{:S(2)}) collective-permute-start(bf16[64,512]{1,0:T(8,128)(2,1)S(1)} %constant_dynamic-slice_fusion.3), channel_id=1, source_target_pairs={{0,0},{1,4},{2,8},{3,12},{4,16},{5,20},{6,24},{7,28},{8,1},{9,5},{... | collective-permute-start | bytes 196616 | tf_op jit(solution)/shard_map/ppermute | solution.py:2412
  20.3 48.7 %copy-start.2 = (f32[1536,1]{1,0:T(8,128)}, f32[1536,1]{1,0:T(8,128)S(1)}, u32[]{:S(2)}) copy-start(f32[1536,1]{1,0:T(8,128)S(1)} %reshape.281.mask) | copy-start | bytes 18436
  22.3 46.8 %copy-start.3 = (f32[8,1,512]{2,1,0:T(1,128)}, f32[8,1,512]{2,1,0:T(1,128)S(1)}, u32[]{:S(2)}) copy-start(f32[8,1,512]{2,1,0:T(1,128)S(1)} %broadcast_in_dim.60.sizes) | copy-start | bytes 49156
  22.4 1.7 copy-start.4
  69.1 1.3 copy-start.7
  70.4 1.1 copy-start.8
  71.5 1.0 copy-start.9
  72.5 0.9 copy-start.10
  73.4 0.6 copy-start.11
  74.0 0.6 copy-start.12
  74.7 418.7 %reduce-scatter.5.cloned.1.call-start = ((), (), s32[]{:S(2)}) async-start(), calls=%async_computation.4 | async-start | bytes 1179648 | tf_op jit(solution)/shard_map/reduce_scatter | solution.py:2559
  333.4 159.9 %reduce-scatter.3.cloned.1.call-start = ((), (), s32[]{:S(2)}) async-start(), calls=%async_computation.3 | async-start | bytes 2949120 | tf_op jit(solution)/shard_map/reduce_scatter | solution.py:2542
  479.8 1.5 copy-start.16
  479.8 2.4 copy-start.15
  479.8 3.3 copy-start.19
  516.3 2.7 copy-start.18
  516.3 3.6 copy-start.17
  517.4 3.3 copy-start.13
  520.8 2.5 copy-start.14
  523.3 2.5 copy-start.1
Sparse Core Ops, SparseCore 0:
  74.8 123.5 all-gather.1
  333.6 68.5 reduce-scatter.4
  406.0 84.5 reduce-scatter.2
